TPU v7x, 32 devices: a whole 2x2x4 slice. The times are simulated.
32 devices in a mesh: groups: 2 (over x), tensor: 16 (over z, y, core).
Axes of the slice: x: 2, y: 2, z: 4, core: 2. Of those that a mesh axis runs over, the one named last changes fastest.
Arguments:
- activations: bfloat16 [2048, 8192], P('groups', 'tensor'), parts along dimension 0, may hold values from -6 to 6
- gate_pre: bfloat16 [2048, 28672], P('groups', 'tensor'), parts along dimension 0, may hold values from -6 to 6
- up_pre: bfloat16 [2048, 28672], P('groups', 'tensor'), parts along dimension 0, may hold values from -6 to 6
- out_grad: bfloat16 [2048, 8192], P('groups', 'tensor'), parts along dimension 0, may hold values from -6 to 6
- down_weight: bfloat16 [28672, 8192], P('tensor'), may hold values from -0.0625 to 0.0625
- in_proj_down: bfloat16 [64, 28672], P(None, 'tensor'), may hold values from -0.03125 to 0.03125
- out_proj_down: bfloat16 [64, 8192], replicated, may hold values from -0.0625 to 0.0625
- in_proj_up: bfloat16 [64, 8192], P(None, 'tensor'), may hold values from -0.0625 to 0.0625
- out_proj_up: bfloat16 [64, 28672], P(None, 'tensor'), may hold values from -0.03125 to 0.03125
- segments: int32 [2048], P('groups'), parts along dimension 0, may hold values from 0 to 15, never falling along the last dimension, each value on 1 to 128 neighbouring positions
- labels: int32 [32], P('groups'), parts along dimension 0, may hold values from 0 to 1, as said below
- queries: bfloat16 [1024, 8192], P('tensor'), may hold values from -0.005859375 to 0.005859375
Outputs:
- scores: float32 [16, 1024], P('groups', 'tensor'), parts along dimension 0
There are 2 independent parts, one for each index of `groups`. A program takes and returns all parts, laid end to end along the dimension named above; an argument that names none is the same for every part. Nothing has to cross between parts.
Inputs may be any that keep to these rules, and one draw needn't show every extreme that they name: labels[2k] + labels[2k + 1] == 1 for every pair k.
All inputs are finite; a program needn't handle non-finite values.
Results may differ from a plain program's by a relative error of at most 0.0041.
Values may be sent and summed in bfloat16 or wider, within the bound.
No kernel may reach another device: no remote copies, remote signals or barrier semaphores. Data moves between devices by JAX's collectives and lax.ppermute only.
A program may use at most 128 MiB of HBM per device.

v0:
```python
import jax
import jax.numpy as jnp
from jax import lax
from jax.sharding import PartitionSpec as P


def pair_outer(weight, left, right):
    return jnp.einsum(
        "tp,tk,tj->pkj", weight, left, right, precision=lax.Precision.HIGHEST
    ).reshape(weight.shape[1], -1)


def project(data, proj):
    return lax.dot_general(data, proj, (((1,), (1,)), ((), ())), preferred_element_type=jnp.float32)


def per_device(
    activations,
    gate_pre,
    up_pre,
    out_grad,
    down_weight,
    in_proj_down,
    out_proj_down,
    in_proj_up,
    out_proj_up,
    segments,
    labels,
    queries,
):
    silu_gate = jax.nn.silu(gate_pre.astype(jnp.float32))
    hidden = (silu_gate * up_pre.astype(jnp.float32)).astype(jnp.bfloat16)
    tok_rows = out_grad.shape[0]
    piece = lax.all_gather(out_grad, "tensor", axis=1, tiled=True)
    dgrad = project(piece, down_weight)
    b_down = project(piece, out_proj_down)
    up_grad = (dgrad * silu_gate).astype(jnp.bfloat16)
    part_adown = project(hidden, in_proj_down)
    part_aup = project(activations, in_proj_up)
    part_bup = project(up_grad, out_proj_up)
    seq_count = labels.shape[0]
    seq_match = segments[:, None] == jnp.arange(seq_count, dtype=jnp.int32)[None, :]
    signs = (2 * labels - 1).astype(jnp.float32)
    per_seq = jnp.where(seq_match, signs[None, :], jnp.float32(0.0))
    weight = per_seq.reshape(tok_rows, seq_count // 2, 2).sum(axis=2)
    a_down, a_up, b_up = lax.psum((part_adown, part_aup, part_bup), "tensor")
    totals = jnp.concatenate(
        [pair_outer(weight, b_down, a_down), pair_outer(weight, b_up, a_up)], axis=1
    )
    grads = totals.astype(jnp.bfloat16)
    return project(grads, queries)


def solution(mesh):
    in_specs = (
        P("groups", "tensor"),
        P("groups", "tensor"),
        P("groups", "tensor"),
        P("groups", "tensor"),
        P("tensor", None),
        P(None, "tensor"),
        P(),
        P(None, "tensor"),
        P(None, "tensor"),
        P("groups"),
        P("groups"),
        P("tensor", None),
    )
    out_specs = P("groups", "tensor")
    return jax.shard_map(
        per_device, mesh=mesh, in_specs=in_specs, out_specs=out_specs, check_vma=False
    )
```

profile of v0, /device:TPU:0, one launch (start us, length us, event | category | flops | bytes accessed | tf_op | source)
XLA Modules:
  0.0 288.8 jit_solution(4919952387941162023)
XLA Ops:
  6.5 0.0 copy-start
  6.5 0.0 all-gather.2.cloned.1.call-start
  6.5 0.7 all-gather.2.cloned.1.call-update
  7.3 0.0 all-reduce.3.cloned.1.call-start
  7.3 0.7 add_convert_fusion
  8.0 0.1 broadcast_in_dim.17
  8.0 0.1 copy.15
  8.1 0.8 select_reduce_fusion
  8.9 0.0 copy-done
  8.9 2.0 fusion.34
  10.9 6.2 %fusion.3 = f32[1024,64]{0,1:T(8,128)} fusion(bf16[64,1792]{1,0:T(8,128)(2,1)} %param.17, bf16[1024,1792]{1,0:T(8,128)(2,1)} %param.14, bf16[1024,1792]{1,0:T(8,128)(2,1)} %param.13), kind=kOutput, calls=%fused_computation.7 | convolution fusion | flops 249561088 | bytes 7831552 | tf_op jit(solution)/shard_map/dot_general | solution.py:14
  17.1 0.0 copy-start.3
  17.1 125.4 %all-gather.2.cloned.1.call-done = bf16[1024,8192]{1,0:T(8,128)(2,1)} async-done(((bf16[1024,512]{1,0:T(8,128)(2,1)}), bf16[1024,8192]{1,0:T(8,128)(2,1)}) %all-gather.2.cloned.1.call-update) | async-done | bytes 16777232 | tf_op jit(solution)/shard_map/all_gather | solution.py:34
  142.6 39.5 %multiply_convert_fusion = bf16[1024,1792]{1,0:T(8,128)(2,1)S(1)} fusion(bf16[1024,8192]{1,0:T(8,128)(2,1)} %all-gather.2.cloned.1.call-done, bf16[1792,8192]{1,0:T(8,128)(2,1)} %param.16, bf16[1024,1792]{1,0:T(8,128)(2,1)} %param.13), kind=kOutput, calls=%fused_computation.5 | convolution fusion | flops 30077616128 | bytes 53477376 | tf_op jit(solution)/shard_map/dot_general | solution.py:14
  182.1 0.0 copy-done.3
  182.1 0.0 copy-start.1
  182.1 1.9 fusion.33
  184.0 0.0 all-reduce.3.cloned.1.call-update
  184.0 0.0 copy-done.1
  184.1 0.0 copy-start.2
  184.1 11.1 %fusion.32 = f32[1024,64]{0,1:T(8,128)S(1)} fusion(bf16[1024,8192]{1,0:T(8,128)(2,1)} %all-gather.2.cloned.1.call-done, bf16[64,8192]{1,0:T(8,128)(2,1)S(1)} %copy-done.1), kind=kOutput, calls=%fused_computation.31 | convolution fusion | flops 1073741824 | bytes 18087936 | tf_op jit(solution)/shard_map/dot_general | solution.py:14
  195.2 79.8 %all-reduce.3.cloned.1.call-done = (f32[1024,64]{0,1:T(8,128)}, f32[1024,64]{0,1:T(8,128)}, f32[1024,64]{0,1:T(8,128)}) async-done(((f32[1024,64]{0,1:T(8,128)}, f32[1024,64]{0,1:T(8,128)}, f32[1024,64]{0,1:T(8,128)}), (f32[1024,64]{0,1:T(8,128)}, f32[1024,64]{0,1:T(8,128)}, f32[1024,64]{0,1:T(8,128)})) %all-reduce.3.cloned.1.call-update) | async-done | bytes 786448 | tf_op jit(solution)/shard_map/psum | solution.py:46
  275.0 2.8 fusion.14
  277.9 0.2 reshape.31
  278.0 2.7 fusion.17
  280.8 0.2 reshape.30
  281.0 0.0 copy-done.2
  281.0 1.0 fusion.26
  (3 shorter events, 0.0 us)
Async XLA Ops:
  6.5 2.4 copy-start
  6.5 136.1 %all-gather.2.cloned.1.call-start = ((), (), s32[]{:S(2)}) async-start(), calls=%async_computation | async-start | bytes 17825792 | tf_op jit(solution)/shard_map/all_gather | solution.py:34
  7.3 267.8 %all-reduce.3.cloned.1.call-start = ((), (), s32[]{:S(2)}) async-start(), calls=%async_computation.1 | async-start | bytes 1572864 | tf_op jit(solution)/shard_map/psum | solution.py:46
  17.1 164.9 %copy-start.3 = (bf16[64,1792]{1,0:T(8,128)(2,1)S(1)}, bf16[64,1792]{1,0:T(8,128)(2,1)}, u32[]{:S(2)}) copy-start(bf16[64,1792]{1,0:T(8,128)(2,1)} %param.20) | copy-start | bytes 688132
  182.1 2.0 copy-start.1
  184.1 96.9 %copy-start.2 = (bf16[64,8192]{1,0:T(8,128)(2,1)S(1)}, bf16[64,8192]{1,0:T(8,128)(2,1)}, u32[]{:S(2)}) copy-start(bf16[64,8192]{1,0:T(8,128)(2,1)} %param.23) | copy-start | bytes 3145732
Sparse Core Ops, SparseCore 0:
  9.5 133.0 all-gather.1
  184.2 90.8 all-reduce.2
where the time goes:
time: 289 us
  waiting for transfers between devices  206 us (71%)
  matrix products  67.3 us (23%)
  between operations  13.5 us (5%)
    all_gather x1, waiting for transfers between devices, per_device(): piece = lax.all_gather(out_grad, 'tensor', axis=1, tiled=True)  125 us
    psum x1, waiting for transfers between devices, per_device(): a_down, a_up, b_up = lax.psum((part_adown, part_aup, part_bup), 'tensor')  79.8 us
    dot_general x6, matrix products, project(): lax.dot_general(data, proj, (((1,), (1,)), ((), ())), preferred_element_t...  61.8 us
  transfers between devices with their start and end apart: 2, of which 2 were waited for; matrix products, arithmetic and copies ran while one was open for 7% of the time, Pallas kernels for 0%

commit v1 on v0

v1 whole, which is shorter than its diff:
```python
import functools

import jax
import jax.numpy as jnp
import numpy as np
from jax import lax
from jax.experimental import pallas as pl
from jax.experimental.pallas import tpu as pltpu
from jax.sharding import PartitionSpec as P

F32, BF16 = jnp.float32, jnp.bfloat16
VMEM_LIMIT = 40 * 1024 * 1024


def dot_t(left, right, precision=None):
    return lax.dot_general(
        left, right, (((1,), (1,)), ((), ())), preferred_element_type=F32, precision=precision
    )


def ring_of(chips):
    if chips == 8:
        return [0, 2, 4, 6, 7, 5, 3, 1]
    return list(range(chips))


def step_kernel(blocks, src_ref, *refs):
    lefts, weights = refs[:blocks], refs[blocks : 2 * blocks]
    acc_ref = refs[2 * blocks] if len(refs) == 2 * blocks + 2 else None
    out_ref = refs[-1]
    total = None if acc_ref is None else acc_ref[...]
    for left, weight in zip(lefts, weights):
        part = dot_t(left[...], weight[...])
        total = part if total is None else total + part
    out_ref[...] = total


def tile_of(units):
    return 256 if units % 256 == 0 else units


def add_step(src, offset, lefts, weight, acc):
    tokens, depth = lefts[0].shape
    units = weight.shape[0]
    tile, blocks = tile_of(units), len(lefts)
    whole = pl.BlockSpec((tokens, depth), lambda i, s: (0, 0))
    tiles = pl.BlockSpec((tokens, tile), lambda i, s: (0, i))
    columns = [
        pl.BlockSpec((tile, depth), lambda i, s, m=m: (i, s[offset + m])) for m in range(blocks)
    ]
    ins = [*lefts, *([weight] * blocks)]
    specs = [whole] * blocks + columns
    aliases = {}
    if acc is not None:
        ins.append(acc)
        specs.append(tiles)
        aliases = {len(ins): 0}
    return pl.pallas_call(
        functools.partial(step_kernel, blocks),
        grid_spec=pltpu.PrefetchScalarGridSpec(
            num_scalar_prefetch=1, grid=(units // tile,), in_specs=specs, out_specs=tiles
        ),
        out_shape=jax.ShapeDtypeStruct((tokens, units), F32),
        input_output_aliases=aliases,
        cost_estimate=pl.CostEstimate(
            flops=2 * tokens * units * depth * blocks,
            bytes_accessed=units * tokens * 8 + units * depth * blocks * 2,
            transcendentals=0,
        ),
        compiler_params=pltpu.CompilerParams(vmem_limit_bytes=VMEM_LIMIT),
    )(src, *ins)


def pair_sums(weight, b, a, out_ref):
    kos, pairs = b.shape[0], weight.shape[0]
    kis = a.shape[0]
    left = jnp.concatenate([weight * b[k : k + 1, :] for k in range(kos)], axis=0)
    sums = dot_t(left, a, lax.Precision.HIGHEST)
    half = kos // 2
    for r in range(half):
        low = sums[r * pairs : (r + 1) * pairs]
        high = sums[(r + half) * pairs : (r + half + 1) * pairs]
        out_ref[:, r * 2 * kis : (r + 1) * 2 * kis] = jnp.concatenate([low, high], axis=1)


def pair_kernel(weight_ref, b_ref, a_ref, out_ref):
    pair_sums(weight_ref[...], b_ref[...], a_ref[...], out_ref)


def pair_outer(weight, b, a):
    return pl.pallas_call(
        pair_kernel,
        out_shape=jax.ShapeDtypeStruct((weight.shape[0], b.shape[0] * a.shape[0]), F32),
        compiler_params=pltpu.CompilerParams(vmem_limit_bytes=VMEM_LIMIT),
    )(weight, b, a)


def last_kernel(
    src_ref, f0, f1, b0, b1, w0, w1, acc_ref, silu_ref, proj_ref, weight_ref, a_ref, out_ref, b_acc
):
    step = pl.program_id(0)
    half = f0.shape[0]

    @pl.when(step == 0)
    def _():
        b_acc[...] = jnp.zeros_like(b_acc)

    for row, own, other in ((0, f0, f1), (half, b0, b1)):
        rows = slice(row, row + half)
        grad = acc_ref[rows, :] + dot_t(own[...], w0[...]) + dot_t(other[...], w1[...])
        up = (grad * silu_ref[rows, :]).astype(BF16)
        b_acc[:, rows] += dot_t(proj_ref[...], up)

    @pl.when(step == pl.num_programs(0) - 1)
    def _():
        pair_sums(weight_ref[...], b_acc[...], a_ref[...], out_ref)


def last_step(src, offset, halves, weight, acc, silu, proj, pair_weight, a_up):
    half, depth = halves[0].shape
    tokens, units = acc.shape
    kos, kis, pairs = proj.shape[0], a_up.shape[0], pair_weight.shape[0]
    tile = tile_of(units)
    piece = pl.BlockSpec((half, depth), lambda i, s: (0, 0))
    tiles = pl.BlockSpec((tokens, tile), lambda i, s: (0, i))
    columns = [pl.BlockSpec((tile, depth), lambda i, s, m=m: (i, s[offset + m])) for m in range(2)]
    return pl.pallas_call(
        last_kernel,
        grid_spec=pltpu.PrefetchScalarGridSpec(
            num_scalar_prefetch=1,
            grid=(units // tile,),
            in_specs=[piece] * 4
            + columns
            + [
                tiles,
                tiles,
                pl.BlockSpec((kos, tile), lambda i, s: (0, i)),
                pl.BlockSpec((pairs, tokens), lambda i, s: (0, 0)),
                pl.BlockSpec((kis, tokens), lambda i, s: (0, 0)),
            ],
            out_specs=pl.BlockSpec((pairs, kos * kis), lambda i, s: (0, 0)),
            scratch_shapes=[pltpu.VMEM((kos, tokens), F32)],
        ),
        out_shape=jax.ShapeDtypeStruct((pairs, kos * kis), F32),
        cost_estimate=pl.CostEstimate(
            flops=2 * tokens * units * (2 * depth + kos),
            bytes_accessed=units * tokens * 8 + units * depth * 4,
            transcendentals=0,
        ),
        compiler_params=pltpu.CompilerParams(vmem_limit_bytes=VMEM_LIMIT),
    )(src, *halves, weight, weight, acc, silu, proj, pair_weight, a_up)


def swap(value, bit, devices):
    return lax.ppermute(value, "tensor", [(i, i ^ bit) for i in range(devices)])


def halves_of(value, mine, axis):
    half = value.shape[axis] // 2
    low, high = lax.slice_in_dim(value, 0, half, axis=axis), lax.slice_in_dim(value, half, 2 * half, axis=axis)
    return jnp.where(mine == 0, low, high), jnp.where(mine == 0, high, low)


def all_sum(value, me, devices, splits, axis):
    bits = [1 << i for i in range(devices.bit_length() - 1)]
    for bit in bits[:splits]:
        keep, give = halves_of(value, (me // bit) % 2, axis)
        value = keep + swap(give, bit, devices)
    for bit in bits[splits:]:
        value = value + swap(value, bit, devices)
    for bit in reversed(bits[:splits]):
        other = swap(value, bit, devices)
        mine = (me // bit) % 2
        value = jnp.where(
            mine == 0,
            jnp.concatenate([value, other], axis=axis),
            jnp.concatenate([other, value], axis=axis),
        )
    return value


def per_device(
    devices,
    activations,
    gate_pre,
    up_pre,
    out_grad,
    down_weight,
    in_proj_down,
    out_proj_down,
    in_proj_up,
    out_proj_up,
    segments,
    labels,
    queries,
):
    tokens, depth = out_grad.shape
    me = lax.axis_index("tensor")
    chips = devices // 2
    ring = ring_of(chips)
    far = chips // 2
    place = {chip: i for i, chip in enumerate(ring)}

    table = np.zeros((devices, devices), np.int32)
    for device in range(devices):
        chip, core = divmod(device, 2)
        order = [chip]
        for step in range(1, far):
            order += [ring[(place[chip] - step) % chips], ring[(place[chip] + step) % chips]]
        order.append(ring[(place[chip] + far) % chips])
        table[device] = [2 * c + k for c in order for k in (core, 1 - core)]
    src = lax.dynamic_index_in_dim(jnp.asarray(table), me, 0, keepdims=False)

    ahead = [
        (2 * ring[i] + core, 2 * ring[(i + 1) % chips] + core) for i in range(chips) for core in (0, 1)
    ]
    back = [(b, a) for a, b in ahead]

    steps = [[out_grad]]
    f = b = out_grad
    for _ in range(1, far):
        f = lax.ppermute(f, "tensor", ahead)
        b = lax.ppermute(b, "tensor", back)
        steps.append([f, b])
    f_last = lax.ppermute(f[: tokens // 2], "tensor", ahead)
    b_last = lax.ppermute(b[tokens // 2 :], "tensor", back)

    silu_gate = jax.nn.silu(gate_pre.astype(F32))
    hidden = (silu_gate * up_pre.astype(F32)).astype(BF16)
    a_down = dot_t(in_proj_down, hidden)
    own_columns = lax.dynamic_slice_in_dim(out_proj_down, me * depth, depth, axis=1)
    a_up = dot_t(in_proj_up, activations)
    b_down = dot_t(own_columns, out_grad)
    both = all_sum(jnp.concatenate([a_up, b_down], axis=0), me, devices, 4, 0)
    kis = a_up.shape[0]
    a_up, b_down = both[:kis], both[kis:]

    seq_count = labels.shape[0]
    seqs = jnp.arange(seq_count, dtype=jnp.int32)[:, None]
    signs = (2 * labels - 1).astype(F32)
    per_seq = jnp.where(segments[None, :] == seqs, signs[:, None], F32(0.0))
    pair_weight = per_seq.reshape(seq_count // 2, 2, tokens).sum(axis=1)

    kos = b_down.shape[0]
    asked = queries.shape[0]
    q = queries.reshape(asked, 2, 2, kos // 2, kis).transpose(1, 0, 3, 2, 4).reshape(2, asked, kos * kis)
    g_down = all_sum(pair_outer(pair_weight, b_down, a_down), me, devices, 1, 1)
    s_down = dot_t(g_down.astype(BF16), q[0])

    acc = None
    offset = 0
    for blocks in steps:
        lefts = [x for block in blocks for x in (block, swap(block, 1, devices))]
        acc = add_step(src, offset, lefts, down_weight, acc)
        offset += len(lefts)
    halves = [f_last, swap(f_last, 1, devices), b_last, swap(b_last, 1, devices)]
    g_up = last_step(
        src, offset, halves, down_weight, acc, silu_gate, out_proj_up, pair_weight, a_up
    )
    g_up = all_sum(g_up, me, devices, 1, 1)
    return s_down + dot_t(g_up.astype(BF16), q[1])


def solution(mesh):
    in_specs = (
        P("groups", "tensor"),
        P("groups", "tensor"),
        P("groups", "tensor"),
        P("groups", "tensor"),
        P("tensor", None),
        P(None, "tensor"),
        P(),
        P(None, "tensor"),
        P(None, "tensor"),
        P("groups"),
        P("groups"),
        P("tensor", None),
    )
    return jax.shard_map(
        functools.partial(per_device, mesh.shape["tensor"]),
        mesh=mesh,
        in_specs=in_specs,
        out_specs=P("groups", "tensor"),
        check_vma=False,
    )
```

time: 289 us -> 192 us (0.66)
  waiting for transfers between devices: 206 us -> 66.7 us
  Pallas kernels: 0 us -> 62.9 us
  matrix products: 67.3 us -> 10.9 us
  starting transfers between devices: 0.04 us -> 32.8 us
  between operations: 13.5 us -> 0.39 us
  local copies, waits for them, and re-layouts: 0.58 us -> 11 us
  other arithmetic: 1.44 us -> 7.15 us
    all_gather x1 -> x0, waiting for transfers between devices: 125 us -> none  [per_device(): piece = lax.all_gather(out_grad, 'tensor', axis=1, tiled=True)]
    psum x1 -> x0, waiting for transfers between devices: 79.8 us -> none  [per_device(): a_down, a_up, b_up = lax.psum((part_adown, part_aup, part_bup), 'tensor')]
    ppermute x0 -> x35, waiting for transfers between devices: none -> 66.7 us  [the longest x27 37.4 us: swap(): return lax.ppermute(value, 'tensor', [(i, i ^ bit) for i in range(devices)])]
    pallas_call x0 -> x6, Pallas kernels: none -> 62.9 us  [the longest x4 45.2 us: add_step(): pl.pallas_call(functools.partial(step_kernel, blocks), grid_spec=pltpu.Pr...]
    dot_general x8 -> x5, matrix products: 67.3 us -> 10.9 us  [dot_t(): lax.dot_general(left, right, (((1,), (1,)), ((), ())), preferred_element_...]
    ppermute x0 -> x35, starting transfers between devices: none -> 32.8 us  [the longest x27 24.4 us: swap(): return lax.ppermute(value, 'tensor', [(i, i ^ bit) for i in range(devices)])]
    reshape x2, local copies, waits for them, and re-layouts: 0.35 us -> 5.75 us  [per_device(): queries.reshape(asked, 2, 2, kos // 2, kis).transpose(1, 0, 3, 2, 4)]
    mul x0 -> x1, other arithmetic: none -> 4.8 us  [per_device(): silu_gate = jax.nn.silu(gate_pre.astype(F32))]
  transfers between devices with their start and end apart: 2 -> 35, of which waited for: 2 -> 15; matrix products, arithmetic and copies ran while one was open for 7% -> 13% of each run, Pallas kernels for 0% -> 25%
where the time goes in v1:
time: 192 us
  waiting for transfers between devices  66.7 us (35%)
  Pallas kernels  62.9 us (33%)
  starting transfers between devices  32.8 us (17%)
  local copies, waits for them, and re-layouts  11 us (6%)
  matrix products  10.9 us (6%)
  other arithmetic  7.15 us (4%)
    pallas_call x4, Pallas kernels, add_step(): pl.pallas_call(functools.partial(step_kernel, blocks), grid_spec=pltpu.Pr...  45.2 us
    ppermute x27, waiting for transfers between devices, swap(): return lax.ppermute(value, 'tensor', [(i, i ^ bit) for i in range(devices)])  37.4 us
    ppermute x3, waiting for transfers between devices, per_device(): f = lax.ppermute(f, 'tensor', ahead)  27.5 us
    ppermute x27, starting transfers between devices, swap(): return lax.ppermute(value, 'tensor', [(i, i ^ bit) for i in range(devices)])  24.4 us
    pallas_call x1, Pallas kernels, last_step(): pl.pallas_call(last_kernel, grid_spec=pltpu.PrefetchScalarGridSpec(num_sc...  15.7 us
    dot_general x5, matrix products, dot_t(): lax.dot_general(left, right, (((1,), (1,)), ((), ())), preferred_element_...  10.9 us
    reshape x2, local copies, waits for them, and re-layouts, per_device(): queries.reshape(asked, 2, 2, kos // 2, kis).transpose(1, 0, 3, 2, 4)  5.75 us
    ppermute x3, starting transfers between devices, per_device(): b = lax.ppermute(b, 'tensor', back)  5.65 us
  transfers between devices with their start and end apart: 35, of which 15 were waited for; matrix products, arithmetic and copies ran while one was open for 13% of the time, Pallas kernels for 25%

profile of v1, /device:TPU:0, one launch (start us, length us, event | category | flops | bytes accessed | tf_op | source)
XLA Modules:
  0.0 191.9 jit_solution(18141787426155780080)
XLA Ops:
  0.0 1.8 fusion.19
  1.8 1.7 broadcast_select_fusion
  3.5 0.5 collective-permute-start
  4.0 1.2 collective-permute-done
  5.2 3.0 %collective-permute-start.1 = (f32[32,1024]{1,0:T(8,128)S(1)}, f32[32,1024]{1,0:T(8,128)S(1)}, u32[]{:S(2)}, u32[]{:S(2)}) collective-permute-start(f32[32,1024]{1,0:T(8,128)S(1)} %slice_select_fusion), channel_id=1, source_target_pairs={{0,2},{1,3},{2,0},{3,1},{4,6},{5,7},{6,4},{7,5},{8,10},{9,11},{10,... | collective-permute-start | bytes 393224 | tf_op jit(solution)/shard_map/ppermute | solution.py:155
  8.2 3.8 %collective-permute-done.1 = f32[32,1024]{1,0:T(8,128)S(1)} collective-permute-done((f32[32,1024]{1,0:T(8,128)S(1)}, f32[32,1024]{1,0:T(8,128)S(1)}, u32[]{:S(2)}, u32[]{:S(2)}) %collective-permute-start.1) | collective-permute-done | bytes 131104 | tf_op jit(solution)/shard_map/ppermute | solution.py:155
  12.0 1.9 collective-permute-start.2
  13.9 2.5 %collective-permute-done.2 = f32[16,1024]{1,0:T(8,128)S(1)} collective-permute-done((f32[16,1024]{1,0:T(8,128)S(1)}, f32[16,1024]{1,0:T(8,128)S(1)}, u32[]{:S(2)}, u32[]{:S(2)}) %collective-permute-start.2) | collective-permute-done | bytes 65568 | tf_op jit(solution)/shard_map/ppermute | solution.py:155
  16.4 2.9 %collective-permute-start.3 = (f32[8,1024]{1,0:T(8,128)S(1)}, f32[8,1024]{1,0:T(8,128)S(1)}, u32[]{:S(2)}, u32[]{:S(2)}) collective-permute-start(f32[8,1024]{1,0:T(8,128)S(1)} %slice_select_fusion.4), channel_id=1, source_target_pairs={{0,8},{1,9},{2,10},{3,11},{4,12},{5,13},{6,14},{7,15},{8,0},{9,1},... | collective-permute-start | bytes 98312 | tf_op jit(solution)/shard_map/ppermute | solution.py:155
  19.2 2.0 %collective-permute-done.3 = f32[8,1024]{1,0:T(8,128)S(1)} collective-permute-done((f32[8,1024]{1,0:T(8,128)S(1)}, f32[8,1024]{1,0:T(8,128)S(1)}, u32[]{:S(2)}, u32[]{:S(2)}) %collective-permute-start.3) | collective-permute-done | bytes 32800 | tf_op jit(solution)/shard_map/ppermute | solution.py:155
  21.3 2.8 %collective-permute-start.4 = (f32[8,1024]{1,0:T(8,128)S(1)}, f32[8,1024]{1,0:T(8,128)S(1)}, u32[]{:S(2)}, u32[]{:S(2)}) collective-permute-start(f32[8,1024]{1,0:T(8,128)S(1)} %select_add_fusion.5), channel_id=1, source_target_pairs={{0,8},{1,9},{2,10},{3,11},{4,12},{5,13},{6,14},{7,15},{8,0},{9,1},... | collective-permute-start | bytes 98312 | tf_op jit(solution)/shard_map/ppermute | solution.py:155
  24.1 2.1 %collective-permute-done.4 = f32[8,1024]{1,0:T(8,128)S(1)} collective-permute-done((f32[8,1024]{1,0:T(8,128)S(1)}, f32[8,1024]{1,0:T(8,128)S(1)}, u32[]{:S(2)}, u32[]{:S(2)}) %collective-permute-start.4) | collective-permute-done | bytes 32800 | tf_op jit(solution)/shard_map/ppermute | solution.py:155
  26.2 2.2 %collective-permute-start.5 = (f32[16,1024]{1,0:T(8,128)S(1)}, f32[16,1024]{1,0:T(8,128)S(1)}, u32[]{:S(2)}, u32[]{:S(2)}) collective-permute-start(f32[16,1024]{1,0:T(8,128)S(1)} %maximum_select_fusion.5), channel_id=1, source_target_pairs={{0,4},{1,5},{2,6},{3,7},{4,0},{5,1},{6,2},{7,3},{8,12},{9,13},{10,... | collective-permute-start | bytes 196616 | tf_op jit(solution)/shard_map/ppermute | solution.py:155
  28.4 0.1 collective-permute-start.13
  28.5 1.9 collective-permute-start.18
  30.4 0.4 collective-permute-done.5
  30.9 1.4 collective-permute-start.6
  32.3 5.3 %fusion.4.a_ref = f32[64,1024]{1,0:T(8,128)S(1)} fusion(bf16[64,1792]{1,0:T(8,128)(2,1)} %param.18, bf16[1024,1792]{1,0:T(8,128)(2,1)} %param.15, bf16[1024,1792]{1,0:T(8,128)(2,1)} %param.14), kind=kOutput, calls=%fused_computation.8 | convolution fusion | flops 249561088 | bytes 7831552 | tf_op jit(solution)/shard_map/dot_general | solution.py:16
  37.6 19.4 %collective-permute-done.6 = f32[32,1024]{1,0:T(8,128)S(1)} collective-permute-done((f32[32,1024]{1,0:T(8,128)S(1)}, f32[32,1024]{1,0:T(8,128)S(1)}, u32[]{:S(2)}, u32[]{:S(2)}) %collective-permute-start.6) | collective-permute-done | bytes 131104 | tf_op jit(solution)/shard_map/ppermute | solution.py:155
  57.0 0.7 maximum_select_fusion.1
  57.7 0.5 collective-permute-start.27
  58.2 2.0 %collective-permute-start.19 = (bf16[1024,512]{1,0:T(8,128)(2,1)S(1)}, bf16[1024,512]{1,0:T(8,128)(2,1)}, u32[]{:S(2)}, u32[]{:S(2)}) collective-permute-start(bf16[1024,512]{1,0:T(8,128)(2,1)S(1)} %collective-permute-done.18.refs_2_), channel_id=1, source_target_pairs={{4,0},{5,1},{8,4},{9,5},{12,8},{13,9},{14,12},{15,13},{10,14},{11,... | collective-permute-start | bytes 3145736 | tf_op jit(solution)/shard_map/ppermute | solution.py:223
  60.3 4.8 %convert_multiply_fusion.silu_ref = f32[1024,1792]{1,0:T(8,128)} fusion(bf16[1024,1792]{1,0:T(8,128)(2,1)S(1)} %copy-done.4), kind=kLoop, calls=%fused_computation | loop fusion | flops 9175040 | bytes 11010048 | tf_op jit(solution)/shard_map/jit(silu)/mul | solution.py:228
  65.1 0.1 broadcast_in_dim.17
  65.2 0.1 copy.18
  65.2 18.2 %collective-permute-done.14.refs_0_ = bf16[1024,512]{1,0:T(8,128)(2,1)} collective-permute-done((bf16[1024,512]{1,0:T(8,128)(2,1)S(1)}, bf16[1024,512]{1,0:T(8,128)(2,1)}, u32[]{:S(2)}, u32[]{:S(2)}) %collective-permute-start.14) | collective-permute-done | bytes 1048608 | tf_op jit(solution)/shard_map/ppermute | solution.py:222
  83.4 0.3 collective-permute-start.15
  83.7 1.7 collective-permute-start.20
  85.4 0.7 dynamic-slice_bitcast_fusion.src_ref
  86.1 0.1 select_reduce_fusion.weight_ref
  86.2 1.3 maximum_select_fusion
  87.6 2.0 %shard_map.127 = f32[8,4096]{1,0:T(8,128)S(1)} custom-call(f32[8,1024]{1,0:T(8,128)S(1)} %select_reduce_fusion.weight_ref, f32[64,1024]{1,0:T(8,128)S(1)} %get-tuple-element.7.b_ref, f32[64,1024]{1,0:T(8,128)S(1)} %fusion.4.a_ref), custom_call_target="tpu_custom_call" | custom-call | tf_op jit(solution)/shard_map/pallas_call | solution.py:91
  89.6 0.5 collective-permute-start.26
  90.1 8.3 %shard_map.128.refs_8_ = f32[1024,1792]{1,0:T(8,128)S(1)} custom-call(s32[16]{0:T(128)S(1)} %dynamic-slice_bitcast_fusion.src_ref, bf16[1024,512]{1,0:T(8,128)(2,1)S(1)} %copy-done.2, bf16[1024,512]{1,0:T(8,128)(2,1)} %collective-permute-done.29.refs_1_, bf16[1792,8192]{1,0:T(8,128)(2,1)} %w1.1, bf16[1792,8192]{1,0:T(8,128)(2,1)} %w1.1), custom_call_target="tpu_custom_call" | custom-call | flops 3758096384 | bytes 18350080 | tf_op jit(solution)/shard_map/pallas_call | solution.py:58
  98.5 9.4 %collective-permute-done.15.refs_0_ = bf16[1024,512]{1,0:T(8,128)(2,1)S(1)} collective-permute-done((bf16[1024,512]{1,0:T(8,128)(2,1)}, bf16[1024,512]{1,0:T(8,128)(2,1)S(1)}, u32[]{:S(2)}, u32[]{:S(2)}) %collective-permute-start.15) | collective-permute-done | bytes 1048608 | tf_op jit(solution)/shard_map/ppermute | solution.py:222
  107.8 0.7 collective-permute-done.20.refs_2_
  108.6 12.3 %shard_map.129.refs_8_ = f32[1024,1792]{1,0:T(8,128)S(1)} custom-call(s32[16]{0:T(128)S(1)} %dynamic-slice_bitcast_fusion.src_ref, bf16[1024,512]{1,0:T(8,128)(2,1)S(1)} %collective-permute-done.13.refs_0_, bf16[1024,512]{1,0:T(8,128)(2,1)} %collective-permute-done.27.refs_1_, ...), custom_call_target="tpu_custom_call", output_to_operand_aliasing={{}: (9, {})} | custom-call | flops 7516192768 | bytes 22020096 | tf_op jit(solution)/shard_map/pallas_call | solution.py:58
  121.0 1.8 collective-permute-start.16
  122.8 0.5 collective-permute-start.21
  123.3 12.7 %shard_map.130.refs_8_ = f32[1024,1792]{1,0:T(8,128)S(1)} custom-call(s32[16]{0:T(128)S(1)} %dynamic-slice_bitcast_fusion.src_ref, bf16[1024,512]{1,0:T(8,128)(2,1)} %collective-permute-done.14.refs_0_, bf16[1024,512]{1,0:T(8,128)(2,1)S(1)} %collective-permute-done.25.refs_1_, ...), custom_call_target="tpu_custom_call", output_to_operand_aliasing={{}: (9, {})} | custom-call | flops 7516192768 | bytes 22020096 | tf_op jit(solution)/shard_map/pallas_call | solution.py:58
  136.0 0.1 collective-permute-start.17
  136.1 1.0 collective-permute-done.21.b0
  137.1 11.9 %shard_map.131.acc_ref = f32[1024,1792]{1,0:T(8,128)S(1)} custom-call(s32[16]{0:T(128)S(1)} %dynamic-slice_bitcast_fusion.src_ref, bf16[1024,512]{1,0:T(8,128)(2,1)S(1)} %collective-permute-done.15.refs_0_, bf16[1024,512]{1,0:T(8,128)(2,1)S(1)} %collective-permute-done.23.refs_1_, ...), custom_call_target="tpu_custom_call", output_to_operand_aliasing={{}: (9, {})} | custom-call | flops 7516192768 | bytes 22020096 | tf_op jit(solution)/shard_map/pallas_call | solution.py:58
  149.1 15.7 %shard_map.132 = f32[8,4096]{1,0:T(8,128)S(1)} custom-call(s32[16]{0:T(128)S(1)} %dynamic-slice_bitcast_fusion.src_ref, bf16[512,512]{1,0:T(8,128)(2,1)S(1)} %collective-permute-done.16.f0, bf16[512,512]{1,0:T(8,128)(2,1)S(1)} %collective-permute-done.17.f1, bf16[512,512]{1,0:T(8,128)(2,1)S(1)} %collective-permute-done.21.b0, ...), custom_call_target="tpu_custom_call" | custom-call | flops 3992977408 | bytes 18350080 | tf_op jit(solution)/shard_map/pallas_call | solution.py:127
  164.8 0.6 collective-permute-start.30
  165.4 0.1 collective-permute-start.8
  165.5 0.8 collective-permute-done.30
  166.3 0.9 collective-permute-start.31
  167.2 1.3 collective-permute-start.9
  168.5 2.8 %collective-permute-done.31 = f32[8,2048]{1,0:T(8,128)S(1)} collective-permute-done((f32[8,2048]{1,0:T(8,128)S(1)}, f32[8,2048]{1,0:T(8,128)S(1)}, u32[]{:S(2)}, u32[]{:S(2)}) %collective-permute-start.31) | collective-permute-done | bytes 65568 | tf_op jit(solution)/shard_map/ppermute | solution.py:155
  171.3 1.8 collective-permute-start.32
  173.1 0.8 collective-permute-start.10
  174.0 1.9 %collective-permute-done.32 = f32[8,2048]{1,0:T(8,128)S(1)} collective-permute-done((f32[8,2048]{1,0:T(8,128)S(1)}, f32[8,2048]{1,0:T(8,128)S(1)}, u32[]{:S(2)}, u32[]{:S(2)}) %collective-permute-start.32) | collective-permute-done | bytes 65568 | tf_op jit(solution)/shard_map/ppermute | solution.py:155
  175.9 2.0 %collective-permute-start.33 = (f32[8,2048]{1,0:T(8,128)S(1)}, f32[8,2048]{1,0:T(8,128)S(1)}, u32[]{:S(2)}, u32[]{:S(2)}) collective-permute-start(f32[8,2048]{1,0:T(8,128)S(1)} %add.97), channel_id=1, source_target_pairs={{0,8},{1,9},{2,10},{3,11},{4,12},{5,13},{6,14},{7,15},{8,0},{9,1},... | collective-permute-start | bytes 196616 | tf_op jit(solution)/shard_map/ppermute | solution.py:155
  177.9 3.3 %reshape.30 = bf16[64,2,2,32,64]{4,3,2,1,0:T(8,128)(2,1)S(1)} reshape(bf16[64,8192]{1,0:T(8,128)(2,1)} %param.24) | data formatting | bytes 2097152 | tf_op jit(solution)/shard_map/reshape | solution.py:246
  181.3 2.4 %copy.21 = bf16[64,2,2,32,64]{4,2,3,0,1:T(2,128)(2,1)S(1)} copy(bf16[64,2,2,32,64]{4,3,2,1,0:T(8,128)(2,1)S(1)} %reshape.30) | data formatting | bytes 2097152 | tf_op jit(solution)/shard_map/reshape | solution.py:246
  183.7 1.0 collective-permute-start.11
  184.8 0.1 collective-permute-start.34
  184.9 1.8 fusion.17
  186.7 1.6 squeeze.12
  188.3 0.8 squeeze.10
  189.1 0.5 collective-permute-done.11
  189.8 1.3 fusion.7
  191.0 0.9 convolution_add_fusion
  (67 shorter events, 0.6 us)
Async XLA Ops:
  0.0 1.8 copy-start
  3.5 1.7 collective-permute-start
  5.2 6.8 %collective-permute-start.1 = (f32[32,1024]{1,0:T(8,128)S(1)}, f32[32,1024]{1,0:T(8,128)S(1)}, u32[]{:S(2)}, u32[]{:S(2)}) collective-permute-start(f32[32,1024]{1,0:T(8,128)S(1)} %slice_select_fusion), channel_id=1, source_target_pairs={{0,2},{1,3},{2,0},{3,1},{4,6},{5,7},{6,4},{7,5},{8,10},{9,11},{10,... | collective-permute-start | bytes 393224 | tf_op jit(solution)/shard_map/ppermute | solution.py:155
  12.0 4.3 %collective-permute-start.2 = (f32[16,1024]{1,0:T(8,128)S(1)}, f32[16,1024]{1,0:T(8,128)S(1)}, u32[]{:S(2)}, u32[]{:S(2)}) collective-permute-start(f32[16,1024]{1,0:T(8,128)S(1)} %slice_select_fusion.3), channel_id=1, source_target_pairs={{0,4},{1,5},{2,6},{3,7},{4,0},{5,1},{6,2},{7,3},{8,12},{9,13},{10,... | collective-permute-start | bytes 196616 | tf_op jit(solution)/shard_map/ppermute | solution.py:155
  16.4 4.9 %collective-permute-start.3 = (f32[8,1024]{1,0:T(8,128)S(1)}, f32[8,1024]{1,0:T(8,128)S(1)}, u32[]{:S(2)}, u32[]{:S(2)}) collective-permute-start(f32[8,1024]{1,0:T(8,128)S(1)} %slice_select_fusion.4), channel_id=1, source_target_pairs={{0,8},{1,9},{2,10},{3,11},{4,12},{5,13},{6,14},{7,15},{8,0},{9,1},... | collective-permute-start | bytes 98312 | tf_op jit(solution)/shard_map/ppermute | solution.py:155
  21.3 4.9 %collective-permute-start.4 = (f32[8,1024]{1,0:T(8,128)S(1)}, f32[8,1024]{1,0:T(8,128)S(1)}, u32[]{:S(2)}, u32[]{:S(2)}) collective-permute-start(f32[8,1024]{1,0:T(8,128)S(1)} %select_add_fusion.5), channel_id=1, source_target_pairs={{0,8},{1,9},{2,10},{3,11},{4,12},{5,13},{6,14},{7,15},{8,0},{9,1},... | collective-permute-start | bytes 98312 | tf_op jit(solution)/shard_map/ppermute | solution.py:155
  26.2 4.7 %collective-permute-start.5 = (f32[16,1024]{1,0:T(8,128)S(1)}, f32[16,1024]{1,0:T(8,128)S(1)}, u32[]{:S(2)}, u32[]{:S(2)}) collective-permute-start(f32[16,1024]{1,0:T(8,128)S(1)} %maximum_select_fusion.5), channel_id=1, source_target_pairs={{0,4},{1,5},{2,6},{3,7},{4,0},{5,1},{6,2},{7,3},{8,12},{9,13},{10,... | collective-permute-start | bytes 196616 | tf_op jit(solution)/shard_map/ppermute | solution.py:155
  28.4 61.2 %collective-permute-start.29 = (bf16[1024,512]{1,0:T(8,128)(2,1)}, bf16[1024,512]{1,0:T(8,128)(2,1)}, u32[]{:S(2)}, u32[]{:S(2)}) collective-permute-start(bf16[1024,512]{1,0:T(8,128)(2,1)} %refs_0_.1), channel_id=1, source_target_pairs={{0,1},{1,0},{2,3},{3,2},{4,5},{5,4},{6,7},{7,6},{8,9},{9,8},{10,11... | collective-permute-start | bytes 3145736 | tf_op jit(solution)/shard_map/ppermute | solution.py:155
  28.4 29.3 %collective-permute-start.13 = (bf16[1024,512]{1,0:T(8,128)(2,1)}, bf16[1024,512]{1,0:T(8,128)(2,1)S(1)}, u32[]{:S(2)}, u32[]{:S(2)}) collective-permute-start(bf16[1024,512]{1,0:T(8,128)(2,1)} %refs_0_.1), channel_id=1, source_target_pairs={{0,4},{1,5},{4,8},{5,9},{8,12},{9,13},{12,14},{13,15},{14,10},{15,... | collective-permute-start | bytes 3145736 | tf_op jit(solution)/shard_map/ppermute | solution.py:222
  28.5 29.7 %collective-permute-start.18 = (bf16[1024,512]{1,0:T(8,128)(2,1)}, bf16[1024,512]{1,0:T(8,128)(2,1)S(1)}, u32[]{:S(2)}, u32[]{:S(2)}) collective-permute-start(bf16[1024,512]{1,0:T(8,128)(2,1)} %refs_0_.1), channel_id=1, source_target_pairs={{4,0},{5,1},{8,4},{9,5},{12,8},{13,9},{14,12},{15,13},{10,14},{11,... | collective-permute-start | bytes 3145736 | tf_op jit(solution)/shard_map/ppermute | solution.py:223
  30.9 29.4 %copy-start.4 = (bf16[1024,1792]{1,0:T(8,128)(2,1)S(1)}, bf16[1024,1792]{1,0:T(8,128)(2,1)}, u32[]{:S(2)}) copy-start(bf16[1024,1792]{1,0:T(8,128)(2,1)} %param.14) | copy-start | bytes 11010052
  30.9 26.1 %collective-permute-start.6 = (f32[32,1024]{1,0:T(8,128)S(1)}, f32[32,1024]{1,0:T(8,128)S(1)}, u32[]{:S(2)}, u32[]{:S(2)}) collective-permute-start(f32[32,1024]{1,0:T(8,128)S(1)} %maximum_select_fusion.2), channel_id=1, source_target_pairs={{0,2},{1,3},{2,0},{3,1},{4,6},{5,7},{6,4},{7,5},{8,10},{9,11},{10,... | collective-permute-start | bytes 393224 | tf_op jit(solution)/shard_map/ppermute | solution.py:155
  37.6 27.5 %copy-start.6 = (s32[16]{0:T(128)S(1)}, s32[16]{0:T(128)}, u32[]{:S(2)}) copy-start(s32[16]{0:T(128)} %param.23) | copy-start | bytes 196
  37.6 48.5 %copy-start.5 = (s32[1024]{0:T(1024)S(1)}, s32[1024]{0:T(1024)}, u32[]{:S(2)}) copy-start(s32[1024]{0:T(1024)} %param.22) | copy-start | bytes 12292
  37.6 52.5 %copy-start.2 = (bf16[1024,512]{1,0:T(8,128)(2,1)S(1)}, bf16[1024,512]{1,0:T(8,128)(2,1)}, u32[]{:S(2)}) copy-start(bf16[1024,512]{1,0:T(8,128)(2,1)} %refs_0_.1) | copy-start | bytes 3145732
  57.7 7.5 %collective-permute-start.7 = (f32[64,1024]{1,0:T(8,128)}, f32[64,1024]{1,0:T(8,128)}, u32[]{:S(2)}, u32[]{:S(2)}) collective-permute-start(f32[64,1024]{1,0:T(8,128)} %maximum_select_fusion.1), channel_id=1, source_target_pairs={{0,1},{1,0},{2,3},{3,2},{4,5},{5,4},{6,7},{7,6},{8,9},{9,8},{10,11... | collective-permute-start | bytes 786440 | tf_op jit(solution)/shard_map/ppermute | solution.py:155
  57.7 31.9 %collective-permute-start.27 = (bf16[1024,512]{1,0:T(8,128)(2,1)S(1)}, bf16[1024,512]{1,0:T(8,128)(2,1)}, u32[]{:S(2)}, u32[]{:S(2)}) collective-permute-start(bf16[1024,512]{1,0:T(8,128)(2,1)S(1)} %collective-permute-done.13.refs_0_), channel_id=1, source_target_pairs={{0,1},{1,0},{2,3},{3,2},{4,5},{5,4},{6,7},{7,6},{8,9},{9,8},{10,11... | collective-permute-start | bytes 3145736 | tf_op jit(solution)/shard_map/ppermute | solution.py:155
  58.2 25.2 %collective-permute-start.14 = (bf16[1024,512]{1,0:T(8,128)(2,1)S(1)}, bf16[1024,512]{1,0:T(8,128)(2,1)}, u32[]{:S(2)}, u32[]{:S(2)}) collective-permute-start(bf16[1024,512]{1,0:T(8,128)(2,1)S(1)} %collective-permute-done.13.refs_0_), channel_id=1, source_target_pairs={{0,4},{1,5},{4,8},{5,9},{8,12},{9,13},{12,14},{13,15},{14,10},{15,... | collective-permute-start | bytes 3145736 | tf_op jit(solution)/shard_map/ppermute | solution.py:222
  58.2 25.5 %collective-permute-start.19 = (bf16[1024,512]{1,0:T(8,128)(2,1)S(1)}, bf16[1024,512]{1,0:T(8,128)(2,1)}, u32[]{:S(2)}, u32[]{:S(2)}) collective-permute-start(bf16[1024,512]{1,0:T(8,128)(2,1)S(1)} %collective-permute-done.18.refs_2_), channel_id=1, source_target_pairs={{4,0},{5,1},{8,4},{9,5},{12,8},{13,9},{14,12},{15,13},{10,14},{11,... | collective-permute-start | bytes 3145736 | tf_op jit(solution)/shard_map/ppermute | solution.py:223
  65.2 43.3 %collective-permute-start.28 = (bf16[1024,512]{1,0:T(8,128)(2,1)S(1)}, bf16[1024,512]{1,0:T(8,128)(2,1)S(1)}, u32[]{:S(2)}, u32[]{:S(2)}) collective-permute-start(bf16[1024,512]{1,0:T(8,128)(2,1)S(1)} %collective-permute-done.18.refs_2_), channel_id=1, source_target_pairs={{0,1},{1,0},{2,3},{3,2},{4,5},{5,4},{6,7},{7,6},{8,9},{9,8},{10,11... | collective-permute-start | bytes 3145736 | tf_op jit(solution)/shard_map/ppermute | solution.py:155
  83.4 24.4 %collective-permute-start.15 = (bf16[1024,512]{1,0:T(8,128)(2,1)}, bf16[1024,512]{1,0:T(8,128)(2,1)S(1)}, u32[]{:S(2)}, u32[]{:S(2)}) collective-permute-start(bf16[1024,512]{1,0:T(8,128)(2,1)} %collective-permute-done.14.refs_0_), channel_id=1, source_target_pairs={{0,4},{1,5},{4,8},{5,9},{8,12},{9,13},{12,14},{13,15},{14,10},{15,... | collective-permute-start | bytes 3145736 | tf_op jit(solution)/shard_map/ppermute | solution.py:222
  83.7 24.9 %collective-permute-start.20 = (bf16[1024,512]{1,0:T(8,128)(2,1)}, bf16[1024,512]{1,0:T(8,128)(2,1)S(1)}, u32[]{:S(2)}, u32[]{:S(2)}) collective-permute-start(bf16[1024,512]{1,0:T(8,128)(2,1)} %collective-permute-done.19.refs_2_), channel_id=1, source_target_pairs={{4,0},{5,1},{8,4},{9,5},{12,8},{13,9},{14,12},{15,13},{10,14},{11,... | collective-permute-start | bytes 3145736 | tf_op jit(solution)/shard_map/ppermute | solution.py:223
  89.6 33.2 %collective-permute-start.25 = (bf16[1024,512]{1,0:T(8,128)(2,1)}, bf16[1024,512]{1,0:T(8,128)(2,1)S(1)}, u32[]{:S(2)}, u32[]{:S(2)}) collective-permute-start(bf16[1024,512]{1,0:T(8,128)(2,1)} %collective-permute-done.14.refs_0_), channel_id=1, source_target_pairs={{0,1},{1,0},{2,3},{3,2},{4,5},{5,4},{6,7},{7,6},{8,9},{9,8},{10,11... | collective-permute-start | bytes 3145736 | tf_op jit(solution)/shard_map/ppermute | solution.py:155
  89.6 33.7 %collective-permute-start.26 = (bf16[1024,512]{1,0:T(8,128)(2,1)}, bf16[1024,512]{1,0:T(8,128)(2,1)S(1)}, u32[]{:S(2)}, u32[]{:S(2)}) collective-permute-start(bf16[1024,512]{1,0:T(8,128)(2,1)} %collective-permute-done.19.refs_2_), channel_id=1, source_target_pairs={{0,1},{1,0},{2,3},{3,2},{4,5},{5,4},{6,7},{7,6},{8,9},{9,8},{10,11... | collective-permute-start | bytes 3145736 | tf_op jit(solution)/shard_map/ppermute | solution.py:155
  107.8 29.3 %collective-permute-start.23 = (bf16[1024,512]{1,0:T(8,128)(2,1)S(1)}, bf16[1024,512]{1,0:T(8,128)(2,1)S(1)}, u32[]{:S(2)}, u32[]{:S(2)}) collective-permute-start(bf16[1024,512]{1,0:T(8,128)(2,1)S(1)} %collective-permute-done.15.refs_0_), channel_id=1, source_target_pairs={{0,1},{1,0},{2,3},{3,2},{4,5},{5,4},{6,7},{7,6},{8,9},{9,8},{10,11... | collective-permute-start | bytes 3145736 | tf_op jit(solution)/shard_map/ppermute | solution.py:155
  108.6 28.5 %collective-permute-start.24 = (bf16[1024,512]{1,0:T(8,128)(2,1)S(1)}, bf16[1024,512]{1,0:T(8,128)(2,1)S(1)}, u32[]{:S(2)}, u32[]{:S(2)}) collective-permute-start(bf16[1024,512]{1,0:T(8,128)(2,1)S(1)} %collective-permute-done.20.refs_2_), channel_id=1, source_target_pairs={{0,1},{1,0},{2,3},{3,2},{4,5},{5,4},{6,7},{7,6},{8,9},{9,8},{10,11... | collective-permute-start | bytes 3145736 | tf_op jit(solution)/shard_map/ppermute | solution.py:155
  121.0 15.0 %collective-permute-start.16 = (bf16[512,512]{1,0:T(8,128)(2,1)S(1)}, bf16[512,512]{1,0:T(8,128)(2,1)S(1)}, u32[]{:S(2)}, u32[]{:S(2)}) collective-permute-start(bf16[512,512]{1,0:T(8,128)(2,1)S(1)} %slice.76), channel_id=1, source_target_pairs={{0,4},{1,5},{4,8},{5,9},{8,12},{9,13},{12,14},{13,15},{14,10},{15,... | collective-permute-start | bytes 1572872 | tf_op jit(solution)/shard_map/ppermute | solution.py:225
  122.8 14.3 %collective-permute-start.21 = (bf16[512,512]{1,0:T(8,128)(2,1)S(1)}, bf16[512,512]{1,0:T(8,128)(2,1)S(1)}, u32[]{:S(2)}, u32[]{:S(2)}) collective-permute-start(bf16[512,512]{1,0:T(8,128)(2,1)S(1)} %slice.77), channel_id=1, source_target_pairs={{4,0},{5,1},{8,4},{9,5},{12,8},{13,9},{14,12},{15,13},{10,14},{11,... | collective-permute-start | bytes 1572872 | tf_op jit(solution)/shard_map/ppermute | solution.py:226
  136.0 13.1 %copy-start.3 = (bf16[64,1792]{1,0:T(8,128)(2,1)S(1)}, bf16[64,1792]{1,0:T(8,128)(2,1)}, u32[]{:S(2)}) copy-start(bf16[64,1792]{1,0:T(8,128)(2,1)} %proj_ref.1) | copy-start | bytes 688132
  136.0 13.0 %collective-permute-start.17 = (bf16[512,512]{1,0:T(8,128)(2,1)S(1)}, bf16[512,512]{1,0:T(8,128)(2,1)S(1)}, u32[]{:S(2)}, u32[]{:S(2)}) collective-permute-start(bf16[512,512]{1,0:T(8,128)(2,1)S(1)} %collective-permute-done.16.f0), channel_id=1, source_target_pairs={{0,1},{1,0},{2,3},{3,2},{4,5},{5,4},{6,7},{7,6},{8,9},{9,8},{10,11... | collective-permute-start | bytes 1572872 | tf_op jit(solution)/shard_map/ppermute | solution.py:155
  137.1 11.9 %collective-permute-start.22 = (bf16[512,512]{1,0:T(8,128)(2,1)S(1)}, bf16[512,512]{1,0:T(8,128)(2,1)S(1)}, u32[]{:S(2)}, u32[]{:S(2)}) collective-permute-start(bf16[512,512]{1,0:T(8,128)(2,1)S(1)} %collective-permute-done.21.b0), channel_id=1, source_target_pairs={{0,1},{1,0},{2,3},{3,2},{4,5},{5,4},{6,7},{7,6},{8,9},{9,8},{10,11... | collective-permute-start | bytes 1572872 | tf_op jit(solution)/shard_map/ppermute | solution.py:155
  164.8 1.5 collective-permute-start.30
  165.4 1.8 collective-permute-start.8
  166.3 5.0 %collective-permute-start.31 = (f32[8,2048]{1,0:T(8,128)S(1)}, f32[8,2048]{1,0:T(8,128)S(1)}, u32[]{:S(2)}, u32[]{:S(2)}) collective-permute-start(f32[8,2048]{1,0:T(8,128)S(1)} %select_add_fusion.2), channel_id=1, source_target_pairs={{0,2},{1,3},{2,0},{3,1},{4,6},{5,7},{6,4},{7,5},{8,10},{9,11},{10,... | collective-permute-start | bytes 196616 | tf_op jit(solution)/shard_map/ppermute | solution.py:155
  167.2 5.9 %collective-permute-start.9 = (f32[8,2048]{1,0:T(8,128)S(1)}, f32[8,2048]{1,0:T(8,128)S(1)}, u32[]{:S(2)}, u32[]{:S(2)}) collective-permute-start(f32[8,2048]{1,0:T(8,128)S(1)} %select_add_fusion.3), channel_id=1, source_target_pairs={{0,2},{1,3},{2,0},{3,1},{4,6},{5,7},{6,4},{7,5},{8,10},{9,11},{10,... | collective-permute-start | bytes 196616 | tf_op jit(solution)/shard_map/ppermute | solution.py:155
  171.3 4.6 %collective-permute-start.32 = (f32[8,2048]{1,0:T(8,128)S(1)}, f32[8,2048]{1,0:T(8,128)S(1)}, u32[]{:S(2)}, u32[]{:S(2)}) collective-permute-start(f32[8,2048]{1,0:T(8,128)S(1)} %add.96), channel_id=1, source_target_pairs={{0,4},{1,5},{2,6},{3,7},{4,0},{5,1},{6,2},{7,3},{8,12},{9,13},{10,... | collective-permute-start | bytes 196616 | tf_op jit(solution)/shard_map/ppermute | solution.py:155
  173.1 10.6 %collective-permute-start.10 = (f32[8,2048]{1,0:T(8,128)S(1)}, f32[8,2048]{1,0:T(8,128)S(1)}, u32[]{:S(2)}, u32[]{:S(2)}) collective-permute-start(f32[8,2048]{1,0:T(8,128)S(1)} %add.91), channel_id=1, source_target_pairs={{0,4},{1,5},{2,6},{3,7},{4,0},{5,1},{6,2},{7,3},{8,12},{9,13},{10,... | collective-permute-start | bytes 196616 | tf_op jit(solution)/shard_map/ppermute | solution.py:155
  175.9 8.9 %collective-permute-start.33 = (f32[8,2048]{1,0:T(8,128)S(1)}, f32[8,2048]{1,0:T(8,128)S(1)}, u32[]{:S(2)}, u32[]{:S(2)}) collective-permute-start(f32[8,2048]{1,0:T(8,128)S(1)} %add.97), channel_id=1, source_target_pairs={{0,8},{1,9},{2,10},{3,11},{4,12},{5,13},{6,14},{7,15},{8,0},{9,1},... | collective-permute-start | bytes 196616 | tf_op jit(solution)/shard_map/ppermute | solution.py:155
  177.9 14.0 %copy-start.1 = (bf16[64,8192]{1,0:T(8,128)(2,1)S(1)}, bf16[64,8192]{1,0:T(8,128)(2,1)}, u32[]{:S(2)}) copy-start(bf16[64,8192]{1,0:T(8,128)(2,1)} %param.19) | copy-start | bytes 3145732
  183.7 5.9 %collective-permute-start.11 = (f32[8,2048]{1,0:T(8,128)S(1)}, f32[8,2048]{1,0:T(8,128)S(1)}, u32[]{:S(2)}, u32[]{:S(2)}) collective-permute-start(f32[8,2048]{1,0:T(8,128)S(1)} %add.92), channel_id=1, source_target_pairs={{0,8},{1,9},{2,10},{3,11},{4,12},{5,13},{6,14},{7,15},{8,0},{9,1},... | collective-permute-start | bytes 196616 | tf_op jit(solution)/shard_map/ppermute | solution.py:155
  184.8 5.0 %collective-permute-start.34 = (bf16[8,2048]{1,0:T(8,128)(2,1)S(1)}, bf16[8,2048]{1,0:T(8,128)(2,1)S(1)}, u32[]{:S(2)}, u32[]{:S(2)}) collective-permute-start(bf16[8,2048]{1,0:T(8,128)(2,1)S(1)} %add.98), channel_id=1, source_target_pairs={{0,1},{1,0},{2,3},{3,2},{4,5},{5,4},{6,7},{7,6},{8,9},{9,8},{10,11... | collective-permute-start | bytes 98312 | tf_op jit(solution)/shard_map/ppermute | solution.py:155
  189.7 1.4 collective-permute-start.12

commit v2 on v0

v2 whole, which is shorter than its diff:
```python
import functools

import jax
import jax.numpy as jnp
import numpy as np
from jax import lax
from jax.experimental import pallas as pl
from jax.experimental.pallas import tpu as pltpu
from jax.sharding import PartitionSpec as P

F32, BF16 = jnp.float32, jnp.bfloat16
VMEM_LIMIT = 30 * 1024 * 1024
SMALL = pl.CostEstimate(flops=1000, bytes_accessed=1000, transcendentals=0)


def dot_t(left, right, precision=None):
    return lax.dot_general(
        left, right, (((1,), (1,)), ((), ())), preferred_element_type=F32, precision=precision
    )


def ring_of(chips):
    if chips == 8:
        return [0, 2, 4, 6, 7, 5, 3, 1]
    return list(range(chips))


def tile_of(units):
    return 256 if units % 256 == 0 else units


def products(lefts, columns, which):
    total = None
    for left, m in zip(lefts, which):
        part = dot_t(left[...], columns[m][...])
        total = part if total is None else total + part
    return total


def step_kernel(which, src_ref, *refs):
    blocks, owners = len(which[0]), 1 + max(map(max, which))
    lefts, weights = refs[: 2 * blocks], refs[2 * blocks : 2 * blocks + owners]
    before_ref = refs[-2] if len(refs) == 2 * blocks + owners + 2 else None
    out_ref = refs[-1]
    half = out_ref.shape[0] // 2
    for i in range(2):
        rows = slice(i * half, (i + 1) * half)
        total = products(lefts[i * blocks : (i + 1) * blocks], weights, which[i])
        out_ref[rows, :] = total if before_ref is None else total + before_ref[rows, :]


def b_step_kernel(which, src_ref, *refs):
    blocks, owners = len(which[0]), 1 + max(map(max, which))
    lefts, weights = refs[: 2 * blocks], refs[2 * blocks : 2 * blocks + owners]
    acc_ref, silu_ref, proj_ref, out_ref, ups = refs[2 * blocks + owners :]
    step, tile = pl.program_id(0), acc_ref.shape[1]
    half = acc_ref.shape[0] // 2
    for i in range(2):
        rows = slice(i * half, (i + 1) * half)
        total = products(lefts[i * blocks : (i + 1) * blocks], weights, which[i])
        ups[step, rows, :] = ((total + acc_ref[rows, :]) * silu_ref[rows, :]).astype(BF16)

    @pl.when(step == ups.shape[0] - 1)
    def _():
        out_ref[...] = projected(ups, proj_ref)


def projected(ups, proj_ref):
    total, tile = None, ups.shape[2]
    for i in range(ups.shape[0]):
        part = dot_t(ups[i], proj_ref[:, i * tile : (i + 1) * tile])
        total = part if total is None else total + part
    return total


def in_hbm(x):
    return pltpu.with_memory_space_constraint(x, pltpu.HBM)


def in_vmem(x):
    return pltpu.with_memory_space_constraint(x, pltpu.VMEM)


def step_parts(units, half, weight):
    depth = units[0][0][0].shape[1]
    tile = tile_of(weight.shape[0])
    places = sorted({place for unit in units for _, _, place in unit})
    ins, specs, which = [], [], []
    for i in range(2):
        for array, row, _ in (unit[i] for unit in units):
            ins.append(in_hbm(array))
            specs.append(pl.BlockSpec((half, depth), lambda i, s, r=row: (r, 0)))
        which.append([places.index(unit[i][2]) for unit in units])
    ins += [in_hbm(weight)] * len(places)
    specs += [pl.BlockSpec((tile, depth), lambda i, s, m=m: (i, s[m])) for m in places]
    return ins, specs, which, tile


def add_step(src, half, units, weight, before):
    ins, specs, which, tile = step_parts(units, half, weight)
    hidden, tokens = weight.shape[0], 2 * half
    tiles = pl.BlockSpec((tokens, tile), lambda i, s: (0, i))
    aliases = {}
    if before is not None:
        ins.append(in_hbm(before))
        specs.append(tiles)
        aliases = {len(ins): 0}
    return pl.pallas_call(
        functools.partial(step_kernel, which),
        grid_spec=pltpu.PrefetchScalarGridSpec(
            num_scalar_prefetch=1, grid=(hidden // tile,), in_specs=specs, out_specs=tiles
        ),
        out_shape=pltpu.HBM((tokens, hidden), F32),
        input_output_aliases=aliases,
        cost_estimate=SMALL,
        compiler_params=pltpu.CompilerParams(vmem_limit_bytes=VMEM_LIMIT),
    )(src, *ins)


def b_step(src, half, units, weight, before, silu, proj_up):
    ins, specs, which, tile = step_parts(units, half, weight)
    hidden, tokens, kos = weight.shape[0], 2 * half, proj_up.shape[0]
    tiles = pl.BlockSpec((tokens, tile), lambda i, s: (0, i))
    return pl.pallas_call(
        functools.partial(b_step_kernel, which),
        grid_spec=pltpu.PrefetchScalarGridSpec(
            num_scalar_prefetch=1,
            grid=(hidden // tile,),
            in_specs=specs + [tiles, tiles, pl.BlockSpec((kos, hidden), lambda i, s: (0, 0))],
            out_specs=pl.BlockSpec((tokens, kos), lambda i, s: (0, 0)),
            scratch_shapes=[pltpu.VMEM((hidden // tile, tokens, tile), BF16)],
        ),
        out_shape=pltpu.VMEM((tokens, kos), F32),
        cost_estimate=SMALL,
        compiler_params=pltpu.CompilerParams(vmem_limit_bytes=VMEM_LIMIT),
    )(src, *ins, in_hbm(before), in_hbm(silu), proj_up)


def columns_kernel(first, src_ref, weight_ref, out_ref, sems):
    depth = out_ref.shape[2]
    copies = []
    for m in range(2):
        start = pl.multiple_of(src_ref[first + m] * depth, depth)
        copies.append(
            pltpu.make_async_copy(weight_ref.at[:, pl.ds(start, depth)], out_ref.at[m], sems.at[m])
        )
    for copy in copies:
        copy.start()
    for copy in copies:
        copy.wait()


def last_columns(src, weight, depth):
    return pl.pallas_call(
        functools.partial(columns_kernel, src.shape[0] - 2),
        grid_spec=pltpu.PrefetchScalarGridSpec(
            num_scalar_prefetch=1,
            grid=(),
            in_specs=[pl.BlockSpec(memory_space=pl.ANY)],
            out_specs=pl.BlockSpec(memory_space=pltpu.VMEM),
            scratch_shapes=[pltpu.SemaphoreType.DMA((2,))],
        ),
        out_shape=pltpu.VMEM((2, weight.shape[0], depth), BF16),
        cost_estimate=SMALL,
        compiler_params=pltpu.CompilerParams(vmem_limit_bytes=VMEM_LIMIT),
    )(src, in_hbm(weight))


def last_kernel(*refs):
    blocks = refs[:4]
    weight_ref, silu_ref, proj_ref, before_ref, high_ref, low_ref, out_ref, lefts, ups, sems = refs[4:]
    half, tile = lefts.shape[1], ups.shape[2]
    copies = [
        pltpu.make_async_copy(block, lefts.at[i], sems.at[i]) for i, block in enumerate(blocks)
    ]
    for copy in copies:
        copy.start()
    for copy in copies:
        copy.wait()
    for i in range(ups.shape[0]):
        cols = slice(i * tile, (i + 1) * tile)
        for h in range(2):
            rows = slice(h * half, (h + 1) * half)
            grad = dot_t(lefts[2 * h], weight_ref[0, cols, :]) + dot_t(
                lefts[2 * h + 1], weight_ref[1, cols, :]
            )
            ups[i, rows, :] = (grad * silu_ref[rows, cols]).astype(BF16)
    b = before_ref[...] + projected(ups, proj_ref)
    b_high = b.astype(BF16)
    b_low = (b - b_high.astype(F32)).astype(BF16)
    kos = b.shape[1]
    sums = jnp.dot(
        high_ref[...], jnp.concatenate([b_high, b_low], axis=1), preferred_element_type=F32
    )
    rest = jnp.dot(low_ref[...], b_high, preferred_element_type=F32)
    out_ref[...] = spread(sums[:, :kos] + (sums[:, kos:] + rest), out_ref.shape[0])


def last_step(blocks, columns, silu, proj_up, b_up, up, pairs):
    half, depth = blocks[0].shape
    tokens, hidden = silu.shape
    tile, kos = tile_of(hidden), proj_up.shape[0]
    whole = pl.BlockSpec(memory_space=pltpu.VMEM)
    ins = [in_vmem(x) for x in (columns, silu, proj_up, b_up, *up)]
    return pl.pallas_call(
        last_kernel,
        in_specs=[pl.BlockSpec(memory_space=pl.ANY)] * 4 + [whole] * len(ins),
        out_specs=whole,
        out_shape=jax.ShapeDtypeStruct((pairs, up[0].shape[0] // pairs * kos), F32),
        scratch_shapes=[
            pltpu.VMEM((4, half, depth), BF16),
            pltpu.VMEM((hidden // tile, tokens, tile), BF16),
            pltpu.SemaphoreType.DMA((4,)),
        ],
        cost_estimate=SMALL,
        compiler_params=pltpu.CompilerParams(vmem_limit_bytes=VMEM_LIMIT),
    )(*[in_hbm(x) for x in blocks], *ins)


def own_kernel(gate_ref, up_ref, down_ref, silu_ref, out_ref, hidden):
    step, tile = pl.program_id(0), gate_ref.shape[1]
    gate = gate_ref[...].astype(F32)
    silu = gate / (1.0 + jnp.exp(-gate))
    silu_ref[...] = silu
    hidden[step] = (silu * up_ref[...].astype(F32)).astype(BF16)

    @pl.when(step == hidden.shape[0] - 1)
    def _():
        total = None
        for i in range(hidden.shape[0]):
            part = dot_t(down_ref[:, i * tile : (i + 1) * tile], hidden[i])
            total = part if total is None else total + part
        out_ref[...] = total


def own_parts(gate, up, in_down):
    tokens, units = gate.shape
    tile, kis = tile_of(units), in_down.shape[0]
    tiles = pl.BlockSpec((tokens, tile), lambda i: (0, i))
    return pl.pallas_call(
        own_kernel,
        grid=(units // tile,),
        in_specs=[tiles, tiles, pl.BlockSpec((kis, units), lambda i: (0, 0))],
        out_specs=(tiles, pl.BlockSpec((kis, tokens), lambda i: (0, 0))),
        out_shape=(pltpu.HBM((tokens, units), F32), jax.ShapeDtypeStruct((kis, tokens), F32)),
        scratch_shapes=[pltpu.VMEM((units // tile, tokens, tile), BF16)],
        cost_estimate=SMALL,
        compiler_params=pltpu.CompilerParams(vmem_limit_bytes=VMEM_LIMIT),
    )(in_hbm(gate), in_hbm(up), in_down)


def turned(q, kos):
    asked, size = q.shape[0], q.shape[1] // 2
    kis = size // kos

    def kernel(q_ref, out_ref, rows):
        rows[...] = q_ref[...].astype(F32).T
        for j in range(kis):
            out_ref[j * kos : (j + 1) * kos, :] = rows[pl.ds(j, kos, stride=kis), :].astype(BF16)

    return pl.pallas_call(
        kernel,
        grid=(2,),
        in_specs=[pl.BlockSpec((asked, size), lambda i: (0, i))],
        out_specs=pl.BlockSpec((size, asked), lambda i: (i, 0)),
        out_shape=jax.ShapeDtypeStruct((2 * size, asked), BF16),
        scratch_shapes=[pltpu.VMEM((size, asked), F32)],
        cost_estimate=SMALL,
        compiler_params=pltpu.CompilerParams(vmem_limit_bytes=VMEM_LIMIT),
    )(in_hbm(q))


def score_kernel(down_ref, up_ref, q_ref, out_ref):
    size = down_ref.shape[1]
    out_ref[...] = jnp.dot(
        down_ref[...].astype(BF16), q_ref[:size, :], preferred_element_type=F32
    ) + jnp.dot(up_ref[...].astype(BF16), q_ref[size:, :], preferred_element_type=F32)


def score(down, up, q):
    return pl.pallas_call(
        score_kernel,
        out_shape=jax.ShapeDtypeStruct((down.shape[0], q.shape[1]), F32),
        cost_estimate=SMALL,
        compiler_params=pltpu.CompilerParams(vmem_limit_bytes=VMEM_LIMIT),
    )(down, up, q)


def weighted(weight, a):
    left = jnp.concatenate([weight * a[j : j + 1, :] for j in range(a.shape[0])], axis=0)
    high = left.astype(BF16)
    return high, (left - high.astype(F32)).astype(BF16)


def spread(sums, pairs):
    return jnp.concatenate([sums[r : r + pairs] for r in range(0, sums.shape[0], pairs)], axis=1)


def first_kernel(core_ref, acts_ref, grad_ref, in_up_ref, columns_ref, keep_ref, give_ref):
    first = core_ref[0] == 0
    a, b = dot_t(in_up_ref[...], acts_ref[...]), dot_t(columns_ref[...], grad_ref[...])
    half = a.shape[0] // 2
    for rows, x in ((slice(0, half), a), (slice(half, 2 * half), b)):
        keep_ref[rows, :] = jnp.where(first, x[:half], x[half:])
        give_ref[rows, :] = jnp.where(first, x[half:], x[:half])


def first_parts(core, acts, grad, in_up, columns):
    shape = jax.ShapeDtypeStruct((in_up.shape[0], acts.shape[0]), F32)
    whole = pl.BlockSpec(memory_space=pltpu.VMEM)
    return pl.pallas_call(
        first_kernel,
        in_specs=[pl.BlockSpec(memory_space=pltpu.SMEM)] + [whole] * 4,
        out_specs=(whole, whole),
        out_shape=(shape, shape),
        cost_estimate=SMALL,
        compiler_params=pltpu.CompilerParams(vmem_limit_bytes=VMEM_LIMIT),
    )(core, acts, grad, in_up, columns)


def pack_kernel(mine_ref, other_ref, part_ref):
    rows, tokens = mine_ref.shape
    depth = part_ref.shape[1]
    for c in range(tokens // depth):
        cols = slice(c * depth, (c + 1) * depth)
        part_ref[c * rows : (c + 1) * rows, :] = (mine_ref[:, cols] + other_ref[:, cols]).astype(BF16)


def packed(mine, other, depth):
    return pl.pallas_call(
        pack_kernel,
        out_shape=jax.ShapeDtypeStruct((mine.size // depth, depth), BF16),
        cost_estimate=SMALL,
        compiler_params=pltpu.CompilerParams(vmem_limit_bytes=VMEM_LIMIT),
    )(mine, other)


def pair_kernel(core_ref, weight_ref, mine_ref, other_ref, a_ref, high_ref, low_ref, out_ref):
    first, mine, other = core_ref[0] == 0, mine_ref[...], other_ref[...]
    low_half, high_half = jnp.where(first, mine, other), jnp.where(first, other, mine)
    half = mine.shape[0] // 2
    a_up = jnp.concatenate([low_half[:half], high_half[:half]], axis=0)
    b_down = jnp.concatenate([low_half[half:], high_half[half:]], axis=0)
    weight = weight_ref[...]
    high_ref[...], low_ref[...] = weighted(weight, a_up)
    b_high = b_down.astype(BF16)
    b_low = (b_down - b_high.astype(F32)).astype(BF16)
    high, low = weighted(weight, a_ref[...])
    sums = dot_t(high, b_high) + (dot_t(high, b_low) + dot_t(low, b_high))
    out_ref[...] = spread(sums, weight.shape[0])


def pair_parts(core, weight, mine, other, a_down):
    pairs, tokens = weight.shape
    kis, kos = a_down.shape[0], mine.shape[0]
    shape = pltpu.VMEM((pairs * kis, tokens), BF16)
    whole = pl.BlockSpec(memory_space=pltpu.VMEM)
    return pl.pallas_call(
        pair_kernel,
        in_specs=[pl.BlockSpec(memory_space=pltpu.SMEM)] + [whole] * 4,
        out_specs=(whole, whole, whole),
        out_shape=(shape, shape, jax.ShapeDtypeStruct((pairs, kis * kos), F32)),
        cost_estimate=SMALL,
        compiler_params=pltpu.CompilerParams(vmem_limit_bytes=VMEM_LIMIT),
    )(core, weight, mine, other, a_down)


def gathered_kernel(*refs):
    total = refs[0][...].astype(F32)
    for ref in refs[1:-1]:
        total = total + ref[...].astype(F32)
    (kis, tokens), depth = refs[-1].shape, total.shape[1]
    for c in range(tokens // depth):
        refs[-1][:, c * depth : (c + 1) * depth] = total[c * kis : (c + 1) * kis]


def gathered_sum(parts, kis, tokens):
    return pl.pallas_call(
        gathered_kernel,
        out_shape=jax.ShapeDtypeStruct((kis, tokens), F32),
        cost_estimate=SMALL,
        compiler_params=pltpu.CompilerParams(vmem_limit_bytes=VMEM_LIMIT),
    )(*parts)


def swap(value, bit, devices):
    return lax.ppermute(value, "tensor", [(i, i ^ bit) for i in range(devices)])


def per_device(
    devices,
    activations,
    gate_pre,
    up_pre,
    out_grad,
    down_weight,
    in_proj_down,
    out_proj_down,
    in_proj_up,
    out_proj_up,
    segments,
    labels,
    queries,
):
    tokens, depth = out_grad.shape
    me = lax.axis_index("tensor")
    chips = devices // 2
    ring = ring_of(chips)
    far = chips // 2
    place = {chip: i for i, chip in enumerate(ring)}

    table = np.zeros((devices, devices), np.int32)
    for device in range(devices):
        chip, core = divmod(device, 2)
        order = [chip]
        for step in range(1, far):
            order += [ring[(place[chip] - step) % chips], ring[(place[chip] + step) % chips]]
        order.append(ring[(place[chip] + far) % chips])
        table[device] = [2 * c + k for c in order for k in (core, 1 - core)]
    src = lax.dynamic_index_in_dim(jnp.asarray(table), me, 0, keepdims=False)

    ahead = [
        (2 * ring[i] + core, 2 * ring[(i + 1) % chips] + core) for i in range(chips) for core in (0, 1)
    ]
    back = [(b, a) for a, b in ahead]

    pin = lax.optimization_barrier
    kis, kos = in_proj_up.shape[0], out_proj_up.shape[0]
    seq_count = labels.shape[0]
    pairs, half = seq_count // 2, tokens // 2

    core = (me % 2)[None]

    core = (me % 2)[None]

    def send(forward, backward):
        return lax.ppermute(forward, "tensor", ahead), lax.ppermute(backward, "tensor", back)

    f, b = send(out_grad, out_grad)
    other = swap(out_grad, 1, devices)
    own_columns = lax.dynamic_slice_in_dim(out_proj_down, me * depth, depth, axis=1)
    keep, give = first_parts(core, activations, out_grad, in_proj_up, own_columns)
    part = packed(keep, swap(give, 1, devices), depth)
    gate_pre, up_pre, part = pin((gate_pre, up_pre, part))
    silu_gate, a_down = own_parts(gate_pre, up_pre, in_proj_down)
    part, a_down = pin((part, a_down))
    part_f, part_b = send(part, part)
    seqs = jnp.arange(seq_count, dtype=jnp.int32)[:, None]
    signs = (2 * labels - 1).astype(F32)
    per_seq = jnp.where(segments[None, :] == seqs, signs[:, None], F32(0.0))
    pair_weight = per_seq.reshape(pairs, 2, tokens).sum(axis=1)

    def halves(array, place):
        return [(array, 0, place), (array, 1, place)]

    f, b, part_f, part_b, other, a_down, pair_weight = pin(
        (f, b, part_f, part_b, other, a_down, pair_weight)
    )
    known, parts, came = None, [part, part_f, part_b], (f, b)
    units = [halves(out_grad, 0), halves(other, 1)]
    for step in range(1, far):
        if step < far - 1:
            f, b = send(f, b)
            part_f, part_b = send(part_f, part_b)
            parts += [part_f, part_b]
            if step == 1:
                part_far = lax.ppermute(
                    part,
                    "tensor",
                    [
                        (2 * ring[i] + k, 2 * ring[(i + far) % chips] + k)
                        for i in range(chips)
                        for k in (0, 1)
                    ],
                )
                parts.append(part_far)
        else:
            f, b = send(f[:half], b[half:])
        place = 4 * step - 2
        for i, array in enumerate(came):
            units += [
                halves(array, place + 2 * i),
                halves(swap(array, 1, devices), place + 2 * i + 1),
            ]
        if step == far - 2:
            columns, q_turned = last_columns(src, down_weight, depth), turned(queries, kos)
            src, columns, q_turned = pin((src, columns, q_turned))
        if step == far - 1:
            mine = gathered_sum(parts, kis, tokens)
            high, low, down = pair_parts(core, pair_weight, mine, swap(mine, 1, devices), a_down)
            src, high, low, down = pin((src, high, low, down))
            b_up = b_step(src, half, units, down_weight, known, silu_gate, out_proj_up)
        else:
            known = add_step(src, half, units, down_weight, known)
            units = []
            f, b, part_f, part_b, parts, known = pin((f, b, part_f, part_b, parts, known))
            came = (f, b)
    f, b, b_up, high, low, down = pin((f, b, b_up, high, low, down))
    blocks = [x for block in (f, b) for x in (block, swap(block, 1, devices))]
    up = last_step(blocks, columns, silu_gate, out_proj_up, b_up, (high, low), pairs)

    first = core == 0
    total = jnp.where(first, down, up) + swap(jnp.where(first, up, down), 1, devices)
    for bit in range(1, devices.bit_length() - 1):
        total = total + swap(total.astype(BF16), 1 << bit, devices).astype(F32)
    theirs = swap(total, 1, devices)
    return score(jnp.where(first, total, theirs), jnp.where(first, theirs, total), q_turned)


def solution(mesh):
    in_specs = (
        P("groups", "tensor"),
        P("groups", "tensor"),
        P("groups", "tensor"),
        P("groups", "tensor"),
        P("tensor", None),
        P(None, "tensor"),
        P(),
        P(None, "tensor"),
        P(None, "tensor"),
        P("groups"),
        P("groups"),
        P("tensor", None),
    )
    return jax.shard_map(
        functools.partial(per_device, mesh.shape["tensor"]),
        mesh=mesh,
        in_specs=in_specs,
        out_specs=P("groups", "tensor"),
        check_vma=False,
    )
```

time: 289 us -> 150 us (0.52)
  waiting for transfers between devices: 206 us -> 34 us
  Pallas kernels: 0 us -> 78.6 us
  matrix products: 67.3 us -> 0 us
  starting transfers between devices: 0.04 us -> 25 us
  between operations: 13.5 us -> 0.34 us
  local copies, waits for them, and re-layouts: 0.58 us -> 10.3 us
    all_gather x1 -> x0, waiting for transfers between devices: 125 us -> none  [per_device(): piece = lax.all_gather(out_grad, 'tensor', axis=1, tiled=True)]
    psum x1 -> x0, waiting for transfers between devices: 79.8 us -> none  [per_device(): a_down, a_up, b_up = lax.psum((part_adown, part_aup, part_bup), 'tensor')]
    pallas_call x0 -> x12, Pallas kernels: none -> 78.6 us  [the longest x2 34.3 us: add_step(): pl.pallas_call(functools.partial(step_kernel, which), grid_spec=pltpu.Pre...]
    dot_general x8 -> x0, matrix products: 67.3 us -> none  [the longest x6 61.8 us: project(): lax.dot_general(data, proj, (((1,), (1,)), ((), ())), preferred_element_t...]
    ppermute x0 -> x31, waiting for transfers between devices: none -> 34 us  [the longest x16 20.3 us: swap(): return lax.ppermute(value, 'tensor', [(i, i ^ bit) for i in range(devices)])]
    ppermute x0 -> x31, starting transfers between devices: none -> 25 us  [the longest x7 13.8 us: send(): lax.ppermute(forward, 'tensor', ahead)]
    unnamed x8 -> x48, local copies, waits for them, and re-layouts: 0.02 us -> 9.34 us
  transfers between devices with their start and end apart: 2 -> 31, of which waited for: 2 -> 15; matrix products, arithmetic and copies ran while one was open for 7% -> 1% of each run, Pallas kernels for 0% -> 47%
where the time goes in v2:
time: 150 us; the launch traced here: 149 us
  Pallas kernels  78.6 us (52%)
  waiting for transfers between devices  34 us (23%)
  starting transfers between devices  25 us (17%)
  local copies, waits for them, and re-layouts  10.3 us (7%)
    pallas_call x2, Pallas kernels, add_step(): pl.pallas_call(functools.partial(step_kernel, which), grid_spec=pltpu.Pre...  34.3 us
    ppermute x16, waiting for transfers between devices, swap(): return lax.ppermute(value, 'tensor', [(i, i ^ bit) for i in range(devices)])  20.3 us
    pallas_call x1, Pallas kernels, b_step(): pl.pallas_call(functools.partial(b_step_kernel, which), grid_spec=pltpu.P...  15.9 us
    ppermute x7, starting transfers between devices, send(): lax.ppermute(forward, 'tensor', ahead)  13.8 us
    pallas_call x1, Pallas kernels, own_parts(): pl.pallas_call(own_kernel, grid=(units // tile,), in_specs=[tiles, tiles,...  10.8 us
    unnamed x48, local copies, waits for them, and re-layouts  9.34 us
    pallas_call x1, Pallas kernels, last_step(): pl.pallas_call(last_kernel, in_specs=[pl.BlockSpec(memory_space=pl.ANY)]...  7.29 us
    ppermute x7, waiting for transfers between devices, send(): lax.ppermute(forward, 'tensor', ahead)  6.51 us
  transfers between devices with their start and end apart: 31, of which 15 were waited for; matrix products, arithmetic and copies ran while one was open for 1% of the time, Pallas kernels for 47%

profile of v2, /device:TPU:0, one launch (start us, length us, event | category | flops | bytes accessed | tf_op | source)
XLA Modules:
  0.0 149.0 jit_solution(1455211582275056703)
XLA Ops:
  0.0 3.0 %collective-permute-start = (bf16[1024,512]{1,0:T(8,128)(2,1)}, bf16[1024,512]{1,0:T(8,128)(2,1)S(1)}, u32[]{:S(2)}, u32[]{:S(2)}) collective-permute-start(bf16[1024,512]{1,0:T(8,128)(2,1)} %refs_6_.2), channel_id=1, source_target_pairs={{0,4},{1,5},{4,8},{5,9},{8,12},{9,13},{12,14},{13,15},{14,10},{15,... | collective-permute-start | bytes 3145736 | tf_op jit(solution)/shard_map/ppermute | solution.py:437
  3.1 1.2 copy-done.2
  4.3 1.2 copy-done.3
  5.6 0.8 copy-done.6
  6.4 0.7 shard_map.127
  7.1 0.5 collective-permute-start.2
  7.7 0.7 add_convert_fusion
  8.3 0.5 collective-permute-done.2.other_ref
  8.9 0.9 copy-done.5
  9.8 10.8 %shard_map.129 = (f32[1024,1792]{1,0:T(8,128)}, f32[64,1024]{1,0:T(8,128)S(1)}) custom-call(bf16[1024,1792]{1,0:T(8,128)(2,1)} %gate_ref, bf16[1024,1792]{1,0:T(8,128)(2,1)} %up_ref, bf16[64,1792]{1,0:T(8,128)(2,1)S(1)} %copy-done.5), custom_call_target="tpu_custom_call" | custom-call | flops 1000 | bytes 1000 | tf_op jit(solution)/shard_map/pallas_call | solution.py:240
  20.6 2.0 %collective-permute-start.3 = (bf16[128,512]{1,0:T(8,128)(2,1)S(1)}, bf16[128,512]{1,0:T(8,128)(2,1)S(1)}, u32[]{:S(2)}, u32[]{:S(2)}) collective-permute-start(bf16[128,512]{1,0:T(8,128)(2,1)S(1)} %shard_map.128.refs_0_), channel_id=1, source_target_pairs={{0,4},{1,5},{4,8},{5,9},{8,12},{9,13},{12,14},{13,15},{14,10},{15,... | collective-permute-start | bytes 393224 | tf_op jit(solution)/shard_map/ppermute | solution.py:437
  22.7 0.1 broadcast_in_dim.39
  22.8 0.1 copy.15
  22.9 0.1 select_reduce_fusion.weight_ref
  22.9 6.2 %collective-permute-done.3.refs_1_ = bf16[128,512]{1,0:T(8,128)(2,1)S(1)} collective-permute-done((bf16[128,512]{1,0:T(8,128)(2,1)S(1)}, bf16[128,512]{1,0:T(8,128)(2,1)S(1)}, u32[]{:S(2)}, u32[]{:S(2)}) %collective-permute-start.3) | collective-permute-done | bytes 131104 | tf_op jit(solution)/shard_map/ppermute | solution.py:437
  29.1 1.5 %collective-permute-done.4.refs_2_ = bf16[128,512]{1,0:T(8,128)(2,1)S(1)} collective-permute-done((bf16[128,512]{1,0:T(8,128)(2,1)S(1)}, bf16[128,512]{1,0:T(8,128)(2,1)S(1)}, u32[]{:S(2)}, u32[]{:S(2)}) %collective-permute-start.4) | collective-permute-done | bytes 131104 | tf_op jit(solution)/shard_map/ppermute | solution.py:437
  30.7 0.1 collective-permute-start.11
  30.8 0.5 collective-permute-start.12
  31.3 1.6 %collective-permute-start.6 = (bf16[1024,512]{1,0:T(8,128)(2,1)S(1)}, bf16[1024,512]{1,0:T(8,128)(2,1)}, u32[]{:S(2)}, u32[]{:S(2)}) collective-permute-start(bf16[1024,512]{1,0:T(8,128)(2,1)S(1)} %collective-permute-done.refs_2_.refs_8_), channel_id=1, source_target_pairs={{0,4},{1,5},{4,8},{5,9},{8,12},{9,13},{12,14},{13,15},{14,10},{15,... | collective-permute-start | bytes 3145736 | tf_op jit(solution)/shard_map/ppermute | solution.py:437
  32.9 0.4 collective-permute-start.7
  33.3 3.4 %collective-permute-start.10 = (bf16[128,512]{1,0:T(8,128)(2,1)S(1)}, bf16[128,512]{1,0:T(8,128)(2,1)S(1)}, u32[]{:S(2)}, u32[]{:S(2)}) collective-permute-start(bf16[128,512]{1,0:T(8,128)(2,1)S(1)} %shard_map.128.refs_0_), channel_id=1, source_target_pairs={{0,14},{1,15},{4,10},{5,11},{8,6},{9,7},{12,2},{13,3},{14,0},{15,1... | collective-permute-start | bytes 393224 | tf_op jit(solution)/shard_map/ppermute | solution.py:467
  36.8 0.9 copy-done.13
  37.7 1.0 copy-done.14
  38.7 1.6 %collective-permute-start.9 = (bf16[128,512]{1,0:T(8,128)(2,1)S(1)}, bf16[128,512]{1,0:T(8,128)(2,1)S(1)}, u32[]{:S(2)}, u32[]{:S(2)}) collective-permute-start(bf16[128,512]{1,0:T(8,128)(2,1)S(1)} %collective-permute-done.4.refs_2_), channel_id=1, source_target_pairs={{4,0},{5,1},{8,4},{9,5},{12,8},{13,9},{14,12},{15,13},{10,14},{11,... | collective-permute-start | bytes 393224 | tf_op jit(solution)/shard_map/ppermute | solution.py:437
  40.3 0.7 dynamic-slice_bitcast_fusion.src_ref
  41.0 18.5 %shard_map.130.refs_12_ = f32[1024,1792]{1,0:T(8,128)} custom-call(s32[16]{0:T(128)S(1)} %dynamic-slice_bitcast_fusion.src_ref, bf16[1024,512]{1,0:T(8,128)(2,1)} %refs_6_.2, bf16[1024,512]{1,0:T(8,128)(2,1)} %collective-permute-done.5.refs_1_.refs_7_, bf16[1024,512]{1,0:T(8,128)(2,1)} %copy-done.9, bf16[1024,512]{1,0:T(8,128)(2,1)} %copy-done.13, ...), custom_call_target="tpu_custom_call" | custom-call | flops 1000 | bytes 1000 | tf_op jit(solution)/shard_map/pallas_call | solution.py:108
  59.5 2.5 %collective-permute-done.10.refs_5_ = bf16[128,512]{1,0:T(8,128)(2,1)S(1)} collective-permute-done((bf16[128,512]{1,0:T(8,128)(2,1)S(1)}, bf16[128,512]{1,0:T(8,128)(2,1)S(1)}, u32[]{:S(2)}, u32[]{:S(2)}) %collective-permute-start.10) | collective-permute-done | bytes 131104 | tf_op jit(solution)/shard_map/ppermute | solution.py:467
  62.0 0.9 collective-permute-done.9.refs_4_
  63.0 0.5 collective-permute-start.18
  63.5 4.7 %collective-permute-start.13 = (bf16[1024,512]{1,0:T(8,128)(2,1)}, bf16[1024,512]{1,0:T(8,128)(2,1)S(1)}, u32[]{:S(2)}, u32[]{:S(2)}) collective-permute-start(bf16[1024,512]{1,0:T(8,128)(2,1)} %collective-permute-done.6.refs_0_.refs_4_), channel_id=1, source_target_pairs={{0,4},{1,5},{4,8},{5,9},{8,12},{9,13},{12,14},{13,15},{14,10},{15,... | collective-permute-start | bytes 3145736 | tf_op jit(solution)/shard_map/ppermute | solution.py:437
  68.2 2.0 %collective-permute-start.15 = (bf16[128,512]{1,0:T(8,128)(2,1)S(1)}, bf16[128,512]{1,0:T(8,128)(2,1)S(1)}, u32[]{:S(2)}, u32[]{:S(2)}) collective-permute-start(bf16[128,512]{1,0:T(8,128)(2,1)S(1)} %collective-permute-done.8.refs_3_), channel_id=1, source_target_pairs={{0,4},{1,5},{4,8},{5,9},{8,12},{9,13},{12,14},{13,15},{14,10},{15,... | collective-permute-start | bytes 393224 | tf_op jit(solution)/shard_map/ppermute | solution.py:437
  70.3 2.6 %shard_map.131.refs_4_ = bf16[2,1792,512]{2,1,0:T(8,128)(2,1)S(1)} custom-call(s32[16]{0:T(128)S(1)} %dynamic-slice_bitcast_fusion.src_ref, bf16[1792,8192]{1,0:T(8,128)(2,1)} %refs_11_.3), custom_call_target="tpu_custom_call" | custom-call | flops 1000 | bytes 1000 | tf_op jit(solution)/shard_map/pallas_call | solution.py:154
  72.9 3.9 %shard_map.132.q_ref = bf16[8192,64]{1,0:T(8,128)(2,1)S(1)} custom-call(bf16[64,8192]{1,0:T(8,128)(2,1)} %q_ref.1), custom_call_target="tpu_custom_call" | custom-call | flops 1000 | bytes 1000 | tf_op jit(solution)/shard_map/pallas_call | solution.py:261
  76.8 1.0 copy-done.16
  77.8 15.8 %shard_map.133.refs_12_ = f32[1024,1792]{1,0:T(8,128)} custom-call(s32[16]{0:T(128)S(1)} %dynamic-slice_bitcast_fusion.src_ref, bf16[1024,512]{1,0:T(8,128)(2,1)} %collective-permute-done.6.refs_0_.refs_4_, bf16[1024,512]{1,0:T(8,128)(2,1)} %copy-done.15, bf16[1024,512]{1,0:T(8,128)(2,1)} %collective-permute-done.7.refs_2_.refs_6_, ...), custom_call_target="tpu_custom_call", output_to_operand_aliasing={{}: (13, {})} | custom-call | flops 1000 | bytes 1000 | tf_op jit(solution)/shard_map/pallas_call | solution.py:108
  93.7 0.3 collective-permute-done.15.refs_6_
  93.9 2.2 %collective-permute-done.16.refs_7_ = bf16[128,512]{1,0:T(8,128)(2,1)S(1)} collective-permute-done((bf16[128,512]{1,0:T(8,128)(2,1)S(1)}, bf16[128,512]{1,0:T(8,128)(2,1)S(1)}, u32[]{:S(2)}, u32[]{:S(2)}) %collective-permute-start.16) | collective-permute-done | bytes 131104 | tf_op jit(solution)/shard_map/ppermute | solution.py:437
  96.1 0.1 collective-permute-start.22
  96.2 0.5 collective-permute-start.23
  96.8 0.4 collective-permute-start.19
  97.2 1.7 %collective-permute-start.20 = (bf16[512,512]{1,0:T(8,128)(2,1)S(1)}, bf16[512,512]{1,0:T(8,128)(2,1)S(1)}, u32[]{:S(2)}, u32[]{:S(2)}) collective-permute-start(bf16[512,512]{1,0:T(8,128)(2,1)S(1)} %slice.7), channel_id=1, source_target_pairs={{4,0},{5,1},{8,4},{9,5},{12,8},{13,9},{14,12},{15,13},{10,14},{11,... | collective-permute-start | bytes 1572872 | tf_op jit(solution)/shard_map/ppermute | solution.py:437
  98.9 0.1 shard_map.134.mine_ref
  99.0 0.1 collective-permute-start.21
  99.1 1.6 %collective-permute-done.21.other_ref = f32[64,1024]{1,0:T(8,128)S(1)} collective-permute-done((f32[64,1024]{1,0:T(8,128)S(1)}, f32[64,1024]{1,0:T(8,128)S(1)}, u32[]{:S(2)}, u32[]{:S(2)}) %collective-permute-start.21) | collective-permute-done | bytes 262176 | tf_op jit(solution)/shard_map/ppermute | solution.py:387
  100.7 1.8 %shard_map.135 = (bf16[512,1024]{1,0:T(8,128)(2,1)S(1)}, bf16[512,1024]{1,0:T(8,128)(2,1)S(1)}, f32[8,4096]{1,0:T(8,128)S(1)}) custom-call(s32[1]{0:T(128)} %bitcast.core_ref, f32[8,1024]{1,0:T(8,128)S(1)} %select_reduce_fusion.weight_ref, f32[64,1024]{1,0:T(8,128)S(1)} %shard_map.134.mine_ref, f32[64,1024]{1,0:T(8,128)S(1)} %collective-permute-done.21.other_ref, ...), custom_call_target="tpu_custom_call" | custom-call | flops 1000 | bytes 1000 | tf_op jit(solution)/shard_map/pallas_call | solution.py:358
  102.6 1.0 copy-done.11
  103.5 0.3 copy-done.12
  103.8 15.9 %shard_map.136.refs_7_ = f32[1024,64]{1,0:T(8,128)S(1)} custom-call(s32[16]{0:T(128)S(1)} %dynamic-slice_bitcast_fusion.src_ref, bf16[1024,512]{1,0:T(8,128)(2,1)} %copy-done.7, bf16[1024,512]{1,0:T(8,128)(2,1)} %copy-done.11, bf16[1024,512]{1,0:T(8,128)(2,1)} %copy-done.8, bf16[1024,512]{1,0:T(8,128)(2,1)} %copy-done.12, bf16[1024,512]{1,0:T(8,128)(2,1)} %copy-done.7, ...), custom_call_target="tpu_custom_call" | custom-call | flops 1000 | bytes 1000 | tf_op jit(solution)/shard_map/pallas_call | solution.py:124
  119.8 0.2 collective-permute-start.24
  120.0 0.4 collective-permute-start.25
  120.4 1.4 collective-permute-done.24.refs_1_
  121.8 0.7 collective-permute-done.25.refs_3_
  122.6 0.8 copy-done.20
  123.4 7.3 %shard_map.137 = f32[8,4096]{1,0:T(8,128)S(1)} custom-call(bf16[512,512]{1,0:T(8,128)(2,1)} %copy-done.17, bf16[512,512]{1,0:T(8,128)(2,1)} %copy-done.19, bf16[512,512]{1,0:T(8,128)(2,1)} %copy-done.18, bf16[512,512]{1,0:T(8,128)(2,1)} %copy-done.20, bf16[2,1792,512]{2,1,0:T(8,128)(2,1)S(1)} %shard_map.131.refs_4_, f32[1024,1792]{1,0:T(8,128)S(1)} %bitcast.5, ...), custom_call_target="tpu_custom_call" | custom-call | flops 1000 | bytes 1000 | tf_op jit(solution)/shard_map/pallas_call | solution.py:205
  130.7 0.2 collective-permute-start.26
  130.9 1.2 collective-permute-done.26
  132.1 0.3 collective-permute-start.27
  132.5 4.0 %collective-permute-done.27 = bf16[8,4096]{1,0:T(8,128)(2,1)S(1)} collective-permute-done((bf16[8,4096]{1,0:T(8,128)(2,1)S(1)}, bf16[8,4096]{1,0:T(8,128)(2,1)S(1)}, u32[]{:S(2)}, u32[]{:S(2)}) %collective-permute-start.27) | collective-permute-done | bytes 65568 | tf_op jit(solution)/shard_map/ppermute | solution.py:387
  136.5 0.4 collective-permute-start.28
  136.9 3.9 %collective-permute-done.28 = bf16[8,4096]{1,0:T(8,128)(2,1)S(1)} collective-permute-done((bf16[8,4096]{1,0:T(8,128)(2,1)S(1)}, bf16[8,4096]{1,0:T(8,128)(2,1)S(1)}, u32[]{:S(2)}, u32[]{:S(2)}) %collective-permute-start.28) | collective-permute-done | bytes 65568 | tf_op jit(solution)/shard_map/ppermute | solution.py:387
  140.9 0.1 collective-permute-start.29
  141.0 5.6 %collective-permute-done.29 = bf16[8,4096]{1,0:T(8,128)(2,1)S(1)} collective-permute-done((bf16[8,4096]{1,0:T(8,128)(2,1)S(1)}, bf16[8,4096]{1,0:T(8,128)(2,1)S(1)}, u32[]{:S(2)}, u32[]{:S(2)}) %collective-permute-start.29) | collective-permute-done | bytes 65568 | tf_op jit(solution)/shard_map/ppermute | solution.py:387
  146.7 1.3 collective-permute-done.30
  148.1 1.0 shard_map.138
  (74 shorter events, 0.5 us)
Async XLA Ops:
  0.0 3.0 %copy-start = (bf16[64,8192]{1,0:T(8,128)(2,1)S(1)}, bf16[64,8192]{1,0:T(8,128)(2,1)}, u32[]{:S(2)}) copy-start(bf16[64,8192]{1,0:T(8,128)(2,1)} %param.19) | copy-start | bytes 3145732
  0.0 22.9 %copy-start.21 = (s32[1024]{0:T(1024)S(1)}, s32[1024]{0:T(1024)}, u32[]{:S(2)}) copy-start(s32[1024]{0:T(1024)} %param.22) | copy-start | bytes 12292
  0.0 30.7 %collective-permute-start = (bf16[1024,512]{1,0:T(8,128)(2,1)}, bf16[1024,512]{1,0:T(8,128)(2,1)S(1)}, u32[]{:S(2)}, u32[]{:S(2)}) collective-permute-start(bf16[1024,512]{1,0:T(8,128)(2,1)} %refs_6_.2), channel_id=1, source_target_pairs={{0,4},{1,5},{4,8},{5,9},{8,12},{9,13},{12,14},{13,15},{14,10},{15,... | collective-permute-start | bytes 3145736 | tf_op jit(solution)/shard_map/ppermute | solution.py:437
  3.0 27.6 %collective-permute-start.1 = (bf16[1024,512]{1,0:T(8,128)(2,1)}, bf16[1024,512]{1,0:T(8,128)(2,1)S(1)}, u32[]{:S(2)}, u32[]{:S(2)}) collective-permute-start(bf16[1024,512]{1,0:T(8,128)(2,1)} %refs_6_.2), channel_id=1, source_target_pairs={{4,0},{5,1},{8,4},{9,5},{12,8},{13,9},{14,12},{15,13},{10,14},{11,... | collective-permute-start | bytes 3145736 | tf_op jit(solution)/shard_map/ppermute | solution.py:437
  3.0 27.7 %collective-permute-start.5 = (bf16[1024,512]{1,0:T(8,128)(2,1)}, bf16[1024,512]{1,0:T(8,128)(2,1)}, u32[]{:S(2)}, u32[]{:S(2)}) collective-permute-start(bf16[1024,512]{1,0:T(8,128)(2,1)} %refs_6_.2), channel_id=1, source_target_pairs={{0,1},{1,0},{2,3},{3,2},{4,5},{5,4},{6,7},{7,6},{8,9},{9,8},{10,11... | collective-permute-start | bytes 3145736 | tf_op jit(solution)/shard_map/ppermute | solution.py:387
  3.1 1.3 copy-start.2
  4.3 1.2 copy-start.3
  5.5 0.8 copy-start.6
  7.1 1.7 %collective-permute-start.2 = (f32[64,1024]{1,0:T(8,128)S(1)}, f32[64,1024]{1,0:T(8,128)S(1)}, u32[]{:S(2)}, u32[]{:S(2)}) collective-permute-start(f32[64,1024]{1,0:T(8,128)S(1)} %get-tuple-element.60), channel_id=1, source_target_pairs={{0,1},{1,0},{2,3},{3,2},{4,5},{5,4},{6,7},{7,6},{8,9},{9,8},{10,11... | collective-permute-start | bytes 786440 | tf_op jit(solution)/shard_map/ppermute | solution.py:387
  8.9 0.9 copy-start.5
  20.6 8.5 %collective-permute-start.3 = (bf16[128,512]{1,0:T(8,128)(2,1)S(1)}, bf16[128,512]{1,0:T(8,128)(2,1)S(1)}, u32[]{:S(2)}, u32[]{:S(2)}) collective-permute-start(bf16[128,512]{1,0:T(8,128)(2,1)S(1)} %shard_map.128.refs_0_), channel_id=1, source_target_pairs={{0,4},{1,5},{4,8},{5,9},{8,12},{9,13},{12,14},{13,15},{14,10},{15,... | collective-permute-start | bytes 393224 | tf_op jit(solution)/shard_map/ppermute | solution.py:437
  22.7 8.0 %collective-permute-start.4 = (bf16[128,512]{1,0:T(8,128)(2,1)S(1)}, bf16[128,512]{1,0:T(8,128)(2,1)S(1)}, u32[]{:S(2)}, u32[]{:S(2)}) collective-permute-start(bf16[128,512]{1,0:T(8,128)(2,1)S(1)} %shard_map.128.refs_0_), channel_id=1, source_target_pairs={{4,0},{5,1},{8,4},{9,5},{12,8},{13,9},{14,12},{15,13},{10,14},{11,... | collective-permute-start | bytes 393224 | tf_op jit(solution)/shard_map/ppermute | solution.py:437
  30.7 10.3 %copy-start.9 = (bf16[1024,512]{1,0:T(8,128)(2,1)}, bf16[1024,512]{1,0:T(8,128)(2,1)S(1)}, u32[]{:S(2)}) copy-start(bf16[1024,512]{1,0:T(8,128)(2,1)S(1)} %collective-permute-done.refs_2_.refs_8_) | copy-start | bytes 3145732
  30.7 10.3 %copy-start.10 = (bf16[1024,512]{1,0:T(8,128)(2,1)}, bf16[1024,512]{1,0:T(8,128)(2,1)S(1)}, u32[]{:S(2)}) copy-start(bf16[1024,512]{1,0:T(8,128)(2,1)S(1)} %collective-permute-done.1.refs_4_.refs_10_) | copy-start | bytes 3145732
  30.7 6.0 %collective-permute-start.11 = (bf16[1024,512]{1,0:T(8,128)(2,1)S(1)}, bf16[1024,512]{1,0:T(8,128)(2,1)S(1)}, u32[]{:S(2)}, u32[]{:S(2)}) collective-permute-start(bf16[1024,512]{1,0:T(8,128)(2,1)S(1)} %collective-permute-done.refs_2_.refs_8_), channel_id=1, source_target_pairs={{0,1},{1,0},{2,3},{3,2},{4,5},{5,4},{6,7},{7,6},{8,9},{9,8},{10,11... | collective-permute-start | bytes 3145736 | tf_op jit(solution)/shard_map/ppermute | solution.py:387
  30.8 6.0 %collective-permute-start.12 = (bf16[1024,512]{1,0:T(8,128)(2,1)S(1)}, bf16[1024,512]{1,0:T(8,128)(2,1)S(1)}, u32[]{:S(2)}, u32[]{:S(2)}) collective-permute-start(bf16[1024,512]{1,0:T(8,128)(2,1)S(1)} %collective-permute-done.1.refs_4_.refs_10_), channel_id=1, source_target_pairs={{0,1},{1,0},{2,3},{3,2},{4,5},{5,4},{6,7},{7,6},{8,9},{9,8},{10,11... | collective-permute-start | bytes 3145736 | tf_op jit(solution)/shard_map/ppermute | solution.py:387
  31.3 31.7 %collective-permute-start.6 = (bf16[1024,512]{1,0:T(8,128)(2,1)S(1)}, bf16[1024,512]{1,0:T(8,128)(2,1)}, u32[]{:S(2)}, u32[]{:S(2)}) collective-permute-start(bf16[1024,512]{1,0:T(8,128)(2,1)S(1)} %collective-permute-done.refs_2_.refs_8_), channel_id=1, source_target_pairs={{0,4},{1,5},{4,8},{5,9},{8,12},{9,13},{12,14},{13,15},{14,10},{15,... | collective-permute-start | bytes 3145736 | tf_op jit(solution)/shard_map/ppermute | solution.py:437
  32.9 30.1 %collective-permute-start.7 = (bf16[1024,512]{1,0:T(8,128)(2,1)S(1)}, bf16[1024,512]{1,0:T(8,128)(2,1)}, u32[]{:S(2)}, u32[]{:S(2)}) collective-permute-start(bf16[1024,512]{1,0:T(8,128)(2,1)S(1)} %collective-permute-done.1.refs_4_.refs_10_), channel_id=1, source_target_pairs={{4,0},{5,1},{8,4},{9,5},{12,8},{13,9},{14,12},{15,13},{10,14},{11,... | collective-permute-start | bytes 3145736 | tf_op jit(solution)/shard_map/ppermute | solution.py:437
  33.3 28.7 %collective-permute-start.10 = (bf16[128,512]{1,0:T(8,128)(2,1)S(1)}, bf16[128,512]{1,0:T(8,128)(2,1)S(1)}, u32[]{:S(2)}, u32[]{:S(2)}) collective-permute-start(bf16[128,512]{1,0:T(8,128)(2,1)S(1)} %shard_map.128.refs_0_), channel_id=1, source_target_pairs={{0,14},{1,15},{4,10},{5,11},{8,6},{9,7},{12,2},{13,3},{14,0},{15,1... | collective-permute-start | bytes 393224 | tf_op jit(solution)/shard_map/ppermute | solution.py:467
  36.7 1.0 copy-start.13
  36.7 25.3 %collective-permute-start.8 = (bf16[128,512]{1,0:T(8,128)(2,1)S(1)}, bf16[128,512]{1,0:T(8,128)(2,1)S(1)}, u32[]{:S(2)}, u32[]{:S(2)}) collective-permute-start(bf16[128,512]{1,0:T(8,128)(2,1)S(1)} %collective-permute-done.3.refs_1_), channel_id=1, source_target_pairs={{0,4},{1,5},{4,8},{5,9},{8,12},{9,13},{12,14},{13,15},{14,10},{15,... | collective-permute-start | bytes 393224 | tf_op jit(solution)/shard_map/ppermute | solution.py:437
  37.7 1.0 copy-start.14
  38.7 24.3 %collective-permute-start.9 = (bf16[128,512]{1,0:T(8,128)(2,1)S(1)}, bf16[128,512]{1,0:T(8,128)(2,1)S(1)}, u32[]{:S(2)}, u32[]{:S(2)}) collective-permute-start(bf16[128,512]{1,0:T(8,128)(2,1)S(1)} %collective-permute-done.4.refs_2_), channel_id=1, source_target_pairs={{4,0},{5,1},{8,4},{9,5},{12,8},{13,9},{14,12},{15,13},{10,14},{11,... | collective-permute-start | bytes 393224 | tf_op jit(solution)/shard_map/ppermute | solution.py:437
  63.0 7.3 %collective-permute-start.17 = (bf16[1024,512]{1,0:T(8,128)(2,1)}, bf16[1024,512]{1,0:T(8,128)(2,1)S(1)}, u32[]{:S(2)}, u32[]{:S(2)}) collective-permute-start(bf16[1024,512]{1,0:T(8,128)(2,1)} %collective-permute-done.6.refs_0_.refs_4_), channel_id=1, source_target_pairs={{0,1},{1,0},{2,3},{3,2},{4,5},{5,4},{6,7},{7,6},{8,9},{9,8},{10,11... | collective-permute-start | bytes 3145736 | tf_op jit(solution)/shard_map/ppermute | solution.py:387
  63.0 13.8 %collective-permute-start.18 = (bf16[1024,512]{1,0:T(8,128)(2,1)}, bf16[1024,512]{1,0:T(8,128)(2,1)S(1)}, u32[]{:S(2)}, u32[]{:S(2)}) collective-permute-start(bf16[1024,512]{1,0:T(8,128)(2,1)} %collective-permute-done.7.refs_2_.refs_6_), channel_id=1, source_target_pairs={{0,1},{1,0},{2,3},{3,2},{4,5},{5,4},{6,7},{7,6},{8,9},{9,8},{10,11... | collective-permute-start | bytes 3145736 | tf_op jit(solution)/shard_map/ppermute | solution.py:387
  63.5 32.6 %collective-permute-start.13 = (bf16[1024,512]{1,0:T(8,128)(2,1)}, bf16[1024,512]{1,0:T(8,128)(2,1)S(1)}, u32[]{:S(2)}, u32[]{:S(2)}) collective-permute-start(bf16[1024,512]{1,0:T(8,128)(2,1)} %collective-permute-done.6.refs_0_.refs_4_), channel_id=1, source_target_pairs={{0,4},{1,5},{4,8},{5,9},{8,12},{9,13},{12,14},{13,15},{14,10},{15,... | collective-permute-start | bytes 3145736 | tf_op jit(solution)/shard_map/ppermute | solution.py:437
  68.2 27.9 %collective-permute-start.14 = (bf16[1024,512]{1,0:T(8,128)(2,1)}, bf16[1024,512]{1,0:T(8,128)(2,1)S(1)}, u32[]{:S(2)}, u32[]{:S(2)}) collective-permute-start(bf16[1024,512]{1,0:T(8,128)(2,1)} %collective-permute-done.7.refs_2_.refs_6_), channel_id=1, source_target_pairs={{4,0},{5,1},{8,4},{9,5},{12,8},{13,9},{14,12},{15,13},{10,14},{11,... | collective-permute-start | bytes 3145736 | tf_op jit(solution)/shard_map/ppermute | solution.py:437
  68.2 25.7 %collective-permute-start.15 = (bf16[128,512]{1,0:T(8,128)(2,1)S(1)}, bf16[128,512]{1,0:T(8,128)(2,1)S(1)}, u32[]{:S(2)}, u32[]{:S(2)}) collective-permute-start(bf16[128,512]{1,0:T(8,128)(2,1)S(1)} %collective-permute-done.8.refs_3_), channel_id=1, source_target_pairs={{0,4},{1,5},{4,8},{5,9},{8,12},{9,13},{12,14},{13,15},{14,10},{15,... | collective-permute-start | bytes 393224 | tf_op jit(solution)/shard_map/ppermute | solution.py:437
  70.3 2.6 %copy-start.15 = (bf16[1024,512]{1,0:T(8,128)(2,1)}, bf16[1024,512]{1,0:T(8,128)(2,1)S(1)}, u32[]{:S(2)}) copy-start(bf16[1024,512]{1,0:T(8,128)(2,1)S(1)} %collective-permute-done.17.refs_1_.refs_5_) | copy-start | bytes 3145732
  70.3 25.8 %collective-permute-start.16 = (bf16[128,512]{1,0:T(8,128)(2,1)S(1)}, bf16[128,512]{1,0:T(8,128)(2,1)S(1)}, u32[]{:S(2)}, u32[]{:S(2)}) collective-permute-start(bf16[128,512]{1,0:T(8,128)(2,1)S(1)} %collective-permute-done.9.refs_4_), channel_id=1, source_target_pairs={{4,0},{5,1},{8,4},{9,5},{12,8},{13,9},{14,12},{15,13},{10,14},{11,... | collective-permute-start | bytes 393224 | tf_op jit(solution)/shard_map/ppermute | solution.py:437
  76.8 27.0 %copy-start.4 = (bf16[64,1792]{1,0:T(8,128)(2,1)S(1)}, bf16[64,1792]{1,0:T(8,128)(2,1)}, u32[]{:S(2)}) copy-start(bf16[64,1792]{1,0:T(8,128)(2,1)} %refs_6_.3) | copy-start | bytes 688132
  76.8 1.0 copy-start.16
  77.8 45.6 %slice-start = ((s8[7340032]{0:T(1024)(128)(4,1)}), s8[4194304]{0:T(1024)(128)(4,1)S(1)}, s32[]{:S(2)}) async-start(s8[7340032]{0:T(1024)(128)(4,1)} %bitcast.4), calls=%async_computation | async-start | bytes 8388608
  96.1 6.4 %copy-start.7 = (bf16[1024,512]{1,0:T(8,128)(2,1)}, bf16[1024,512]{1,0:T(8,128)(2,1)S(1)}, u32[]{:S(2)}) copy-start(bf16[1024,512]{1,0:T(8,128)(2,1)S(1)} %collective-permute-done.13.refs_0_.refs_4_) | copy-start | bytes 3145732
  96.1 6.4 %copy-start.8 = (bf16[1024,512]{1,0:T(8,128)(2,1)}, bf16[1024,512]{1,0:T(8,128)(2,1)S(1)}, u32[]{:S(2)}) copy-start(bf16[1024,512]{1,0:T(8,128)(2,1)S(1)} %collective-permute-done.14.refs_2_.refs_6_) | copy-start | bytes 3145732
  96.1 6.4 %collective-permute-start.22 = (bf16[1024,512]{1,0:T(8,128)(2,1)S(1)}, bf16[1024,512]{1,0:T(8,128)(2,1)S(1)}, u32[]{:S(2)}, u32[]{:S(2)}) collective-permute-start(bf16[1024,512]{1,0:T(8,128)(2,1)S(1)} %collective-permute-done.13.refs_0_.refs_4_), channel_id=1, source_target_pairs={{0,1},{1,0},{2,3},{3,2},{4,5},{5,4},{6,7},{7,6},{8,9},{9,8},{10,11... | collective-permute-start | bytes 3145736 | tf_op jit(solution)/shard_map/ppermute | solution.py:387
  96.2 6.3 %collective-permute-start.23 = (bf16[1024,512]{1,0:T(8,128)(2,1)S(1)}, bf16[1024,512]{1,0:T(8,128)(2,1)S(1)}, u32[]{:S(2)}, u32[]{:S(2)}) collective-permute-start(bf16[1024,512]{1,0:T(8,128)(2,1)S(1)} %collective-permute-done.14.refs_2_.refs_6_), channel_id=1, source_target_pairs={{0,1},{1,0},{2,3},{3,2},{4,5},{5,4},{6,7},{7,6},{8,9},{9,8},{10,11... | collective-permute-start | bytes 3145736 | tf_op jit(solution)/shard_map/ppermute | solution.py:387
  96.8 26.6 %slice-start.1 = ((s8[7340032]{0:T(1024)(128)(4,1)}), s8[3145728]{0:T(1024)(128)(4,1)S(1)}, s32[]{:S(2)}) async-start(s8[7340032]{0:T(1024)(128)(4,1)} %bitcast.4), calls=%async_computation.1 | async-start | bytes 6291456
  96.8 23.0 %collective-permute-start.19 = (bf16[512,512]{1,0:T(8,128)(2,1)S(1)}, bf16[512,512]{1,0:T(8,128)(2,1)S(1)}, u32[]{:S(2)}, u32[]{:S(2)}) collective-permute-start(bf16[512,512]{1,0:T(8,128)(2,1)S(1)} %slice.6), channel_id=1, source_target_pairs={{0,4},{1,5},{4,8},{5,9},{8,12},{9,13},{12,14},{13,15},{14,10},{15,... | collective-permute-start | bytes 1572872 | tf_op jit(solution)/shard_map/ppermute | solution.py:437
  97.2 22.6 %collective-permute-start.20 = (bf16[512,512]{1,0:T(8,128)(2,1)S(1)}, bf16[512,512]{1,0:T(8,128)(2,1)S(1)}, u32[]{:S(2)}, u32[]{:S(2)}) collective-permute-start(bf16[512,512]{1,0:T(8,128)(2,1)S(1)} %slice.7), channel_id=1, source_target_pairs={{4,0},{5,1},{8,4},{9,5},{12,8},{13,9},{14,12},{15,13},{10,14},{11,... | collective-permute-start | bytes 1572872 | tf_op jit(solution)/shard_map/ppermute | solution.py:437
  99.0 1.7 %collective-permute-start.21 = (f32[64,1024]{1,0:T(8,128)S(1)}, f32[64,1024]{1,0:T(8,128)S(1)}, u32[]{:S(2)}, u32[]{:S(2)}) collective-permute-start(f32[64,1024]{1,0:T(8,128)S(1)} %shard_map.134.mine_ref), channel_id=1, source_target_pairs={{0,1},{1,0},{2,3},{3,2},{4,5},{5,4},{6,7},{7,6},{8,9},{9,8},{10,11... | collective-permute-start | bytes 786440 | tf_op jit(solution)/shard_map/ppermute | solution.py:387
  102.5 1.0 copy-start.11
  102.5 1.3 copy-start.12
  119.8 2.8 %copy-start.17 = (bf16[512,512]{1,0:T(8,128)(2,1)}, bf16[512,512]{1,0:T(8,128)(2,1)S(1)}, u32[]{:S(2)}) copy-start(bf16[512,512]{1,0:T(8,128)(2,1)S(1)} %collective-permute-done.19.refs_0_) | copy-start | bytes 1572868
  119.8 2.7 %copy-start.18 = (bf16[512,512]{1,0:T(8,128)(2,1)}, bf16[512,512]{1,0:T(8,128)(2,1)S(1)}, u32[]{:S(2)}) copy-start(bf16[512,512]{1,0:T(8,128)(2,1)S(1)} %collective-permute-done.20.refs_2_) | copy-start | bytes 1572868
  119.8 2.0 %collective-permute-start.24 = (bf16[512,512]{1,0:T(8,128)(2,1)S(1)}, bf16[512,512]{1,0:T(8,128)(2,1)S(1)}, u32[]{:S(2)}, u32[]{:S(2)}) collective-permute-start(bf16[512,512]{1,0:T(8,128)(2,1)S(1)} %collective-permute-done.19.refs_0_), channel_id=1, source_target_pairs={{0,1},{1,0},{2,3},{3,2},{4,5},{5,4},{6,7},{7,6},{8,9},{9,8},{10,11... | collective-permute-start | bytes 1572872 | tf_op jit(solution)/shard_map/ppermute | solution.py:387
  120.0 2.5 %collective-permute-start.25 = (bf16[512,512]{1,0:T(8,128)(2,1)S(1)}, bf16[512,512]{1,0:T(8,128)(2,1)S(1)}, u32[]{:S(2)}, u32[]{:S(2)}) collective-permute-start(bf16[512,512]{1,0:T(8,128)(2,1)S(1)} %collective-permute-done.20.refs_2_), channel_id=1, source_target_pairs={{0,1},{1,0},{2,3},{3,2},{4,5},{5,4},{6,7},{7,6},{8,9},{9,8},{10,11... | collective-permute-start | bytes 1572872 | tf_op jit(solution)/shard_map/ppermute | solution.py:387
  120.4 28.7 %copy-start.1 = (bf16[64,8192]{1,0:T(8,128)(2,1)S(1)}, bf16[64,8192]{1,0:T(8,128)(2,1)}, u32[]{:S(2)}) copy-start(bf16[64,8192]{1,0:T(8,128)(2,1)} %param.19) | copy-start | bytes 3145732
  121.8 0.8 copy-start.19
  122.6 0.8 copy-start.20
  130.7 1.4 collective-permute-start.26
  132.1 4.3 %collective-permute-start.27 = (bf16[8,4096]{1,0:T(8,128)(2,1)S(1)}, bf16[8,4096]{1,0:T(8,128)(2,1)S(1)}, u32[]{:S(2)}, u32[]{:S(2)}) collective-permute-start(bf16[8,4096]{1,0:T(8,128)(2,1)S(1)} %get-tuple-element.113), channel_id=1, source_target_pairs={{0,2},{1,3},{2,0},{3,1},{4,6},{5,7},{6,4},{7,5},{8,10},{9,11},{10,... | collective-permute-start | bytes 196616 | tf_op jit(solution)/shard_map/ppermute | solution.py:387
  136.5 4.3 %collective-permute-start.28 = (bf16[8,4096]{1,0:T(8,128)(2,1)S(1)}, bf16[8,4096]{1,0:T(8,128)(2,1)S(1)}, u32[]{:S(2)}, u32[]{:S(2)}) collective-permute-start(bf16[8,4096]{1,0:T(8,128)(2,1)S(1)} %fusion), channel_id=1, source_target_pairs={{0,4},{1,5},{2,6},{3,7},{4,0},{5,1},{6,2},{7,3},{8,12},{9,13},{10,... | collective-permute-start | bytes 196616 | tf_op jit(solution)/shard_map/ppermute | solution.py:387
  140.9 5.7 %collective-permute-start.29 = (bf16[8,4096]{1,0:T(8,128)(2,1)S(1)}, bf16[8,4096]{1,0:T(8,128)(2,1)S(1)}, u32[]{:S(2)}, u32[]{:S(2)}) collective-permute-start(bf16[8,4096]{1,0:T(8,128)(2,1)S(1)} %fusion.1), channel_id=1, source_target_pairs={{0,8},{1,9},{2,10},{3,11},{4,12},{5,13},{6,14},{7,15},{8,0},{9,1},... | collective-permute-start | bytes 196616 | tf_op jit(solution)/shard_map/ppermute | solution.py:387
  146.6 1.4 collective-permute-start.30

commit v3 on v2

v3 whole, which is shorter than its diff:
```python
import functools

import jax
import jax.numpy as jnp
import numpy as np
from jax import lax
from jax.experimental import pallas as pl
from jax.experimental.pallas import tpu as pltpu
from jax.sharding import PartitionSpec as P

F32, BF16 = jnp.float32, jnp.bfloat16
VMEM_LIMIT = 24 * 1024 * 1024
SMALL = pl.CostEstimate(flops=1000, bytes_accessed=1000, transcendentals=0)


def dot_t(left, right, precision=None):
    return lax.dot_general(
        left, right, (((1,), (1,)), ((), ())), preferred_element_type=F32, precision=precision
    )


def ring_of(chips):
    if chips == 8:
        return [0, 2, 4, 6, 7, 5, 3, 1]
    return list(range(chips))


def tile_of(units):
    return 256 if units % 256 == 0 else units


def products(lefts, weights):
    total = None
    for i, weight in enumerate(weights):
        part = dot_t(lefts[i], weight[...])
        total = part if total is None else total + part
    return total


def load(blocks, lefts, sems):
    half = lefts.shape[1] // 2
    copies = []
    for i, (array, row) in enumerate(blocks):
        rows = pl.ds((i % 2) * half, half)
        source = array.at[pl.ds(row * half, half)]
        copies.append(pltpu.make_async_copy(source, lefts.at[i // 2, rows], sems.at[i]))
    for copy in copies:
        copy.start()
    for copy in copies:
        copy.wait()


def step_kernel(count, src_ref, *refs):
    blocks, weights = refs[:count], refs[count : 2 * count]
    out_ref, lefts, sems = refs[-3:]
    before_ref = refs[2 * count] if len(refs) == 2 * count + 4 else None
    step = pl.program_id(0)

    @pl.when(step == 0)
    def _():
        load([(block, i) for block in blocks for i in range(2)], lefts, sems)

    total = products(lefts, weights)
    out_ref[step] = total if before_ref is None else total + before_ref[step]


def projected(ups, proj_ref):
    total, tile = None, ups.shape[2]
    for i in range(ups.shape[0]):
        part = dot_t(ups[i], proj_ref[:, i * tile : (i + 1) * tile])
        total = part if total is None else total + part
    return total


def in_hbm(x):
    return pltpu.with_memory_space_constraint(x, pltpu.HBM)


def in_vmem(x):
    return pltpu.with_memory_space_constraint(x, pltpu.VMEM)


ANYWHERE = pl.BlockSpec(memory_space=pl.ANY)
WHOLE = pl.BlockSpec(memory_space=pltpu.VMEM)


def step_parts(units, weight):
    tokens, depth = units[0][0].shape
    tile = tile_of(weight.shape[0])
    ins = [in_hbm(array) for array, _ in units] + [in_hbm(weight)] * len(units)
    specs = [ANYWHERE] * len(units)
    specs += [pl.BlockSpec((tile, depth), lambda i, s, m=m: (i, s[m])) for _, m in units]
    scratch = [
        pltpu.VMEM((len(units), tokens, depth), BF16),
        pltpu.SemaphoreType.DMA((2 * len(units),)),
    ]
    return ins, specs, scratch, tile


def add_step(src, units, weight, before):
    ins, specs, scratch, tile = step_parts(units, weight)
    tokens, hidden = units[0][0].shape[0], weight.shape[0]
    aliases = {}
    if before is not None:
        ins.append(in_vmem(before))
        specs.append(WHOLE)
        aliases = {len(ins): 0}
    return pl.pallas_call(
        functools.partial(step_kernel, len(units)),
        grid_spec=pltpu.PrefetchScalarGridSpec(
            num_scalar_prefetch=1,
            grid=(hidden // tile,),
            in_specs=specs,
            out_specs=WHOLE,
            scratch_shapes=scratch,
        ),
        out_shape=pltpu.VMEM((hidden // tile, tokens, tile), F32),
        input_output_aliases=aliases,
        cost_estimate=SMALL,
        compiler_params=pltpu.CompilerParams(vmem_limit_bytes=VMEM_LIMIT),
    )(src, *ins)


def columns_kernel(first, src_ref, weight_ref, out_ref, sems):
    depth = out_ref.shape[2]
    copies = []
    for m in range(2):
        start = pl.multiple_of(src_ref[first + m] * depth, depth)
        copies.append(
            pltpu.make_async_copy(weight_ref.at[:, pl.ds(start, depth)], out_ref.at[m], sems.at[m])
        )
    for copy in copies:
        copy.start()
    for copy in copies:
        copy.wait()


def last_columns(src, weight, depth):
    return pl.pallas_call(
        functools.partial(columns_kernel, src.shape[0] - 2),
        grid_spec=pltpu.PrefetchScalarGridSpec(
            num_scalar_prefetch=1,
            grid=(),
            in_specs=[pl.BlockSpec(memory_space=pl.ANY)],
            out_specs=pl.BlockSpec(memory_space=pltpu.VMEM),
            scratch_shapes=[pltpu.SemaphoreType.DMA((2,))],
        ),
        out_shape=pltpu.VMEM((2, weight.shape[0], depth), BF16),
        cost_estimate=SMALL,
        compiler_params=pltpu.CompilerParams(vmem_limit_bytes=VMEM_LIMIT),
    )(src, in_hbm(weight))


def last_kernel(*refs):
    blocks = refs[:4]
    weight_ref, silu_ref, proj_ref, before_ref, high_ref, low_ref, out_ref, lefts, ups, sems = refs[4:]
    half, tile = lefts.shape[1] // 2, ups.shape[2]
    load([(block, 0) for block in (blocks[0], blocks[2], blocks[1], blocks[3])], lefts, sems)
    for i in range(ups.shape[0]):
        cols = slice(i * tile, (i + 1) * tile)
        for h in range(2):
            rows = slice(h * half, (h + 1) * half)
            grad = dot_t(lefts[0, rows, :], weight_ref[0, cols, :]) + dot_t(
                lefts[1, rows, :], weight_ref[1, cols, :]
            )
            grad = grad + before_ref[i, rows, :]
            ups[i, rows, :] = (grad * silu_ref[i, rows, :]).astype(BF16)
    b_high, b_low = parts_of(projected(ups, proj_ref))
    kos = b_high.shape[1]
    sums = jnp.dot(
        high_ref[...], jnp.concatenate([b_high, b_low], axis=1), preferred_element_type=F32
    )
    rest = jnp.dot(low_ref[...], b_high, preferred_element_type=F32)
    out_ref[...] = spread(sums[:, :kos] + (sums[:, kos:] + rest), out_ref.shape[0])


def last_step(blocks, columns, silu, proj_up, before, up, pairs):
    half, depth = blocks[0].shape
    tiles, tokens, tile = silu.shape
    kos = proj_up.shape[0]
    ins = [in_vmem(x) for x in (columns, silu, proj_up, before, *up)]
    return pl.pallas_call(
        last_kernel,
        in_specs=[ANYWHERE] * 4 + [WHOLE] * len(ins),
        out_specs=WHOLE,
        out_shape=jax.ShapeDtypeStruct((pairs, up[0].shape[0] // pairs * kos), F32),
        scratch_shapes=[
            pltpu.VMEM((2, tokens, depth), BF16),
            pltpu.VMEM((tiles, tokens, tile), BF16),
            pltpu.SemaphoreType.DMA((4,)),
        ],
        cost_estimate=SMALL,
        compiler_params=pltpu.CompilerParams(vmem_limit_bytes=VMEM_LIMIT),
    )(*[in_hbm(x) for x in blocks], *ins)


def own_kernel(gate_ref, up_ref, down_ref, silu_ref, out_ref, hidden):
    step, tile = pl.program_id(0), gate_ref.shape[1]
    gate = gate_ref[...].astype(F32)
    silu = gate / (1.0 + jnp.exp(-gate))
    silu_ref[step] = silu
    hidden[step] = (silu * up_ref[...].astype(F32)).astype(BF16)

    @pl.when(step == hidden.shape[0] - 1)
    def _():
        total = None
        for i in range(hidden.shape[0]):
            part = dot_t(down_ref[:, i * tile : (i + 1) * tile], hidden[i])
            total = part if total is None else total + part
        out_ref[...] = total


def own_parts(gate, up, in_down):
    tokens, units = gate.shape
    tile, kis = tile_of(units), in_down.shape[0]
    tiles = pl.BlockSpec((tokens, tile), lambda i: (0, i))
    return pl.pallas_call(
        own_kernel,
        grid=(units // tile,),
        in_specs=[tiles, tiles, pl.BlockSpec((kis, units), lambda i: (0, 0))],
        out_specs=(WHOLE, pl.BlockSpec((kis, tokens), lambda i: (0, 0))),
        out_shape=(
            pltpu.VMEM((units // tile, tokens, tile), F32),
            jax.ShapeDtypeStruct((kis, tokens), F32),
        ),
        scratch_shapes=[pltpu.VMEM((units // tile, tokens, tile), BF16)],
        cost_estimate=SMALL,
        compiler_params=pltpu.CompilerParams(vmem_limit_bytes=VMEM_LIMIT),
    )(in_hbm(gate), in_hbm(up), in_down)


def turned(q, kos):
    asked, size = q.shape[0], q.shape[1] // 2
    kis = size // kos

    def kernel(q_ref, out_ref, rows):
        rows[...] = q_ref[...].astype(F32).T
        for j in range(kis):
            out_ref[j * kos : (j + 1) * kos, :] = rows[pl.ds(j, kos, stride=kis), :].astype(BF16)

    return pl.pallas_call(
        kernel,
        grid=(2,),
        in_specs=[pl.BlockSpec((asked, size), lambda i: (0, i))],
        out_specs=pl.BlockSpec((size, asked), lambda i: (i, 0)),
        out_shape=jax.ShapeDtypeStruct((2 * size, asked), BF16),
        scratch_shapes=[pltpu.VMEM((size, asked), F32)],
        cost_estimate=SMALL,
        compiler_params=pltpu.CompilerParams(vmem_limit_bytes=VMEM_LIMIT),
    )(in_hbm(q))


def score_kernel(down_ref, up_ref, q_ref, out_ref):
    pairs, size = down_ref.shape
    total = None
    for i, ref in enumerate((down_ref, up_ref)):
        both = jnp.concatenate(parts_of(ref[...]), axis=0)
        part = jnp.dot(both, q_ref[i * size : (i + 1) * size, :], preferred_element_type=F32)
        total = part if total is None else total + part
    out_ref[...] = total[:pairs] + total[pairs:]


def score(down, up, q):
    return pl.pallas_call(
        score_kernel,
        out_shape=jax.ShapeDtypeStruct((down.shape[0], q.shape[1]), F32),
        cost_estimate=SMALL,
        compiler_params=pltpu.CompilerParams(vmem_limit_bytes=VMEM_LIMIT),
    )(down, up, q)


def parts_of(x):
    high = x.astype(BF16)
    return high, (x - high.astype(F32)).astype(BF16)


def weighted(weight, a):
    return parts_of(jnp.concatenate([weight * a[j : j + 1, :] for j in range(a.shape[0])], axis=0))


def spread(sums, pairs):
    return jnp.concatenate([sums[r : r + pairs] for r in range(0, sums.shape[0], pairs)], axis=1)


def first_kernel(core_ref, acts_ref, grad_ref, in_up_ref, columns_ref, keep_ref, give_ref):
    first = core_ref[0] == 0
    a, b = dot_t(in_up_ref[...], acts_ref[...]), dot_t(columns_ref[...], grad_ref[...])
    half = a.shape[0] // 2
    for rows, x in ((slice(0, half), a), (slice(half, 2 * half), b)):
        keep_ref[rows, :] = jnp.where(first, x[:half], x[half:])
        give_ref[rows, :] = jnp.where(first, x[half:], x[:half])


def first_parts(core, acts, grad, in_up, columns):
    shape = jax.ShapeDtypeStruct((in_up.shape[0], acts.shape[0]), F32)
    whole = pl.BlockSpec(memory_space=pltpu.VMEM)
    return pl.pallas_call(
        first_kernel,
        in_specs=[pl.BlockSpec(memory_space=pltpu.SMEM)] + [whole] * 4,
        out_specs=(whole, whole),
        out_shape=(shape, shape),
        cost_estimate=SMALL,
        compiler_params=pltpu.CompilerParams(vmem_limit_bytes=VMEM_LIMIT),
    )(core, acts, grad, in_up, columns)


def pair_kernel(place_ref, weight_ref, mine_ref, across_ref, mine1_ref, across1_ref, a_ref, high_ref, low_ref, out_ref):
    first, near = place_ref[0] == 0, place_ref[1] == 0
    rows = []
    for mine, across in ((mine_ref, across_ref), (mine1_ref, across1_ref)):
        mine, across = mine[...], across[...]
        rows.append((jnp.where(near, mine, across), jnp.where(near, across, mine)))
    (a0, b0), (a1, b1) = rows
    a_up = jnp.concatenate([jnp.where(first, a0, a1), jnp.where(first, a1, a0)], axis=0)
    b_down = jnp.concatenate([jnp.where(first, b0, b1), jnp.where(first, b1, b0)], axis=0)
    weight = weight_ref[...]
    high_ref[...], low_ref[...] = weighted(weight, a_up)
    b_high, b_low = parts_of(b_down)
    high, low = weighted(weight, a_ref[...])
    sums = dot_t(high, b_high) + (dot_t(high, b_low) + dot_t(low, b_high))
    out_ref[...] = spread(sums, weight.shape[0])


def pair_parts(place, weight, quarters, a_down):
    pairs, tokens = weight.shape
    kis, kos = a_down.shape[0], 2 * quarters[0].shape[0]
    shape = pltpu.VMEM((pairs * kis, tokens), BF16)
    return pl.pallas_call(
        pair_kernel,
        in_specs=[pl.BlockSpec(memory_space=pltpu.SMEM)] + [WHOLE] * 6,
        out_specs=(WHOLE, WHOLE, WHOLE),
        out_shape=(shape, shape, jax.ShapeDtypeStruct((pairs, kis * kos), F32)),
        cost_estimate=SMALL,
        compiler_params=pltpu.CompilerParams(vmem_limit_bytes=VMEM_LIMIT),
    )(place, weight, *quarters, a_down)


def swap(value, bit, devices):
    return lax.ppermute(value, "tensor", [(i, i ^ bit) for i in range(devices)])


def per_device(
    devices,
    activations,
    gate_pre,
    up_pre,
    out_grad,
    down_weight,
    in_proj_down,
    out_proj_down,
    in_proj_up,
    out_proj_up,
    segments,
    labels,
    queries,
):
    tokens, depth = out_grad.shape
    me = lax.axis_index("tensor")
    chips = devices // 2
    ring = ring_of(chips)
    far = chips // 2
    place = {chip: i for i, chip in enumerate(ring)}

    table = np.zeros((devices, devices), np.int32)
    for device in range(devices):
        chip, core = divmod(device, 2)
        order = [chip]
        for step in range(1, far):
            order += [ring[(place[chip] - step) % chips], ring[(place[chip] + step) % chips]]
        order.append(ring[(place[chip] + far) % chips])
        table[device] = [2 * c + k for c in order for k in (core, 1 - core)]
    src = lax.dynamic_index_in_dim(jnp.asarray(table), me, 0, keepdims=False)

    ahead = [
        (2 * ring[i] + core, 2 * ring[(i + 1) % chips] + core) for i in range(chips) for core in (0, 1)
    ]
    back = [(b, a) for a, b in ahead]

    pin = lax.optimization_barrier
    kis, kos = in_proj_up.shape[0], out_proj_up.shape[0]
    seq_count = labels.shape[0]
    pairs, half = seq_count // 2, tokens // 2

    core = (me % 2)[None]

    def send(forward, backward):
        return lax.ppermute(forward, "tensor", ahead), lax.ppermute(backward, "tensor", back)

    f, b = send(out_grad, out_grad)
    other = swap(out_grad, 1, devices)
    own_columns = lax.dynamic_slice_in_dim(out_proj_down, me * depth, depth, axis=1)
    keep, give = first_parts(core, activations, out_grad, in_proj_up, own_columns)
    part = keep + swap(give, 1, devices)
    gate_pre, up_pre, part = pin((gate_pre, up_pre, part))
    silu_gate, a_down = own_parts(gate_pre, up_pre, in_proj_down)
    bits = [1 << i for i in range(2, devices.bit_length() - 1)]
    rounds = [[]] + [[int(bit) for bit in some] for some in np.array_split(bits, far - 2)]
    row = part.shape[0] // 2
    side = (me // 2) % 2
    give = lax.dynamic_slice_in_dim(part, (1 - side) * row, row, axis=0)
    part = lax.dynamic_slice_in_dim(part, side * row, row, axis=0)

    def ask(part, step):
        return [swap(part.astype(BF16), bit, devices) for bit in rounds[step]]

    def added(part, theirs):
        for more in theirs:
            part = part + more.astype(F32)
        return part

    theirs = [swap(give.astype(BF16), 2, devices)]
    seqs = jnp.arange(seq_count, dtype=jnp.int32)[:, None]
    signs = (2 * labels - 1).astype(F32)
    per_seq = jnp.where(segments[None, :] == seqs, signs[:, None], F32(0.0))
    pair_weight = per_seq.reshape(pairs, 2, tokens).sum(axis=1)

    f, b, theirs, other, a_down, pair_weight = pin((f, b, theirs, other, a_down, pair_weight))
    part = added(part, theirs)
    known, came = None, (f, b)
    units = [(out_grad, 0), (other, 1)]
    for step in range(1, far):
        if step < far - 1:
            f, b = send(f, b)
            theirs = ask(part, step)
        else:
            f, b = send(f[:half], b[half:])
        place = 4 * step - 2
        for i, array in enumerate(came):
            units += [(array, place + 2 * i), (swap(array, 1, devices), place + 2 * i + 1)]
        if step == far - 2:
            columns, q_turned = last_columns(src, down_weight, depth), turned(queries, kos)
            src, columns, q_turned = pin((src, columns, q_turned))
        if step == far - 1:
            known = add_step(src, units, down_weight, known)
            across = swap(part, 2, devices)
            known, part, across = pin((known, part, across))
            high, low, down = pair_parts(
                jnp.stack([me % 2, side]),
                pair_weight,
                (part, across, swap(part, 1, devices), swap(across, 1, devices)),
                a_down,
            )
        else:
            known = add_step(src, units, down_weight, known)
            units = []
            f, b, theirs, known = pin((f, b, theirs, known))
            part = added(part, theirs)
            came = (f, b)
    f, b, known = pin((f, b, known))
    blocks = [x for block in (f, b) for x in (block, swap(block, 1, devices))]
    up = last_step(blocks, columns, silu_gate, out_proj_up, known, (high, low), pairs)

    first = core == 0
    total = jnp.where(first, down, up) + swap(jnp.where(first, up, down), 1, devices)
    for bit in range(1, devices.bit_length() - 1):
        if bit < 3:
            total = total + swap(total, 1 << bit, devices)
        else:
            total = total + swap(total.astype(BF16), 1 << bit, devices).astype(F32)
    rest = swap(total, 1, devices)
    return score(jnp.where(first, total, rest), jnp.where(first, rest, total), q_turned)


def solution(mesh):
    in_specs = (
        P("groups", "tensor"),
        P("groups", "tensor"),
        P("groups", "tensor"),
        P("groups", "tensor"),
        P("tensor", None),
        P(None, "tensor"),
        P(),
        P(None, "tensor"),
        P(None, "tensor"),
        P("groups"),
        P("groups"),
        P("tensor", None),
    )
    return jax.shard_map(
        functools.partial(per_device, mesh.shape["tensor"]),
        mesh=mesh,
        in_specs=in_specs,
        out_specs=P("groups", "tensor"),
        check_vma=False,
    )
```

time: 150 us -> 143 us (0.953)
  Pallas kernels: 78.6 us -> 72.7 us
  starting transfers between devices: 25 us -> 22.6 us
  local copies, waits for them, and re-layouts: 10.3 us -> 11.9 us
    ppermute x16 -> x21, waiting for transfers between devices: 20.3 us -> 33.4 us  [swap(): return lax.ppermute(value, 'tensor', [(i, i ^ bit) for i in range(devices)])]
    ppermute x16 -> x21, starting transfers between devices: 3.99 us -> 13.4 us  [swap(): return lax.ppermute(value, 'tensor', [(i, i ^ bit) for i in range(devices)])]
    ppermute x7 -> x4, starting transfers between devices: 13.8 us -> 6.21 us  [send(): lax.ppermute(forward, 'tensor', ahead)]
    ppermute x7 -> x4, waiting for transfers between devices: 6.51 us -> 0.01 us  [send(): lax.ppermute(forward, 'tensor', ahead)]
    ppermute x7 -> x4, waiting for transfers between devices: 4.67 us -> 0.12 us  [send(): lax.ppermute(backward, 'tensor', back)]
    ppermute x1 -> x0, starting transfers between devices: 3.43 us -> none  [per_device(): lax.ppermute(part, 'tensor', [(2 * ring[i] + k, 2 * ring[(i + far) % chip...]
    pallas_call x1, Pallas kernels: 10.8 us -> 7.61 us  [own_parts(): pl.pallas_call(own_kernel, grid=(units // tile,), in_specs=[tiles, tiles,...]
    pallas_call x6 -> x4, Pallas kernels: 57.7 us -> 54.6 us  [the longest x3 46 us: add_step(): pl.pallas_call(functools.partial(step_kernel, len(units)), grid_spec=pltp...]
  transfers between devices with their start and end apart: 31 -> 29, of which waited for: 15 -> 13; matrix products, arithmetic and copies ran while one was open for 1% -> 2% of each run, Pallas kernels for 47% -> 44%
where the time goes in v3:
time: 143 us
  Pallas kernels  72.7 us (51%)
  waiting for transfers between devices  33.6 us (23%)
  starting transfers between devices  22.6 us (16%)
  local copies, waits for them, and re-layouts  11.9 us (8%)
  other arithmetic  1.72 us (1%)
    pallas_call x3, Pallas kernels, add_step(): pl.pallas_call(functools.partial(step_kernel, len(units)), grid_spec=pltp...  46 us
    ppermute x21, waiting for transfers between devices, swap(): return lax.ppermute(value, 'tensor', [(i, i ^ bit) for i in range(devices)])  33.4 us
    ppermute x21, starting transfers between devices, swap(): return lax.ppermute(value, 'tensor', [(i, i ^ bit) for i in range(devices)])  13.4 us
    unnamed x44, local copies, waits for them, and re-layouts  10.9 us
    pallas_call x1, Pallas kernels, last_step(): pl.pallas_call(last_kernel, in_specs=[ANYWHERE] * 4 + [WHOLE] * len(ins),...  8.58 us
    pallas_call x1, Pallas kernels, own_parts(): pl.pallas_call(own_kernel, grid=(units // tile,), in_specs=[tiles, tiles,...  7.61 us
    ppermute x4, starting transfers between devices, send(): lax.ppermute(forward, 'tensor', ahead)  6.21 us
    pallas_call x1, Pallas kernels, turned(): pl.pallas_call(kernel, grid=(2,), in_specs=[pl.BlockSpec((asked, size), l...  3.88 us
  transfers between devices with their start and end apart: 29, of which 13 were waited for; matrix products, arithmetic and copies ran while one was open for 2% of the time, Pallas kernels for 44%

profile of v3, /device:TPU:0, one launch (start us, length us, event | category | flops | bytes accessed | tf_op | source)
XLA Modules:
  0.0 142.9 jit_solution(15625334028031604543)
XLA Ops:
  0.0 3.0 %collective-permute-start = (bf16[1024,512]{1,0:T(8,128)(2,1)}, bf16[1024,512]{1,0:T(8,128)(2,1)S(1)}, u32[]{:S(2)}, u32[]{:S(2)}) collective-permute-start(bf16[1024,512]{1,0:T(8,128)(2,1)} %refs_0_.1), channel_id=1, source_target_pairs={{0,4},{1,5},{4,8},{5,9},{8,12},{9,13},{12,14},{13,15},{14,10},{15,... | collective-permute-start | bytes 3145736 | tf_op jit(solution)/shard_map/ppermute | solution.py:387
  3.1 1.3 copy-done.3
  4.3 1.2 copy-done.4
  5.5 0.8 copy-done.7
  6.4 0.7 shard_map.127
  7.1 0.5 collective-permute-start.2
  7.7 0.7 add_convert_fusion
  8.3 0.1 broadcast_in_dim.39
  8.4 0.1 copy.16
  8.5 0.3 collective-permute-done.2
  8.9 2.0 %collective-permute-start.3 = (bf16[32,1024]{1,0:T(8,128)(2,1)S(1)}, bf16[32,1024]{1,0:T(8,128)(2,1)S(1)}, u32[]{:S(2)}, u32[]{:S(2)}) collective-permute-start(bf16[32,1024]{1,0:T(8,128)(2,1)S(1)} %dynamic-slice_convert_fusion), channel_id=1, source_target_pairs={{0,2},{1,3},{2,0},{3,1},{4,6},{5,7},{6,4},{7,5},{8,10},{9,11},{10,... | collective-permute-start | bytes 196616 | tf_op jit(solution)/shard_map/ppermute | solution.py:339
  10.9 0.8 select_reduce_fusion.weight_ref
  11.7 0.9 copy-done.6
  12.6 7.6 %shard_map.128 = (f32[7,1024,256]{2,1,0:T(8,128)S(1)}, f32[64,1024]{1,0:T(8,128)S(1)}) custom-call(bf16[1024,1792]{1,0:T(8,128)(2,1)} %gate_ref, bf16[1024,1792]{1,0:T(8,128)(2,1)} %up_ref, bf16[64,1792]{1,0:T(8,128)(2,1)S(1)} %copy-done.6), custom_call_target="tpu_custom_call" | custom-call | flops 1000 | bytes 1000 | tf_op jit(solution)/shard_map/pallas_call | solution.py:217
  20.3 2.9 %copy-done.2 = f32[7,1024,256]{2,1,0:T(8,128)} copy-done((f32[7,1024,256]{2,1,0:T(8,128)}, f32[7,1024,256]{2,1,0:T(8,128)S(1)}, u32[]{:S(2)}) %copy-start.2) | copy-done | bytes 7340056
  23.1 4.6 %collective-permute-done.3 = bf16[32,1024]{1,0:T(8,128)(2,1)S(1)} collective-permute-done((bf16[32,1024]{1,0:T(8,128)(2,1)S(1)}, bf16[32,1024]{1,0:T(8,128)(2,1)S(1)}, u32[]{:S(2)}, u32[]{:S(2)}) %collective-permute-start.3) | collective-permute-done | bytes 65568 | tf_op jit(solution)/shard_map/ppermute | solution.py:339
  27.7 0.1 collective-permute-done.1.refs_4_
  27.9 0.5 collective-permute-start.9
  28.4 1.6 %collective-permute-start.5 = (bf16[1024,512]{1,0:T(8,128)(2,1)S(1)}, bf16[1024,512]{1,0:T(8,128)(2,1)}, u32[]{:S(2)}, u32[]{:S(2)}) collective-permute-start(bf16[1024,512]{1,0:T(8,128)(2,1)S(1)} %collective-permute-done.refs_2_), channel_id=1, source_target_pairs={{0,4},{1,5},{4,8},{5,9},{8,12},{9,13},{12,14},{13,15},{14,10},{15,... | collective-permute-start | bytes 3145736 | tf_op jit(solution)/shard_map/ppermute | solution.py:387
  30.0 0.4 collective-permute-start.6
  30.4 1.6 %collective-permute-start.7 = (bf16[32,1024]{1,0:T(8,128)(2,1)S(1)}, bf16[32,1024]{1,0:T(8,128)(2,1)S(1)}, u32[]{:S(2)}, u32[]{:S(2)}) collective-permute-start(bf16[32,1024]{1,0:T(8,128)(2,1)S(1)} %fusion.1), channel_id=1, source_target_pairs={{0,4},{1,5},{2,6},{3,7},{4,0},{5,1},{6,2},{7,3},{8,12},{9,13},{10,... | collective-permute-start | bytes 196616 | tf_op jit(solution)/shard_map/ppermute | solution.py:339
  32.1 0.7 fusion.2.src_ref
  32.8 18.3 %shard_map.131.refs_8_ = f32[7,1024,256]{2,1,0:T(8,128)S(1)} custom-call(s32[16]{0:T(128)S(1)} %fusion.2.src_ref, bf16[1024,512]{1,0:T(8,128)(2,1)} %refs_0_.1, bf16[1024,512]{1,0:T(8,128)(2,1)} %collective-permute-done.4.refs_1_, bf16[1024,512]{1,0:T(8,128)(2,1)} %copy-done.10, bf16[1024,512]{1,0:T(8,128)(2,1)} %collective-permute-done.8.refs_3_, ...), custom_call_target="tpu_custom_call" | custom-call | flops 1000 | bytes 1000 | tf_op jit(solution)/shard_map/pallas_call | solution.py:108
  51.1 5.1 %collective-permute-done.7 = bf16[32,1024]{1,0:T(8,128)(2,1)S(1)} collective-permute-done((bf16[32,1024]{1,0:T(8,128)(2,1)S(1)}, bf16[32,1024]{1,0:T(8,128)(2,1)S(1)}, u32[]{:S(2)}, u32[]{:S(2)}) %collective-permute-start.7) | collective-permute-done | bytes 65568 | tf_op jit(solution)/shard_map/ppermute | solution.py:339
  56.2 0.5 collective-permute-start.14
  56.7 1.6 %collective-permute-start.10 = (bf16[1024,512]{1,0:T(8,128)(2,1)}, bf16[1024,512]{1,0:T(8,128)(2,1)S(1)}, u32[]{:S(2)}, u32[]{:S(2)}) collective-permute-start(bf16[1024,512]{1,0:T(8,128)(2,1)} %collective-permute-done.5.refs_0_), channel_id=1, source_target_pairs={{0,4},{1,5},{4,8},{5,9},{8,12},{9,13},{12,14},{13,15},{14,10},{15,... | collective-permute-start | bytes 3145736 | tf_op jit(solution)/shard_map/ppermute | solution.py:387
  58.3 0.5 collective-permute-start.11
  58.8 4.1 %collective-permute-start.12 = (bf16[32,1024]{1,0:T(8,128)(2,1)S(1)}, bf16[32,1024]{1,0:T(8,128)(2,1)S(1)}, u32[]{:S(2)}, u32[]{:S(2)}) collective-permute-start(bf16[32,1024]{1,0:T(8,128)(2,1)S(1)} %fusion), channel_id=1, source_target_pairs={{0,8},{1,9},{2,10},{3,11},{4,12},{5,13},{6,14},{7,15},{8,0},{9,1},... | collective-permute-start | bytes 196616 | tf_op jit(solution)/shard_map/ppermute | solution.py:339
  62.9 2.6 %shard_map.129.refs_4_ = bf16[2,1792,512]{2,1,0:T(8,128)(2,1)S(1)} custom-call(s32[16]{0:T(128)S(1)} %fusion.2.src_ref, bf16[1792,8192]{1,0:T(8,128)(2,1)} %refs_7_.5), custom_call_target="tpu_custom_call" | custom-call | flops 1000 | bytes 1000 | tf_op jit(solution)/shard_map/pallas_call | solution.py:139
  65.5 3.9 %shard_map.130.q_ref = bf16[8192,64]{1,0:T(8,128)(2,1)S(1)} custom-call(bf16[64,8192]{1,0:T(8,128)(2,1)} %q_ref.1), custom_call_target="tpu_custom_call" | custom-call | flops 1000 | bytes 1000 | tf_op jit(solution)/shard_map/pallas_call | solution.py:241
  69.4 0.9 copy-done.14
  70.4 1.0 copy-done.15
  71.3 13.9 %shard_map.132.refs_8_ = f32[7,1024,256]{2,1,0:T(8,128)S(1)} custom-call(s32[16]{0:T(128)S(1)} %fusion.2.src_ref, bf16[1024,512]{1,0:T(8,128)(2,1)} %collective-permute-done.5.refs_0_, bf16[1024,512]{1,0:T(8,128)(2,1)} %copy-done.14, bf16[1024,512]{1,0:T(8,128)(2,1)} %collective-permute-done.6.refs_2_, ...), custom_call_target="tpu_custom_call", output_to_operand_aliasing={{}: (9, {})} | custom-call | flops 1000 | bytes 1000 | tf_op jit(solution)/shard_map/pallas_call | solution.py:108
  85.2 3.4 %collective-permute-done.12 = bf16[32,1024]{1,0:T(8,128)(2,1)S(1)} collective-permute-done((bf16[32,1024]{1,0:T(8,128)(2,1)S(1)}, bf16[32,1024]{1,0:T(8,128)(2,1)S(1)}, u32[]{:S(2)}, u32[]{:S(2)}) %collective-permute-start.12) | collective-permute-done | bytes 65568 | tf_op jit(solution)/shard_map/ppermute | solution.py:339
  88.7 0.1 collective-permute-start.15
  88.7 0.5 collective-permute-start.16
  89.3 0.1 collective-permute-start.20
  89.4 2.0 %collective-permute-start.21 = (bf16[512,512]{1,0:T(8,128)(2,1)S(1)}, bf16[512,512]{1,0:T(8,128)(2,1)S(1)}, u32[]{:S(2)}, u32[]{:S(2)}) collective-permute-start(bf16[512,512]{1,0:T(8,128)(2,1)S(1)} %slice.7), channel_id=1, source_target_pairs={{4,0},{5,1},{8,4},{9,5},{12,8},{13,9},{14,12},{15,13},{10,14},{11,... | collective-permute-start | bytes 1572872 | tf_op jit(solution)/shard_map/ppermute | solution.py:387
  91.5 0.1 collective-permute-start.17
  91.6 1.3 collective-permute-done.16.refs_3_
  92.9 0.9 copy-done.13
  93.9 13.9 %shard_map.133.refs_7_ = f32[7,1024,256]{2,1,0:T(8,128)S(1)} custom-call(s32[16]{0:T(128)S(1)} %fusion.2.src_ref, bf16[1024,512]{1,0:T(8,128)(2,1)} %copy-done.8, bf16[1024,512]{1,0:T(8,128)(2,1)} %copy-done.12, bf16[1024,512]{1,0:T(8,128)(2,1)} %copy-done.9, bf16[1024,512]{1,0:T(8,128)(2,1)} %copy-done.13, ...), custom_call_target="tpu_custom_call", output_to_operand_aliasing={{}: (9, {})} | custom-call | flops 1000 | bytes 1000 | tf_op jit(solution)/shard_map/pallas_call | solution.py:108
  107.8 0.2 collective-permute-start.22
  108.0 0.4 collective-permute-start.23
  108.4 0.1 collective-permute-start.18
  108.5 0.4 collective-permute-start.19
  108.9 0.1 pad_add_fusion.place_ref
  108.9 1.8 %collective-permute-done.18.mine1_ref = f32[32,1024]{1,0:T(8,128)S(1)} collective-permute-done((f32[32,1024]{1,0:T(8,128)S(1)}, f32[32,1024]{1,0:T(8,128)S(1)}, u32[]{:S(2)}, u32[]{:S(2)}) %collective-permute-start.18) | collective-permute-done | bytes 131104 | tf_op jit(solution)/shard_map/ppermute | solution.py:339
  110.7 0.2 collective-permute-done.19.across1_ref
  110.9 2.3 %shard_map.134 = (bf16[512,1024]{1,0:T(8,128)(2,1)S(1)}, bf16[512,1024]{1,0:T(8,128)(2,1)S(1)}, f32[8,4096]{1,0:T(8,128)S(1)}) custom-call(s32[2]{0:T(128)S(1)} %pad_add_fusion.place_ref, f32[8,1024]{1,0:T(8,128)S(1)} %select_reduce_fusion.weight_ref, f32[32,1024]{1,0:T(8,128)S(1)} %convert_add_fusion.1.mine_ref, ...), custom_call_target="tpu_custom_call" | custom-call | flops 1000 | bytes 1000 | tf_op jit(solution)/shard_map/pallas_call | solution.py:328
  113.2 0.8 copy-done.18
  114.0 0.2 copy-done.19
  114.1 8.6 %shard_map.135 = f32[8,4096]{1,0:T(8,128)S(1)} custom-call(bf16[512,512]{1,0:T(8,128)(2,1)} %copy-done.16, bf16[512,512]{1,0:T(8,128)(2,1)} %copy-done.18, bf16[512,512]{1,0:T(8,128)(2,1)} %copy-done.17, bf16[512,512]{1,0:T(8,128)(2,1)} %copy-done.19, bf16[2,1792,512]{2,1,0:T(8,128)(2,1)S(1)} %shard_map.129.refs_4_, f32[7,1024,256]{2,1,0:T(8,128)S(1)} %bitcast.6, ...), custom_call_target="tpu_custom_call" | custom-call | flops 1000 | bytes 1000 | tf_op jit(solution)/shard_map/pallas_call | solution.py:182
  122.8 0.2 collective-permute-start.24
  123.0 1.2 collective-permute-done.24
  124.2 1.8 %collective-permute-start.25 = (f32[8,4096]{1,0:T(8,128)S(1)}, f32[8,4096]{1,0:T(8,128)S(1)}, u32[]{:S(2)}, u32[]{:S(2)}) collective-permute-start(f32[8,4096]{1,0:T(8,128)S(1)} %select_add_fusion), channel_id=1, source_target_pairs={{0,2},{1,3},{2,0},{3,1},{4,6},{5,7},{6,4},{7,5},{8,10},{9,11},{10,... | collective-permute-start | bytes 393224 | tf_op jit(solution)/shard_map/ppermute | solution.py:339
  126.0 3.9 %collective-permute-done.25 = f32[8,4096]{1,0:T(8,128)S(1)} collective-permute-done((f32[8,4096]{1,0:T(8,128)S(1)}, f32[8,4096]{1,0:T(8,128)S(1)}, u32[]{:S(2)}, u32[]{:S(2)}) %collective-permute-start.25) | collective-permute-done | bytes 131104 | tf_op jit(solution)/shard_map/ppermute | solution.py:339
  129.8 0.3 collective-permute-start.26
  130.1 4.8 %collective-permute-done.26 = f32[8,4096]{1,0:T(8,128)S(1)} collective-permute-done((f32[8,4096]{1,0:T(8,128)S(1)}, f32[8,4096]{1,0:T(8,128)S(1)}, u32[]{:S(2)}, u32[]{:S(2)}) %collective-permute-start.26) | collective-permute-done | bytes 131104 | tf_op jit(solution)/shard_map/ppermute | solution.py:339
  134.9 0.1 collective-permute-start.27
  135.0 5.5 %collective-permute-done.27 = bf16[8,4096]{1,0:T(8,128)(2,1)S(1)} collective-permute-done((bf16[8,4096]{1,0:T(8,128)(2,1)S(1)}, bf16[8,4096]{1,0:T(8,128)(2,1)S(1)}, u32[]{:S(2)}, u32[]{:S(2)}) %collective-permute-start.27) | collective-permute-done | bytes 65568 | tf_op jit(solution)/shard_map/ppermute | solution.py:339
  140.5 0.1 collective-permute-start.28
  140.5 1.3 collective-permute-done.28
  141.9 1.0 shard_map.136
  (70 shorter events, 0.4 us)
Async XLA Ops:
  0.0 3.0 %copy-start = (bf16[64,8192]{1,0:T(8,128)(2,1)S(1)}, bf16[64,8192]{1,0:T(8,128)(2,1)}, u32[]{:S(2)}) copy-start(bf16[64,8192]{1,0:T(8,128)(2,1)} %param.19) | copy-start | bytes 3145732
  0.0 27.7 %collective-permute-start = (bf16[1024,512]{1,0:T(8,128)(2,1)}, bf16[1024,512]{1,0:T(8,128)(2,1)S(1)}, u32[]{:S(2)}, u32[]{:S(2)}) collective-permute-start(bf16[1024,512]{1,0:T(8,128)(2,1)} %refs_0_.1), channel_id=1, source_target_pairs={{0,4},{1,5},{4,8},{5,9},{8,12},{9,13},{12,14},{13,15},{14,10},{15,... | collective-permute-start | bytes 3145736 | tf_op jit(solution)/shard_map/ppermute | solution.py:387
  3.0 24.8 %collective-permute-start.1 = (bf16[1024,512]{1,0:T(8,128)(2,1)}, bf16[1024,512]{1,0:T(8,128)(2,1)S(1)}, u32[]{:S(2)}, u32[]{:S(2)}) collective-permute-start(bf16[1024,512]{1,0:T(8,128)(2,1)} %refs_0_.1), channel_id=1, source_target_pairs={{4,0},{5,1},{8,4},{9,5},{12,8},{13,9},{14,12},{15,13},{10,14},{11,... | collective-permute-start | bytes 3145736 | tf_op jit(solution)/shard_map/ppermute | solution.py:387
  3.0 24.8 %collective-permute-start.4 = (bf16[1024,512]{1,0:T(8,128)(2,1)}, bf16[1024,512]{1,0:T(8,128)(2,1)}, u32[]{:S(2)}, u32[]{:S(2)}) collective-permute-start(bf16[1024,512]{1,0:T(8,128)(2,1)} %refs_0_.1), channel_id=1, source_target_pairs={{0,1},{1,0},{2,3},{3,2},{4,5},{5,4},{6,7},{7,6},{8,9},{9,8},{10,11... | collective-permute-start | bytes 3145736 | tf_op jit(solution)/shard_map/ppermute | solution.py:339
  3.1 1.3 copy-start.3
  4.3 1.2 copy-start.4
  5.5 0.8 copy-start.7
  7.1 1.7 %collective-permute-start.2 = (f32[64,1024]{1,0:T(8,128)S(1)}, f32[64,1024]{1,0:T(8,128)S(1)}, u32[]{:S(2)}, u32[]{:S(2)}) collective-permute-start(f32[64,1024]{1,0:T(8,128)S(1)} %get-tuple-element.39), channel_id=1, source_target_pairs={{0,1},{1,0},{2,3},{3,2},{4,5},{5,4},{6,7},{7,6},{8,9},{9,8},{10,11... | collective-permute-start | bytes 786440 | tf_op jit(solution)/shard_map/ppermute | solution.py:339
  8.9 18.9 %collective-permute-start.3 = (bf16[32,1024]{1,0:T(8,128)(2,1)S(1)}, bf16[32,1024]{1,0:T(8,128)(2,1)S(1)}, u32[]{:S(2)}, u32[]{:S(2)}) collective-permute-start(bf16[32,1024]{1,0:T(8,128)(2,1)S(1)} %dynamic-slice_convert_fusion), channel_id=1, source_target_pairs={{0,2},{1,3},{2,0},{3,1},{4,6},{5,7},{6,4},{7,5},{8,10},{9,11},{10,... | collective-permute-start | bytes 196616 | tf_op jit(solution)/shard_map/ppermute | solution.py:339
  11.7 0.9 copy-start.6
  20.3 2.9 %copy-start.2 = (f32[7,1024,256]{2,1,0:T(8,128)}, f32[7,1024,256]{2,1,0:T(8,128)S(1)}, u32[]{:S(2)}) copy-start(f32[7,1024,256]{2,1,0:T(8,128)S(1)} %get-tuple-element.66.refs_5_) | copy-start | bytes 22020100
  27.7 5.0 %copy-start.10 = (bf16[1024,512]{1,0:T(8,128)(2,1)}, bf16[1024,512]{1,0:T(8,128)(2,1)S(1)}, u32[]{:S(2)}) copy-start(bf16[1024,512]{1,0:T(8,128)(2,1)S(1)} %collective-permute-done.refs_2_) | copy-start | bytes 3145732
  27.9 4.9 %copy-start.11 = (bf16[1024,512]{1,0:T(8,128)(2,1)}, bf16[1024,512]{1,0:T(8,128)(2,1)S(1)}, u32[]{:S(2)}) copy-start(bf16[1024,512]{1,0:T(8,128)(2,1)S(1)} %collective-permute-done.1.refs_4_) | copy-start | bytes 3145732
  27.9 4.9 %collective-permute-start.8 = (bf16[1024,512]{1,0:T(8,128)(2,1)S(1)}, bf16[1024,512]{1,0:T(8,128)(2,1)}, u32[]{:S(2)}, u32[]{:S(2)}) collective-permute-start(bf16[1024,512]{1,0:T(8,128)(2,1)S(1)} %collective-permute-done.refs_2_), channel_id=1, source_target_pairs={{0,1},{1,0},{2,3},{3,2},{4,5},{5,4},{6,7},{7,6},{8,9},{9,8},{10,11... | collective-permute-start | bytes 3145736 | tf_op jit(solution)/shard_map/ppermute | solution.py:339
  27.9 4.9 %collective-permute-start.9 = (bf16[1024,512]{1,0:T(8,128)(2,1)S(1)}, bf16[1024,512]{1,0:T(8,128)(2,1)}, u32[]{:S(2)}, u32[]{:S(2)}) collective-permute-start(bf16[1024,512]{1,0:T(8,128)(2,1)S(1)} %collective-permute-done.1.refs_4_), channel_id=1, source_target_pairs={{0,1},{1,0},{2,3},{3,2},{4,5},{5,4},{6,7},{7,6},{8,9},{9,8},{10,11... | collective-permute-start | bytes 3145736 | tf_op jit(solution)/shard_map/ppermute | solution.py:339
  28.4 27.8 %collective-permute-start.5 = (bf16[1024,512]{1,0:T(8,128)(2,1)S(1)}, bf16[1024,512]{1,0:T(8,128)(2,1)}, u32[]{:S(2)}, u32[]{:S(2)}) collective-permute-start(bf16[1024,512]{1,0:T(8,128)(2,1)S(1)} %collective-permute-done.refs_2_), channel_id=1, source_target_pairs={{0,4},{1,5},{4,8},{5,9},{8,12},{9,13},{12,14},{13,15},{14,10},{15,... | collective-permute-start | bytes 3145736 | tf_op jit(solution)/shard_map/ppermute | solution.py:387
  30.0 26.3 %collective-permute-start.6 = (bf16[1024,512]{1,0:T(8,128)(2,1)S(1)}, bf16[1024,512]{1,0:T(8,128)(2,1)}, u32[]{:S(2)}, u32[]{:S(2)}) collective-permute-start(bf16[1024,512]{1,0:T(8,128)(2,1)S(1)} %collective-permute-done.1.refs_4_), channel_id=1, source_target_pairs={{4,0},{5,1},{8,4},{9,5},{12,8},{13,9},{14,12},{15,13},{10,14},{11,... | collective-permute-start | bytes 3145736 | tf_op jit(solution)/shard_map/ppermute | solution.py:387
  30.4 25.8 %collective-permute-start.7 = (bf16[32,1024]{1,0:T(8,128)(2,1)S(1)}, bf16[32,1024]{1,0:T(8,128)(2,1)S(1)}, u32[]{:S(2)}, u32[]{:S(2)}) collective-permute-start(bf16[32,1024]{1,0:T(8,128)(2,1)S(1)} %fusion.1), channel_id=1, source_target_pairs={{0,4},{1,5},{2,6},{3,7},{4,0},{5,1},{6,2},{7,3},{8,12},{9,13},{10,... | collective-permute-start | bytes 196616 | tf_op jit(solution)/shard_map/ppermute | solution.py:339
  56.2 13.2 %collective-permute-start.13 = (bf16[1024,512]{1,0:T(8,128)(2,1)}, bf16[1024,512]{1,0:T(8,128)(2,1)S(1)}, u32[]{:S(2)}, u32[]{:S(2)}) collective-permute-start(bf16[1024,512]{1,0:T(8,128)(2,1)} %collective-permute-done.5.refs_0_), channel_id=1, source_target_pairs={{0,1},{1,0},{2,3},{3,2},{4,5},{5,4},{6,7},{7,6},{8,9},{9,8},{10,11... | collective-permute-start | bytes 3145736 | tf_op jit(solution)/shard_map/ppermute | solution.py:339
  56.2 13.2 %collective-permute-start.14 = (bf16[1024,512]{1,0:T(8,128)(2,1)}, bf16[1024,512]{1,0:T(8,128)(2,1)S(1)}, u32[]{:S(2)}, u32[]{:S(2)}) collective-permute-start(bf16[1024,512]{1,0:T(8,128)(2,1)} %collective-permute-done.6.refs_2_), channel_id=1, source_target_pairs={{0,1},{1,0},{2,3},{3,2},{4,5},{5,4},{6,7},{7,6},{8,9},{9,8},{10,11... | collective-permute-start | bytes 3145736 | tf_op jit(solution)/shard_map/ppermute | solution.py:339
  56.7 31.9 %collective-permute-start.10 = (bf16[1024,512]{1,0:T(8,128)(2,1)}, bf16[1024,512]{1,0:T(8,128)(2,1)S(1)}, u32[]{:S(2)}, u32[]{:S(2)}) collective-permute-start(bf16[1024,512]{1,0:T(8,128)(2,1)} %collective-permute-done.5.refs_0_), channel_id=1, source_target_pairs={{0,4},{1,5},{4,8},{5,9},{8,12},{9,13},{12,14},{13,15},{14,10},{15,... | collective-permute-start | bytes 3145736 | tf_op jit(solution)/shard_map/ppermute | solution.py:387
  58.3 30.4 %collective-permute-start.11 = (bf16[1024,512]{1,0:T(8,128)(2,1)}, bf16[1024,512]{1,0:T(8,128)(2,1)S(1)}, u32[]{:S(2)}, u32[]{:S(2)}) collective-permute-start(bf16[1024,512]{1,0:T(8,128)(2,1)} %collective-permute-done.6.refs_2_), channel_id=1, source_target_pairs={{4,0},{5,1},{8,4},{9,5},{12,8},{13,9},{14,12},{15,13},{10,14},{11,... | collective-permute-start | bytes 3145736 | tf_op jit(solution)/shard_map/ppermute | solution.py:387
  58.8 29.9 %collective-permute-start.12 = (bf16[32,1024]{1,0:T(8,128)(2,1)S(1)}, bf16[32,1024]{1,0:T(8,128)(2,1)S(1)}, u32[]{:S(2)}, u32[]{:S(2)}) collective-permute-start(bf16[32,1024]{1,0:T(8,128)(2,1)S(1)} %fusion), channel_id=1, source_target_pairs={{0,8},{1,9},{2,10},{3,11},{4,12},{5,13},{6,14},{7,15},{8,0},{9,1},... | collective-permute-start | bytes 196616 | tf_op jit(solution)/shard_map/ppermute | solution.py:339
  69.4 1.0 copy-start.14
  70.4 1.0 copy-start.15
  88.6 4.2 %copy-start.8 = (bf16[1024,512]{1,0:T(8,128)(2,1)}, bf16[1024,512]{1,0:T(8,128)(2,1)S(1)}, u32[]{:S(2)}) copy-start(bf16[1024,512]{1,0:T(8,128)(2,1)S(1)} %collective-permute-done.10.refs_0_) | copy-start | bytes 3145732
  88.7 4.2 %copy-start.9 = (bf16[1024,512]{1,0:T(8,128)(2,1)}, bf16[1024,512]{1,0:T(8,128)(2,1)S(1)}, u32[]{:S(2)}) copy-start(bf16[1024,512]{1,0:T(8,128)(2,1)S(1)} %collective-permute-done.11.refs_2_) | copy-start | bytes 3145732
  88.7 2.9 %collective-permute-start.15 = (bf16[1024,512]{1,0:T(8,128)(2,1)S(1)}, bf16[1024,512]{1,0:T(8,128)(2,1)S(1)}, u32[]{:S(2)}, u32[]{:S(2)}) collective-permute-start(bf16[1024,512]{1,0:T(8,128)(2,1)S(1)} %collective-permute-done.10.refs_0_), channel_id=1, source_target_pairs={{0,1},{1,0},{2,3},{3,2},{4,5},{5,4},{6,7},{7,6},{8,9},{9,8},{10,11... | collective-permute-start | bytes 3145736 | tf_op jit(solution)/shard_map/ppermute | solution.py:339
  88.7 4.1 %collective-permute-start.16 = (bf16[1024,512]{1,0:T(8,128)(2,1)S(1)}, bf16[1024,512]{1,0:T(8,128)(2,1)S(1)}, u32[]{:S(2)}, u32[]{:S(2)}) collective-permute-start(bf16[1024,512]{1,0:T(8,128)(2,1)S(1)} %collective-permute-done.11.refs_2_), channel_id=1, source_target_pairs={{0,1},{1,0},{2,3},{3,2},{4,5},{5,4},{6,7},{7,6},{8,9},{9,8},{10,11... | collective-permute-start | bytes 3145736 | tf_op jit(solution)/shard_map/ppermute | solution.py:339
  89.3 18.4 %collective-permute-start.20 = (bf16[512,512]{1,0:T(8,128)(2,1)S(1)}, bf16[512,512]{1,0:T(8,128)(2,1)S(1)}, u32[]{:S(2)}, u32[]{:S(2)}) collective-permute-start(bf16[512,512]{1,0:T(8,128)(2,1)S(1)} %slice.6), channel_id=1, source_target_pairs={{0,4},{1,5},{4,8},{5,9},{8,12},{9,13},{12,14},{13,15},{14,10},{15,... | collective-permute-start | bytes 1572872 | tf_op jit(solution)/shard_map/ppermute | solution.py:387
  89.4 18.4 %collective-permute-start.21 = (bf16[512,512]{1,0:T(8,128)(2,1)S(1)}, bf16[512,512]{1,0:T(8,128)(2,1)S(1)}, u32[]{:S(2)}, u32[]{:S(2)}) collective-permute-start(bf16[512,512]{1,0:T(8,128)(2,1)S(1)} %slice.7), channel_id=1, source_target_pairs={{4,0},{5,1},{8,4},{9,5},{12,8},{13,9},{14,12},{15,13},{10,14},{11,... | collective-permute-start | bytes 1572872 | tf_op jit(solution)/shard_map/ppermute | solution.py:387
  91.4 22.7 %slice-start = ((s8[7340032]{0:T(1024)(128)(4,1)}), s8[4194304]{0:T(1024)(128)(4,1)S(1)}, s32[]{:S(2)}) async-start(s8[7340032]{0:T(1024)(128)(4,1)} %bitcast.5), calls=%async_computation | async-start | bytes 8388608
  91.4 22.7 %slice-start.1 = ((s8[7340032]{0:T(1024)(128)(4,1)}), s8[3145728]{0:T(1024)(128)(4,1)S(1)}, s32[]{:S(2)}) async-start(s8[7340032]{0:T(1024)(128)(4,1)} %bitcast.5), calls=%async_computation.1 | async-start | bytes 6291456
  91.4 22.7 %copy-start.5 = (bf16[64,1792]{1,0:T(8,128)(2,1)S(1)}, bf16[64,1792]{1,0:T(8,128)(2,1)}, u32[]{:S(2)}) copy-start(bf16[64,1792]{1,0:T(8,128)(2,1)} %refs_6_.7) | copy-start | bytes 688132
  91.5 16.3 %collective-permute-start.17 = (f32[32,1024]{1,0:T(8,128)S(1)}, f32[32,1024]{1,0:T(8,128)S(1)}, u32[]{:S(2)}, u32[]{:S(2)}) collective-permute-start(f32[32,1024]{1,0:T(8,128)S(1)} %convert_add_fusion.1.mine_ref), channel_id=1, source_target_pairs={{0,2},{1,3},{2,0},{3,1},{4,6},{5,7},{6,4},{7,5},{8,10},{9,11},{10,... | collective-permute-start | bytes 393224 | tf_op jit(solution)/shard_map/ppermute | solution.py:339
  91.6 1.3 copy-start.12
  92.9 1.0 copy-start.13
  107.7 5.4 %copy-start.16 = (bf16[512,512]{1,0:T(8,128)(2,1)}, bf16[512,512]{1,0:T(8,128)(2,1)S(1)}, u32[]{:S(2)}) copy-start(bf16[512,512]{1,0:T(8,128)(2,1)S(1)} %collective-permute-done.20.refs_0_) | copy-start | bytes 1572868
  107.8 5.4 %copy-start.17 = (bf16[512,512]{1,0:T(8,128)(2,1)}, bf16[512,512]{1,0:T(8,128)(2,1)S(1)}, u32[]{:S(2)}) copy-start(bf16[512,512]{1,0:T(8,128)(2,1)S(1)} %collective-permute-done.21.refs_2_) | copy-start | bytes 1572868
  107.8 5.4 %collective-permute-start.22 = (bf16[512,512]{1,0:T(8,128)(2,1)S(1)}, bf16[512,512]{1,0:T(8,128)(2,1)S(1)}, u32[]{:S(2)}, u32[]{:S(2)}) collective-permute-start(bf16[512,512]{1,0:T(8,128)(2,1)S(1)} %collective-permute-done.20.refs_0_), channel_id=1, source_target_pairs={{0,1},{1,0},{2,3},{3,2},{4,5},{5,4},{6,7},{7,6},{8,9},{9,8},{10,11... | collective-permute-start | bytes 1572872 | tf_op jit(solution)/shard_map/ppermute | solution.py:339
  108.0 5.2 %collective-permute-start.23 = (bf16[512,512]{1,0:T(8,128)(2,1)S(1)}, bf16[512,512]{1,0:T(8,128)(2,1)S(1)}, u32[]{:S(2)}, u32[]{:S(2)}) collective-permute-start(bf16[512,512]{1,0:T(8,128)(2,1)S(1)} %collective-permute-done.21.refs_2_), channel_id=1, source_target_pairs={{0,1},{1,0},{2,3},{3,2},{4,5},{5,4},{6,7},{7,6},{8,9},{9,8},{10,11... | collective-permute-start | bytes 1572872 | tf_op jit(solution)/shard_map/ppermute | solution.py:339
  108.4 2.3 %collective-permute-start.18 = (f32[32,1024]{1,0:T(8,128)S(1)}, f32[32,1024]{1,0:T(8,128)S(1)}, u32[]{:S(2)}, u32[]{:S(2)}) collective-permute-start(f32[32,1024]{1,0:T(8,128)S(1)} %convert_add_fusion.1.mine_ref), channel_id=1, source_target_pairs={{0,1},{1,0},{2,3},{3,2},{4,5},{5,4},{6,7},{7,6},{8,9},{9,8},{10,11... | collective-permute-start | bytes 393224 | tf_op jit(solution)/shard_map/ppermute | solution.py:339
  108.5 2.4 %collective-permute-start.19 = (f32[32,1024]{1,0:T(8,128)S(1)}, f32[32,1024]{1,0:T(8,128)S(1)}, u32[]{:S(2)}, u32[]{:S(2)}) collective-permute-start(f32[32,1024]{1,0:T(8,128)S(1)} %collective-permute-done.17.across_ref), channel_id=1, source_target_pairs={{0,1},{1,0},{2,3},{3,2},{4,5},{5,4},{6,7},{7,6},{8,9},{9,8},{10,11... | collective-permute-start | bytes 393224 | tf_op jit(solution)/shard_map/ppermute | solution.py:339
  113.1 0.8 copy-start.18
  113.2 0.9 copy-start.19
  114.1 28.8 %copy-start.1 = (bf16[64,8192]{1,0:T(8,128)(2,1)S(1)}, bf16[64,8192]{1,0:T(8,128)(2,1)}, u32[]{:S(2)}) copy-start(bf16[64,8192]{1,0:T(8,128)(2,1)} %param.19) | copy-start | bytes 3145732
  122.8 1.4 collective-permute-start.24
  124.2 5.6 %collective-permute-start.25 = (f32[8,4096]{1,0:T(8,128)S(1)}, f32[8,4096]{1,0:T(8,128)S(1)}, u32[]{:S(2)}, u32[]{:S(2)}) collective-permute-start(f32[8,4096]{1,0:T(8,128)S(1)} %select_add_fusion), channel_id=1, source_target_pairs={{0,2},{1,3},{2,0},{3,1},{4,6},{5,7},{6,4},{7,5},{8,10},{9,11},{10,... | collective-permute-start | bytes 393224 | tf_op jit(solution)/shard_map/ppermute | solution.py:339
  129.8 5.0 %collective-permute-start.26 = (f32[8,4096]{1,0:T(8,128)S(1)}, f32[8,4096]{1,0:T(8,128)S(1)}, u32[]{:S(2)}, u32[]{:S(2)}) collective-permute-start(f32[8,4096]{1,0:T(8,128)S(1)} %add.62), channel_id=1, source_target_pairs={{0,4},{1,5},{2,6},{3,7},{4,0},{5,1},{6,2},{7,3},{8,12},{9,13},{10,... | collective-permute-start | bytes 393224 | tf_op jit(solution)/shard_map/ppermute | solution.py:339
  134.9 5.6 %collective-permute-start.27 = (bf16[8,4096]{1,0:T(8,128)(2,1)S(1)}, bf16[8,4096]{1,0:T(8,128)(2,1)S(1)}, u32[]{:S(2)}, u32[]{:S(2)}) collective-permute-start(bf16[8,4096]{1,0:T(8,128)(2,1)S(1)} %get-tuple-element.71), channel_id=1, source_target_pairs={{0,8},{1,9},{2,10},{3,11},{4,12},{5,13},{6,14},{7,15},{8,0},{9,1},... | collective-permute-start | bytes 196616 | tf_op jit(solution)/shard_map/ppermute | solution.py:339
  140.5 1.4 collective-permute-start.28

commit v4 on v3

--- a/solution.py
+++ b/solution.py
@@ -87,7 +87,8 @@
 def step_parts(units, weight):
     tokens, depth = units[0][0].shape
     tile = tile_of(weight.shape[0])
-    ins = [in_hbm(array) for array, _ in units] + [in_hbm(weight)] * len(units)
+    ins = [in_hbm(array) if place == 0 else array for array, place in units]
+    ins += [in_hbm(weight)] * len(units)
     specs = [ANYWHERE] * len(units)
     specs += [pl.BlockSpec((tile, depth), lambda i, s, m=m: (i, s[m])) for _, m in units]
     scratch = [
@@ -121,13 +122,13 @@
     )(src, *ins)
 
 
-def columns_kernel(first, src_ref, weight_ref, out_ref, sems):
+def columns_kernel(places, src_ref, weight_ref, out_ref, sems):
     depth = out_ref.shape[2]
     copies = []
-    for m in range(2):
-        start = pl.multiple_of(src_ref[first + m] * depth, depth)
+    for i, place in enumerate(places):
+        start = pl.multiple_of(src_ref[place] * depth, depth)
         copies.append(
-            pltpu.make_async_copy(weight_ref.at[:, pl.ds(start, depth)], out_ref.at[m], sems.at[m])
+            pltpu.make_async_copy(weight_ref.at[:, pl.ds(start, depth)], out_ref.at[i], sems.at[i])
         )
     for copy in copies:
         copy.start()
@@ -135,35 +136,34 @@
         copy.wait()
 
 
-def last_columns(src, weight, depth):
-    return pl.pallas_call(
-        functools.partial(columns_kernel, src.shape[0] - 2),
+def columns_of(src, weight, depth, places):
+    return pl.pallas_call(
+        functools.partial(columns_kernel, places),
         grid_spec=pltpu.PrefetchScalarGridSpec(
             num_scalar_prefetch=1,
             grid=(),
-            in_specs=[pl.BlockSpec(memory_space=pl.ANY)],
-            out_specs=pl.BlockSpec(memory_space=pltpu.VMEM),
-            scratch_shapes=[pltpu.SemaphoreType.DMA((2,))],
+            in_specs=[ANYWHERE],
+            out_specs=WHOLE,
+            scratch_shapes=[pltpu.SemaphoreType.DMA((len(places),))],
         ),
-        out_shape=pltpu.VMEM((2, weight.shape[0], depth), BF16),
+        out_shape=pltpu.VMEM((len(places), weight.shape[0], depth), BF16),
         cost_estimate=SMALL,
         compiler_params=pltpu.CompilerParams(vmem_limit_bytes=VMEM_LIMIT),
     )(src, in_hbm(weight))
 
 
 def last_kernel(*refs):
-    blocks = refs[:4]
+    halves = refs[:4]
     weight_ref, silu_ref, proj_ref, before_ref, high_ref, low_ref, out_ref, lefts, ups, sems = refs[4:]
     half, tile = lefts.shape[1] // 2, ups.shape[2]
-    load([(block, 0) for block in (blocks[0], blocks[2], blocks[1], blocks[3])], lefts, sems)
+    load([(halves[i], 0) for i in (0, 2, 1, 3)], lefts, sems)
     for i in range(ups.shape[0]):
         cols = slice(i * tile, (i + 1) * tile)
         for h in range(2):
             rows = slice(h * half, (h + 1) * half)
-            grad = dot_t(lefts[0, rows, :], weight_ref[0, cols, :]) + dot_t(
-                lefts[1, rows, :], weight_ref[1, cols, :]
-            )
-            grad = grad + before_ref[i, rows, :]
+            grad = before_ref[i, rows, :]
+            for m in range(lefts.shape[0]):
+                grad = grad + dot_t(lefts[m, rows, :], weight_ref[m, cols, :])
             ups[i, rows, :] = (grad * silu_ref[i, rows, :]).astype(BF16)
     b_high, b_low = parts_of(projected(ups, proj_ref))
     kos = b_high.shape[1]
@@ -174,10 +174,9 @@
     out_ref[...] = spread(sums[:, :kos] + (sums[:, kos:] + rest), out_ref.shape[0])
 
 
-def last_step(blocks, columns, silu, proj_up, before, up, pairs):
-    half, depth = blocks[0].shape
+def last_step(halves, columns, silu, proj_up, before, up, pairs):
     tiles, tokens, tile = silu.shape
-    kos = proj_up.shape[0]
+    depth, kos = halves[0].shape[1], proj_up.shape[0]
     ins = [in_vmem(x) for x in (columns, silu, proj_up, before, *up)]
     return pl.pallas_call(
         last_kernel,
@@ -191,7 +190,7 @@
         ],
         cost_estimate=SMALL,
         compiler_params=pltpu.CompilerParams(vmem_limit_bytes=VMEM_LIMIT),
-    )(*[in_hbm(x) for x in blocks], *ins)
+    )(*halves, *ins)
 
 
 def own_kernel(gate_ref, up_ref, down_ref, silu_ref, out_ref, hidden):
@@ -393,7 +392,7 @@
     part = keep + swap(give, 1, devices)
     gate_pre, up_pre, part = pin((gate_pre, up_pre, part))
     silu_gate, a_down = own_parts(gate_pre, up_pre, in_proj_down)
-    bits = [1 << i for i in range(2, devices.bit_length() - 1)]
+    bits = [1 << i for i in reversed(range(2, devices.bit_length() - 1))]
     rounds = [[]] + [[int(bit) for bit in some] for some in np.array_split(bits, far - 2)]
     row = part.shape[0] // 2
     side = (me // 2) % 2
@@ -414,7 +413,7 @@
     per_seq = jnp.where(segments[None, :] == seqs, signs[:, None], F32(0.0))
     pair_weight = per_seq.reshape(pairs, 2, tokens).sum(axis=1)
 
-    f, b, theirs, other, a_down, pair_weight = pin((f, b, theirs, other, a_down, pair_weight))
+    f, b, theirs, a_down, pair_weight = pin((f, b, theirs, a_down, pair_weight))
     part = added(part, theirs)
     known, came = None, (f, b)
     units = [(out_grad, 0), (other, 1)]
@@ -425,20 +424,21 @@
         else:
             f, b = send(f[:half], b[half:])
         place = 4 * step - 2
-        for i, array in enumerate(came):
-            units += [(array, place + 2 * i), (swap(array, 1, devices), place + 2 * i + 1)]
+        theirs_of = [swap(array, 1, devices) for array in came]
+        units += [(array, place + 2 * i) for i, array in enumerate(came)]
+        units += [(array, place + 2 * i + 1) for i, array in enumerate(theirs_of)]
+        if step == far - 3:
+            q_turned = turned(queries, kos)
+            src, q_turned = pin((src, q_turned))
         if step == far - 2:
-            columns, q_turned = last_columns(src, down_weight, depth), turned(queries, kos)
-            src, columns, q_turned = pin((src, columns, q_turned))
+            columns = columns_of(src, down_weight, depth, (devices - 2, devices - 1))
+            src, columns = pin((src, columns))
         if step == far - 1:
+            quarters = [part] + [swap(part, bit, devices) for bit in (2, 1, 3)]
             known = add_step(src, units, down_weight, known)
-            across = swap(part, 2, devices)
-            known, part, across = pin((known, part, across))
+            known, quarters = pin((known, quarters))
             high, low, down = pair_parts(
-                jnp.stack([me % 2, side]),
-                pair_weight,
-                (part, across, swap(part, 1, devices), swap(across, 1, devices)),
-                a_down,
+                jnp.stack([me % 2, side]), pair_weight, quarters, a_down
             )
         else:
             known = add_step(src, units, down_weight, known)
@@ -447,16 +447,13 @@
             part = added(part, theirs)
             came = (f, b)
     f, b, known = pin((f, b, known))
-    blocks = [x for block in (f, b) for x in (block, swap(block, 1, devices))]
-    up = last_step(blocks, columns, silu_gate, out_proj_up, known, (high, low), pairs)
+    halves = [x for block in (f, b) for x in (block, swap(block, 1, devices))]
+    up = last_step(halves, columns, silu_gate, out_proj_up, known, (high, low), pairs)
 
     first = core == 0
     total = jnp.where(first, down, up) + swap(jnp.where(first, up, down), 1, devices)
     for bit in range(1, devices.bit_length() - 1):
-        if bit < 3:
-            total = total + swap(total, 1 << bit, devices)
-        else:
-            total = total + swap(total.astype(BF16), 1 << bit, devices).astype(F32)
+        total = total + swap(total.astype(BF16), 1 << bit, devices).astype(F32)
     rest = swap(total, 1, devices)
     return score(jnp.where(first, total, rest), jnp.where(first, rest, total), q_turned)
 

time: 143 us -> 136 us (0.951)
  Pallas kernels: 72.7 us -> 68.2 us
  waiting for transfers between devices: 33.6 us -> 30 us
  other arithmetic: 1.72 us -> 5.3 us
  local copies, waits for them, and re-layouts: 11.9 us -> 9.02 us
    unnamed x44 -> x20, local copies, waits for them, and re-layouts: 10.9 us -> 7.17 us
    ppermute x21, waiting for transfers between devices: 33.4 us -> 29.8 us  [swap(): return lax.ppermute(value, 'tensor', [(i, i ^ bit) for i in range(devices)])]
    pallas_call x3, Pallas kernels: 46 us -> 42.9 us  [add_step(): pl.pallas_call(functools.partial(step_kernel, len(units)), grid_spec=pltp...]
    convert_element_type x2, other arithmetic: 0.04 us -> 1.85 us  [ask(): return [swap(part.astype(BF16), bit, devices) for bit in rounds[step]]]
  transfers between devices with their start and end apart: 29 -> 29, of which waited for: 13 -> 13; matrix products, arithmetic and copies ran while one was open for 2% -> 5% of each run, Pallas kernels for 44% -> 44%
where the time goes in v4:
time: 136 us; the launch traced here: 135 us
  Pallas kernels  68.2 us (50%)
  waiting for transfers between devices  30 us (22%)
  starting transfers between devices  22.5 us (17%)
  local copies, waits for them, and re-layouts  9.02 us (7%)
  other arithmetic  5.3 us (4%)
    pallas_call x3, Pallas kernels, add_step(): pl.pallas_call(functools.partial(step_kernel, len(units)), grid_spec=pltp...  42.9 us
    ppermute x21, waiting for transfers between devices, swap(): return lax.ppermute(value, 'tensor', [(i, i ^ bit) for i in range(devices)])  29.8 us
    ppermute x21, starting transfers between devices, swap(): return lax.ppermute(value, 'tensor', [(i, i ^ bit) for i in range(devices)])  13.3 us
    pallas_call x1, Pallas kernels, own_parts(): pl.pallas_call(own_kernel, grid=(units // tile,), in_specs=[tiles, tiles,...  7.61 us
    pallas_call x1, Pallas kernels, last_step(): pl.pallas_call(last_kernel, in_specs=[ANYWHERE] * 4 + [WHOLE] * len(ins),...  7.2 us
    unnamed x20, local copies, waits for them, and re-layouts  7.17 us
    ppermute x4, starting transfers between devices, send(): lax.ppermute(forward, 'tensor', ahead)  5.37 us
    pallas_call x1, Pallas kernels, turned(): pl.pallas_call(kernel, grid=(2,), in_specs=[pl.BlockSpec((asked, size), l...  3.87 us
  transfers between devices with their start and end apart: 29, of which 13 were waited for; matrix products, arithmetic and copies ran while one was open for 5% of the time, Pallas kernels for 44%

profile of v4, /device:TPU:0, one launch (start us, length us, event | category | flops | bytes accessed | tf_op | source)
XLA Modules:
  0.0 135.3 jit_solution(5646023461228088797)
XLA Ops:
  0.0 3.0 %collective-permute-start = (bf16[1024,512]{1,0:T(8,128)(2,1)}, bf16[1024,512]{1,0:T(8,128)(2,1)}, u32[]{:S(2)}, u32[]{:S(2)}) collective-permute-start(bf16[1024,512]{1,0:T(8,128)(2,1)} %refs_0_.1), channel_id=1, source_target_pairs={{0,4},{1,5},{4,8},{5,9},{8,12},{9,13},{12,14},{13,15},{14,10},{15,... | collective-permute-start | bytes 3145736 | tf_op jit(solution)/shard_map/ppermute | solution.py:386
  3.1 0.0 copy-start.3
  3.1 1.3 copy-done.3
  4.3 1.2 copy-done.4
  5.5 0.8 copy-done.7
  6.4 0.7 shard_map.127
  7.1 0.5 collective-permute-start.2
  7.7 0.7 add_convert_fusion
  8.3 0.1 broadcast_in_dim.39
  8.4 0.1 copy.16
  8.5 0.3 collective-permute-done.2
  8.8 0.7 add.54
  9.6 0.9 dynamic-slice_convert_fusion
  10.5 2.0 %collective-permute-start.3 = (bf16[32,1024]{1,0:T(8,128)(2,1)S(1)}, bf16[32,1024]{1,0:T(8,128)(2,1)S(1)}, u32[]{:S(2)}, u32[]{:S(2)}) collective-permute-start(bf16[32,1024]{1,0:T(8,128)(2,1)S(1)} %dynamic-slice_convert_fusion), channel_id=1, source_target_pairs={{0,2},{1,3},{2,0},{3,1},{4,6},{5,7},{6,4},{7,5},{8,10},{9,11},{10,... | collective-permute-start | bytes 196616 | tf_op jit(solution)/shard_map/ppermute | solution.py:338
  12.5 0.8 select_reduce_fusion.weight_ref
  13.3 0.9 copy-done.6
  14.2 7.6 %shard_map.128 = (f32[7,1024,256]{2,1,0:T(8,128)S(1)}, f32[64,1024]{1,0:T(8,128)S(1)}) custom-call(bf16[1024,1792]{1,0:T(8,128)(2,1)} %gate_ref, bf16[1024,1792]{1,0:T(8,128)(2,1)} %up_ref, bf16[64,1792]{1,0:T(8,128)(2,1)S(1)} %copy-done.6), custom_call_target="tpu_custom_call" | custom-call | flops 1000 | bytes 1000 | tf_op jit(solution)/shard_map/pallas_call | solution.py:216
  21.8 2.9 %copy-done.2 = f32[7,1024,256]{2,1,0:T(8,128)} copy-done((f32[7,1024,256]{2,1,0:T(8,128)}, f32[7,1024,256]{2,1,0:T(8,128)S(1)}, u32[]{:S(2)}) %copy-start.2) | copy-done | bytes 7340056
  24.7 3.0 %collective-permute-done.3 = bf16[32,1024]{1,0:T(8,128)(2,1)S(1)} collective-permute-done((bf16[32,1024]{1,0:T(8,128)(2,1)S(1)}, bf16[32,1024]{1,0:T(8,128)(2,1)S(1)}, u32[]{:S(2)}, u32[]{:S(2)}) %collective-permute-start.3) | collective-permute-done | bytes 65568 | tf_op jit(solution)/shard_map/ppermute | solution.py:338
  27.7 0.2 collective-permute-done.1.refs_3_
  28.0 0.5 collective-permute-start.9
  28.5 1.6 %collective-permute-start.4 = (bf16[1024,512]{1,0:T(8,128)(2,1)}, bf16[1024,512]{1,0:T(8,128)(2,1)}, u32[]{:S(2)}, u32[]{:S(2)}) collective-permute-start(bf16[1024,512]{1,0:T(8,128)(2,1)} %collective-permute-done.refs_2_), channel_id=1, source_target_pairs={{0,4},{1,5},{4,8},{5,9},{8,12},{9,13},{12,14},{13,15},{14,10},{15,... | collective-permute-start | bytes 3145736 | tf_op jit(solution)/shard_map/ppermute | solution.py:386
  30.1 0.4 collective-permute-start.5
  30.5 3.9 %shard_map.129.q_ref = bf16[8192,64]{1,0:T(8,128)(2,1)S(1)} custom-call(bf16[64,8192]{1,0:T(8,128)(2,1)} %q_ref.1), custom_call_target="tpu_custom_call" | custom-call | flops 1000 | bytes 1000 | tf_op jit(solution)/shard_map/pallas_call | solution.py:240
  34.4 0.9 fusion.3
  35.3 3.5 %collective-permute-start.6 = (bf16[32,1024]{1,0:T(8,128)(2,1)S(1)}, bf16[32,1024]{1,0:T(8,128)(2,1)S(1)}, u32[]{:S(2)}, u32[]{:S(2)}) collective-permute-start(bf16[32,1024]{1,0:T(8,128)(2,1)S(1)} %fusion.3), channel_id=1, source_target_pairs={{0,8},{1,9},{2,10},{3,11},{4,12},{5,13},{6,14},{7,15},{8,0},{9,1},... | collective-permute-start | bytes 196616 | tf_op jit(solution)/shard_map/ppermute | solution.py:338
  38.8 0.7 fusion.4.src_ref
  39.5 17.9 %shard_map.131.refs_8_ = f32[7,1024,256]{2,1,0:T(8,128)S(1)} custom-call(s32[16]{0:T(128)S(1)} %fusion.4.src_ref, bf16[1024,512]{1,0:T(8,128)(2,1)} %refs_0_.1, bf16[1024,512]{1,0:T(8,128)(2,1)} %collective-permute-done.7.refs_1_, bf16[1024,512]{1,0:T(8,128)(2,1)} %collective-permute-done.refs_2_, bf16[1024,512]{1,0:T(8,128)(2,1)} %collective-permute-done.1.refs_3_, ...), custom_call_target="tpu_custom_call" | custom-call | flops 1000 | bytes 1000 | tf_op jit(solution)/shard_map/pallas_call | solution.py:109
  57.4 2.7 %collective-permute-done.6 = bf16[32,1024]{1,0:T(8,128)(2,1)S(1)} collective-permute-done((bf16[32,1024]{1,0:T(8,128)(2,1)S(1)}, bf16[32,1024]{1,0:T(8,128)(2,1)S(1)}, u32[]{:S(2)}, u32[]{:S(2)}) %collective-permute-start.6) | collective-permute-done | bytes 65568 | tf_op jit(solution)/shard_map/ppermute | solution.py:338
  60.0 0.5 collective-permute-start.14
  60.5 0.4 collective-permute-start.10
  61.0 1.6 %collective-permute-start.11 = (bf16[1024,512]{1,0:T(8,128)(2,1)}, bf16[1024,512]{1,0:T(8,128)(2,1)S(1)}, u32[]{:S(2)}, u32[]{:S(2)}) collective-permute-start(bf16[1024,512]{1,0:T(8,128)(2,1)} %collective-permute-done.5.refs_1_), channel_id=1, source_target_pairs={{4,0},{5,1},{8,4},{9,5},{12,8},{13,9},{14,12},{15,13},{10,14},{11,... | collective-permute-start | bytes 3145736 | tf_op jit(solution)/shard_map/ppermute | solution.py:386
  62.6 0.9 fusion
  63.5 0.5 collective-permute-start.12
  64.0 2.6 %shard_map.130.refs_4_ = bf16[2,1792,512]{2,1,0:T(8,128)(2,1)S(1)} custom-call(s32[16]{0:T(128)S(1)} %fusion.4.src_ref, bf16[1792,8192]{1,0:T(8,128)(2,1)} %refs_7_.5), custom_call_target="tpu_custom_call" | custom-call | flops 1000 | bytes 1000 | tf_op jit(solution)/shard_map/pallas_call | solution.py:140
  66.7 13.2 %shard_map.132.refs_8_ = f32[7,1024,256]{2,1,0:T(8,128)S(1)} custom-call(s32[16]{0:T(128)S(1)} %fusion.4.src_ref, bf16[1024,512]{1,0:T(8,128)(2,1)} %collective-permute-done.4.refs_0_, bf16[1024,512]{1,0:T(8,128)(2,1)} %collective-permute-done.5.refs_1_, bf16[1024,512]{1,0:T(8,128)(2,1)S(1)} %collective-permute-done.13.refs_2_, ...), custom_call_target="tpu_custom_call", output_to_operand_aliasing={{}: (9, {})} | custom-call | flops 1000 | bytes 1000 | tf_op jit(solution)/shard_map/pallas_call | solution.py:109
  79.8 7.6 %collective-permute-done.12 = bf16[32,1024]{1,0:T(8,128)(2,1)S(1)} collective-permute-done((bf16[32,1024]{1,0:T(8,128)(2,1)S(1)}, bf16[32,1024]{1,0:T(8,128)(2,1)S(1)}, u32[]{:S(2)}, u32[]{:S(2)}) %collective-permute-start.12) | collective-permute-done | bytes 65568 | tf_op jit(solution)/shard_map/ppermute | solution.py:338
  87.5 0.5 collective-permute-start.16
  88.1 0.3 collective-permute-start.20
  88.4 1.7 %collective-permute-start.21 = (bf16[512,512]{1,0:T(8,128)(2,1)S(1)}, bf16[512,512]{1,0:T(8,128)(2,1)S(1)}, u32[]{:S(2)}, u32[]{:S(2)}) collective-permute-start(bf16[512,512]{1,0:T(8,128)(2,1)S(1)} %slice.7), channel_id=1, source_target_pairs={{4,0},{5,1},{8,4},{9,5},{12,8},{13,9},{14,12},{15,13},{10,14},{11,... | collective-permute-start | bytes 1572872 | tf_op jit(solution)/shard_map/ppermute | solution.py:386
  90.1 1.1 convert_add_fusion.3.mine_ref
  91.2 0.0 copy-start.5
  91.2 0.2 collective-permute-start.17
  91.5 0.1 collective-permute-done.16.refs_3_
  91.6 1.8 %collective-permute-start.19 = (f32[32,1024]{1,0:T(8,128)S(1)}, f32[32,1024]{1,0:T(8,128)S(1)}, u32[]{:S(2)}, u32[]{:S(2)}) collective-permute-start(f32[32,1024]{1,0:T(8,128)S(1)} %convert_add_fusion.3.mine_ref), channel_id=1, source_target_pairs={{0,3},{1,2},{2,1},{3,0},{4,7},{5,6},{6,5},{7,4},{8,11},{9,10},{10,... | collective-permute-start | bytes 393224 | tf_op jit(solution)/shard_map/ppermute | solution.py:338
  93.5 11.8 %shard_map.133.refs_7_ = f32[7,1024,256]{2,1,0:T(8,128)S(1)} custom-call(s32[16]{0:T(128)S(1)} %fusion.4.src_ref, bf16[1024,512]{1,0:T(8,128)(2,1)S(1)} %collective-permute-done.10.refs_0_, bf16[1024,512]{1,0:T(8,128)(2,1)S(1)} %collective-permute-done.11.refs_1_, ...), custom_call_target="tpu_custom_call", output_to_operand_aliasing={{}: (9, {})} | custom-call | flops 1000 | bytes 1000 | tf_op jit(solution)/shard_map/pallas_call | solution.py:109
  105.3 0.4 collective-permute-done.17.across_ref
  105.7 1.2 collective-permute-done.19.across1_ref
  106.9 0.6 collective-permute-start.22
  107.5 0.1 collective-permute-start.23
  107.5 0.1 pad_add_fusion.place_ref
  107.6 2.3 %shard_map.134 = (bf16[512,1024]{1,0:T(8,128)(2,1)S(1)}, bf16[512,1024]{1,0:T(8,128)(2,1)S(1)}, f32[8,4096]{1,0:T(8,128)S(1)}) custom-call(s32[2]{0:T(128)S(1)} %pad_add_fusion.place_ref, f32[8,1024]{1,0:T(8,128)S(1)} %select_reduce_fusion.weight_ref, f32[32,1024]{1,0:T(8,128)S(1)} %convert_add_fusion.3.mine_ref, ...), custom_call_target="tpu_custom_call" | custom-call | flops 1000 | bytes 1000 | tf_op jit(solution)/shard_map/pallas_call | solution.py:327
  109.9 7.2 %shard_map.135 = f32[8,4096]{1,0:T(8,128)S(1)} custom-call(bf16[512,512]{1,0:T(8,128)(2,1)S(1)} %collective-permute-done.20.refs_0_, bf16[512,512]{1,0:T(8,128)(2,1)S(1)} %collective-permute-done.22.refs_1_, bf16[512,512]{1,0:T(8,128)(2,1)S(1)} %collective-permute-done.21.refs_2_, bf16[512,512]{1,0:T(8,128)(2,1)S(1)} %collective-permute-done.23.refs_3_, ...), custom_call_target="tpu_custom_call" | custom-call | flops 1000 | bytes 1000 | tf_op jit(solution)/shard_map/pallas_call | solution.py:181
  117.2 0.5 collective-permute-start.24
  117.7 1.0 collective-permute-done.24
  118.7 1.8 %collective-permute-start.25 = (bf16[8,4096]{1,0:T(8,128)(2,1)S(1)}, bf16[8,4096]{1,0:T(8,128)(2,1)S(1)}, u32[]{:S(2)}, u32[]{:S(2)}) collective-permute-start(bf16[8,4096]{1,0:T(8,128)(2,1)S(1)} %get-tuple-element.75), channel_id=1, source_target_pairs={{0,2},{1,3},{2,0},{3,1},{4,6},{5,7},{6,4},{7,5},{8,10},{9,11},{10,... | collective-permute-start | bytes 196616 | tf_op jit(solution)/shard_map/ppermute | solution.py:338
  120.5 2.6 %collective-permute-done.25 = bf16[8,4096]{1,0:T(8,128)(2,1)S(1)} collective-permute-done((bf16[8,4096]{1,0:T(8,128)(2,1)S(1)}, bf16[8,4096]{1,0:T(8,128)(2,1)S(1)}, u32[]{:S(2)}, u32[]{:S(2)}) %collective-permute-start.25) | collective-permute-done | bytes 65568 | tf_op jit(solution)/shard_map/ppermute | solution.py:338
  123.1 0.1 collective-permute-start.26
  123.2 4.3 %collective-permute-done.26 = bf16[8,4096]{1,0:T(8,128)(2,1)S(1)} collective-permute-done((bf16[8,4096]{1,0:T(8,128)(2,1)S(1)}, bf16[8,4096]{1,0:T(8,128)(2,1)S(1)}, u32[]{:S(2)}, u32[]{:S(2)}) %collective-permute-start.26) | collective-permute-done | bytes 65568 | tf_op jit(solution)/shard_map/ppermute | solution.py:338
  127.5 0.1 collective-permute-start.27
  127.6 5.3 %collective-permute-done.27 = bf16[8,4096]{1,0:T(8,128)(2,1)S(1)} collective-permute-done((bf16[8,4096]{1,0:T(8,128)(2,1)S(1)}, bf16[8,4096]{1,0:T(8,128)(2,1)S(1)}, u32[]{:S(2)}, u32[]{:S(2)}) %collective-permute-start.27) | collective-permute-done | bytes 65568 | tf_op jit(solution)/shard_map/ppermute | solution.py:338
  132.9 0.1 collective-permute-start.28
  133.0 1.3 collective-permute-done.28
  134.3 1.0 shard_map.136
  (46 shorter events, 0.3 us)
Async XLA Ops:
  0.0 3.0 %copy-start = (bf16[64,8192]{1,0:T(8,128)(2,1)S(1)}, bf16[64,8192]{1,0:T(8,128)(2,1)}, u32[]{:S(2)}) copy-start(bf16[64,8192]{1,0:T(8,128)(2,1)} %param.19) | copy-start | bytes 3145732
  0.0 27.7 %collective-permute-start = (bf16[1024,512]{1,0:T(8,128)(2,1)}, bf16[1024,512]{1,0:T(8,128)(2,1)}, u32[]{:S(2)}, u32[]{:S(2)}) collective-permute-start(bf16[1024,512]{1,0:T(8,128)(2,1)} %refs_0_.1), channel_id=1, source_target_pairs={{0,4},{1,5},{4,8},{5,9},{8,12},{9,13},{12,14},{13,15},{14,10},{15,... | collective-permute-start | bytes 3145736 | tf_op jit(solution)/shard_map/ppermute | solution.py:386
  3.0 24.9 %collective-permute-start.1 = (bf16[1024,512]{1,0:T(8,128)(2,1)}, bf16[1024,512]{1,0:T(8,128)(2,1)}, u32[]{:S(2)}, u32[]{:S(2)}) collective-permute-start(bf16[1024,512]{1,0:T(8,128)(2,1)} %refs_0_.1), channel_id=1, source_target_pairs={{4,0},{5,1},{8,4},{9,5},{12,8},{13,9},{14,12},{15,13},{10,14},{11,... | collective-permute-start | bytes 3145736 | tf_op jit(solution)/shard_map/ppermute | solution.py:386
  3.0 32.3 %collective-permute-start.7 = (bf16[1024,512]{1,0:T(8,128)(2,1)}, bf16[1024,512]{1,0:T(8,128)(2,1)}, u32[]{:S(2)}, u32[]{:S(2)}) collective-permute-start(bf16[1024,512]{1,0:T(8,128)(2,1)} %refs_0_.1), channel_id=1, source_target_pairs={{0,1},{1,0},{2,3},{3,2},{4,5},{5,4},{6,7},{7,6},{8,9},{9,8},{10,11... | collective-permute-start | bytes 3145736 | tf_op jit(solution)/shard_map/ppermute | solution.py:338
  3.1 1.3 copy-start.3
  4.3 1.2 copy-start.4
  5.5 0.8 copy-start.7
  7.1 1.7 %collective-permute-start.2 = (f32[64,1024]{1,0:T(8,128)S(1)}, f32[64,1024]{1,0:T(8,128)S(1)}, u32[]{:S(2)}, u32[]{:S(2)}) collective-permute-start(f32[64,1024]{1,0:T(8,128)S(1)} %get-tuple-element.41), channel_id=1, source_target_pairs={{0,1},{1,0},{2,3},{3,2},{4,5},{5,4},{6,7},{7,6},{8,9},{9,8},{10,11... | collective-permute-start | bytes 786440 | tf_op jit(solution)/shard_map/ppermute | solution.py:338
  10.5 17.3 %collective-permute-start.3 = (bf16[32,1024]{1,0:T(8,128)(2,1)S(1)}, bf16[32,1024]{1,0:T(8,128)(2,1)S(1)}, u32[]{:S(2)}, u32[]{:S(2)}) collective-permute-start(bf16[32,1024]{1,0:T(8,128)(2,1)S(1)} %dynamic-slice_convert_fusion), channel_id=1, source_target_pairs={{0,2},{1,3},{2,0},{3,1},{4,6},{5,7},{6,4},{7,5},{8,10},{9,11},{10,... | collective-permute-start | bytes 196616 | tf_op jit(solution)/shard_map/ppermute | solution.py:338
  13.3 0.9 copy-start.6
  21.8 2.9 %copy-start.2 = (f32[7,1024,256]{2,1,0:T(8,128)}, f32[7,1024,256]{2,1,0:T(8,128)S(1)}, u32[]{:S(2)}) copy-start(f32[7,1024,256]{2,1,0:T(8,128)S(1)} %get-tuple-element.70.refs_5_) | copy-start | bytes 22020100
  28.0 11.5 %collective-permute-start.8 = (bf16[1024,512]{1,0:T(8,128)(2,1)}, bf16[1024,512]{1,0:T(8,128)(2,1)S(1)}, u32[]{:S(2)}, u32[]{:S(2)}) collective-permute-start(bf16[1024,512]{1,0:T(8,128)(2,1)} %collective-permute-done.refs_2_), channel_id=1, source_target_pairs={{0,1},{1,0},{2,3},{3,2},{4,5},{5,4},{6,7},{7,6},{8,9},{9,8},{10,11... | collective-permute-start | bytes 3145736 | tf_op jit(solution)/shard_map/ppermute | solution.py:338
  28.0 11.5 %collective-permute-start.9 = (bf16[1024,512]{1,0:T(8,128)(2,1)}, bf16[1024,512]{1,0:T(8,128)(2,1)}, u32[]{:S(2)}, u32[]{:S(2)}) collective-permute-start(bf16[1024,512]{1,0:T(8,128)(2,1)} %collective-permute-done.1.refs_3_), channel_id=1, source_target_pairs={{0,1},{1,0},{2,3},{3,2},{4,5},{5,4},{6,7},{7,6},{8,9},{9,8},{10,11... | collective-permute-start | bytes 3145736 | tf_op jit(solution)/shard_map/ppermute | solution.py:338
  28.5 31.6 %collective-permute-start.4 = (bf16[1024,512]{1,0:T(8,128)(2,1)}, bf16[1024,512]{1,0:T(8,128)(2,1)}, u32[]{:S(2)}, u32[]{:S(2)}) collective-permute-start(bf16[1024,512]{1,0:T(8,128)(2,1)} %collective-permute-done.refs_2_), channel_id=1, source_target_pairs={{0,4},{1,5},{4,8},{5,9},{8,12},{9,13},{12,14},{13,15},{14,10},{15,... | collective-permute-start | bytes 3145736 | tf_op jit(solution)/shard_map/ppermute | solution.py:386
  30.1 30.0 %collective-permute-start.5 = (bf16[1024,512]{1,0:T(8,128)(2,1)}, bf16[1024,512]{1,0:T(8,128)(2,1)}, u32[]{:S(2)}, u32[]{:S(2)}) collective-permute-start(bf16[1024,512]{1,0:T(8,128)(2,1)} %collective-permute-done.1.refs_3_), channel_id=1, source_target_pairs={{4,0},{5,1},{8,4},{9,5},{12,8},{13,9},{14,12},{15,13},{10,14},{11,... | collective-permute-start | bytes 3145736 | tf_op jit(solution)/shard_map/ppermute | solution.py:386
  35.3 24.7 %collective-permute-start.6 = (bf16[32,1024]{1,0:T(8,128)(2,1)S(1)}, bf16[32,1024]{1,0:T(8,128)(2,1)S(1)}, u32[]{:S(2)}, u32[]{:S(2)}) collective-permute-start(bf16[32,1024]{1,0:T(8,128)(2,1)S(1)} %fusion.3), channel_id=1, source_target_pairs={{0,8},{1,9},{2,10},{3,11},{4,12},{5,13},{6,14},{7,15},{8,0},{9,1},... | collective-permute-start | bytes 196616 | tf_op jit(solution)/shard_map/ppermute | solution.py:338
  60.0 6.6 %collective-permute-start.13 = (bf16[1024,512]{1,0:T(8,128)(2,1)}, bf16[1024,512]{1,0:T(8,128)(2,1)S(1)}, u32[]{:S(2)}, u32[]{:S(2)}) collective-permute-start(bf16[1024,512]{1,0:T(8,128)(2,1)} %collective-permute-done.4.refs_0_), channel_id=1, source_target_pairs={{0,1},{1,0},{2,3},{3,2},{4,5},{5,4},{6,7},{7,6},{8,9},{9,8},{10,11... | collective-permute-start | bytes 3145736 | tf_op jit(solution)/shard_map/ppermute | solution.py:338
  60.0 6.6 %collective-permute-start.14 = (bf16[1024,512]{1,0:T(8,128)(2,1)}, bf16[1024,512]{1,0:T(8,128)(2,1)S(1)}, u32[]{:S(2)}, u32[]{:S(2)}) collective-permute-start(bf16[1024,512]{1,0:T(8,128)(2,1)} %collective-permute-done.5.refs_1_), channel_id=1, source_target_pairs={{0,1},{1,0},{2,3},{3,2},{4,5},{5,4},{6,7},{7,6},{8,9},{9,8},{10,11... | collective-permute-start | bytes 3145736 | tf_op jit(solution)/shard_map/ppermute | solution.py:338
  60.5 26.9 %collective-permute-start.10 = (bf16[1024,512]{1,0:T(8,128)(2,1)}, bf16[1024,512]{1,0:T(8,128)(2,1)S(1)}, u32[]{:S(2)}, u32[]{:S(2)}) collective-permute-start(bf16[1024,512]{1,0:T(8,128)(2,1)} %collective-permute-done.4.refs_0_), channel_id=1, source_target_pairs={{0,4},{1,5},{4,8},{5,9},{8,12},{9,13},{12,14},{13,15},{14,10},{15,... | collective-permute-start | bytes 3145736 | tf_op jit(solution)/shard_map/ppermute | solution.py:386
  61.0 26.5 %collective-permute-start.11 = (bf16[1024,512]{1,0:T(8,128)(2,1)}, bf16[1024,512]{1,0:T(8,128)(2,1)S(1)}, u32[]{:S(2)}, u32[]{:S(2)}) collective-permute-start(bf16[1024,512]{1,0:T(8,128)(2,1)} %collective-permute-done.5.refs_1_), channel_id=1, source_target_pairs={{4,0},{5,1},{8,4},{9,5},{12,8},{13,9},{14,12},{15,13},{10,14},{11,... | collective-permute-start | bytes 3145736 | tf_op jit(solution)/shard_map/ppermute | solution.py:386
  63.5 23.9 %collective-permute-start.12 = (bf16[32,1024]{1,0:T(8,128)(2,1)S(1)}, bf16[32,1024]{1,0:T(8,128)(2,1)S(1)}, u32[]{:S(2)}, u32[]{:S(2)}) collective-permute-start(bf16[32,1024]{1,0:T(8,128)(2,1)S(1)} %fusion), channel_id=1, source_target_pairs={{0,4},{1,5},{2,6},{3,7},{4,0},{5,1},{6,2},{7,3},{8,12},{9,13},{10,... | collective-permute-start | bytes 196616 | tf_op jit(solution)/shard_map/ppermute | solution.py:338
  87.5 4.0 %collective-permute-start.15 = (bf16[1024,512]{1,0:T(8,128)(2,1)S(1)}, bf16[1024,512]{1,0:T(8,128)(2,1)S(1)}, u32[]{:S(2)}, u32[]{:S(2)}) collective-permute-start(bf16[1024,512]{1,0:T(8,128)(2,1)S(1)} %collective-permute-done.10.refs_0_), channel_id=1, source_target_pairs={{0,1},{1,0},{2,3},{3,2},{4,5},{5,4},{6,7},{7,6},{8,9},{9,8},{10,11... | collective-permute-start | bytes 3145736 | tf_op jit(solution)/shard_map/ppermute | solution.py:338
  87.5 4.2 %collective-permute-start.16 = (bf16[1024,512]{1,0:T(8,128)(2,1)S(1)}, bf16[1024,512]{1,0:T(8,128)(2,1)S(1)}, u32[]{:S(2)}, u32[]{:S(2)}) collective-permute-start(bf16[1024,512]{1,0:T(8,128)(2,1)S(1)} %collective-permute-done.11.refs_1_), channel_id=1, source_target_pairs={{0,1},{1,0},{2,3},{3,2},{4,5},{5,4},{6,7},{7,6},{8,9},{9,8},{10,11... | collective-permute-start | bytes 3145736 | tf_op jit(solution)/shard_map/ppermute | solution.py:338
  88.1 18.8 %collective-permute-start.20 = (bf16[512,512]{1,0:T(8,128)(2,1)S(1)}, bf16[512,512]{1,0:T(8,128)(2,1)S(1)}, u32[]{:S(2)}, u32[]{:S(2)}) collective-permute-start(bf16[512,512]{1,0:T(8,128)(2,1)S(1)} %slice.6), channel_id=1, source_target_pairs={{0,4},{1,5},{4,8},{5,9},{8,12},{9,13},{12,14},{13,15},{14,10},{15,... | collective-permute-start | bytes 1572872 | tf_op jit(solution)/shard_map/ppermute | solution.py:386
  88.4 18.5 %collective-permute-start.21 = (bf16[512,512]{1,0:T(8,128)(2,1)S(1)}, bf16[512,512]{1,0:T(8,128)(2,1)S(1)}, u32[]{:S(2)}, u32[]{:S(2)}) collective-permute-start(bf16[512,512]{1,0:T(8,128)(2,1)S(1)} %slice.7), channel_id=1, source_target_pairs={{4,0},{5,1},{8,4},{9,5},{12,8},{13,9},{14,12},{15,13},{10,14},{11,... | collective-permute-start | bytes 1572872 | tf_op jit(solution)/shard_map/ppermute | solution.py:386
  90.1 19.7 %slice-start = ((s8[7340032]{0:T(1024)(128)(4,1)}), s8[4194304]{0:T(1024)(128)(4,1)S(1)}, s32[]{:S(2)}) async-start(s8[7340032]{0:T(1024)(128)(4,1)} %bitcast.5), calls=%async_computation | async-start | bytes 8388608
  91.2 18.7 %slice-start.1 = ((s8[7340032]{0:T(1024)(128)(4,1)}), s8[3145728]{0:T(1024)(128)(4,1)S(1)}, s32[]{:S(2)}) async-start(s8[7340032]{0:T(1024)(128)(4,1)} %bitcast.5), calls=%async_computation.1 | async-start | bytes 6291456
  91.2 18.7 %copy-start.5 = (bf16[64,1792]{1,0:T(8,128)(2,1)S(1)}, bf16[64,1792]{1,0:T(8,128)(2,1)}, u32[]{:S(2)}) copy-start(bf16[64,1792]{1,0:T(8,128)(2,1)} %refs_6_.7) | copy-start | bytes 688132
  91.2 14.4 %collective-permute-start.17 = (f32[32,1024]{1,0:T(8,128)S(1)}, f32[32,1024]{1,0:T(8,128)S(1)}, u32[]{:S(2)}, u32[]{:S(2)}) collective-permute-start(f32[32,1024]{1,0:T(8,128)S(1)} %convert_add_fusion.3.mine_ref), channel_id=1, source_target_pairs={{0,2},{1,3},{2,0},{3,1},{4,6},{5,7},{6,4},{7,5},{8,10},{9,11},{10,... | collective-permute-start | bytes 393224 | tf_op jit(solution)/shard_map/ppermute | solution.py:338
  91.5 14.2 %collective-permute-start.18 = (f32[32,1024]{1,0:T(8,128)S(1)}, f32[32,1024]{1,0:T(8,128)S(1)}, u32[]{:S(2)}, u32[]{:S(2)}) collective-permute-start(f32[32,1024]{1,0:T(8,128)S(1)} %convert_add_fusion.3.mine_ref), channel_id=1, source_target_pairs={{0,1},{1,0},{2,3},{3,2},{4,5},{5,4},{6,7},{7,6},{8,9},{9,8},{10,11... | collective-permute-start | bytes 393224 | tf_op jit(solution)/shard_map/ppermute | solution.py:338
  91.6 15.3 %collective-permute-start.19 = (f32[32,1024]{1,0:T(8,128)S(1)}, f32[32,1024]{1,0:T(8,128)S(1)}, u32[]{:S(2)}, u32[]{:S(2)}) collective-permute-start(f32[32,1024]{1,0:T(8,128)S(1)} %convert_add_fusion.3.mine_ref), channel_id=1, source_target_pairs={{0,3},{1,2},{2,1},{3,0},{4,7},{5,6},{6,5},{7,4},{8,11},{9,10},{10,... | collective-permute-start | bytes 393224 | tf_op jit(solution)/shard_map/ppermute | solution.py:338
  106.9 3.0 %collective-permute-start.22 = (bf16[512,512]{1,0:T(8,128)(2,1)S(1)}, bf16[512,512]{1,0:T(8,128)(2,1)S(1)}, u32[]{:S(2)}, u32[]{:S(2)}) collective-permute-start(bf16[512,512]{1,0:T(8,128)(2,1)S(1)} %collective-permute-done.20.refs_0_), channel_id=1, source_target_pairs={{0,1},{1,0},{2,3},{3,2},{4,5},{5,4},{6,7},{7,6},{8,9},{9,8},{10,11... | collective-permute-start | bytes 1572872 | tf_op jit(solution)/shard_map/ppermute | solution.py:338
  107.5 2.4 %collective-permute-start.23 = (bf16[512,512]{1,0:T(8,128)(2,1)S(1)}, bf16[512,512]{1,0:T(8,128)(2,1)S(1)}, u32[]{:S(2)}, u32[]{:S(2)}) collective-permute-start(bf16[512,512]{1,0:T(8,128)(2,1)S(1)} %collective-permute-done.21.refs_2_), channel_id=1, source_target_pairs={{0,1},{1,0},{2,3},{3,2},{4,5},{5,4},{6,7},{7,6},{8,9},{9,8},{10,11... | collective-permute-start | bytes 1572872 | tf_op jit(solution)/shard_map/ppermute | solution.py:338
  109.9 25.4 %copy-start.1 = (bf16[64,8192]{1,0:T(8,128)(2,1)S(1)}, bf16[64,8192]{1,0:T(8,128)(2,1)}, u32[]{:S(2)}) copy-start(bf16[64,8192]{1,0:T(8,128)(2,1)} %param.19) | copy-start | bytes 3145732
  117.2 1.5 %collective-permute-start.24 = (f32[8,4096]{1,0:T(8,128)S(1)}, f32[8,4096]{1,0:T(8,128)S(1)}, u32[]{:S(2)}, u32[]{:S(2)}) collective-permute-start(f32[8,4096]{1,0:T(8,128)S(1)} %broadcast_select_fusion.2), channel_id=1, source_target_pairs={{0,1},{1,0},{2,3},{3,2},{4,5},{5,4},{6,7},{7,6},{8,9},{9,8},{10,11... | collective-permute-start | bytes 393224 | tf_op jit(solution)/shard_map/ppermute | solution.py:338
  118.7 4.4 %collective-permute-start.25 = (bf16[8,4096]{1,0:T(8,128)(2,1)S(1)}, bf16[8,4096]{1,0:T(8,128)(2,1)S(1)}, u32[]{:S(2)}, u32[]{:S(2)}) collective-permute-start(bf16[8,4096]{1,0:T(8,128)(2,1)S(1)} %get-tuple-element.75), channel_id=1, source_target_pairs={{0,2},{1,3},{2,0},{3,1},{4,6},{5,7},{6,4},{7,5},{8,10},{9,11},{10,... | collective-permute-start | bytes 196616 | tf_op jit(solution)/shard_map/ppermute | solution.py:338
  123.1 4.3 %collective-permute-start.26 = (bf16[8,4096]{1,0:T(8,128)(2,1)S(1)}, bf16[8,4096]{1,0:T(8,128)(2,1)S(1)}, u32[]{:S(2)}, u32[]{:S(2)}) collective-permute-start(bf16[8,4096]{1,0:T(8,128)(2,1)S(1)} %fusion.1), channel_id=1, source_target_pairs={{0,4},{1,5},{2,6},{3,7},{4,0},{5,1},{6,2},{7,3},{8,12},{9,13},{10,... | collective-permute-start | bytes 196616 | tf_op jit(solution)/shard_map/ppermute | solution.py:338
  127.5 5.4 %collective-permute-start.27 = (bf16[8,4096]{1,0:T(8,128)(2,1)S(1)}, bf16[8,4096]{1,0:T(8,128)(2,1)S(1)}, u32[]{:S(2)}, u32[]{:S(2)}) collective-permute-start(bf16[8,4096]{1,0:T(8,128)(2,1)S(1)} %fusion.2), channel_id=1, source_target_pairs={{0,8},{1,9},{2,10},{3,11},{4,12},{5,13},{6,14},{7,15},{8,0},{9,1},... | collective-permute-start | bytes 196616 | tf_op jit(solution)/shard_map/ppermute | solution.py:338
  132.9 1.4 %collective-permute-start.28 = (f32[8,4096]{1,0:T(8,128)S(1)}, f32[8,4096]{1,0:T(8,128)S(1)}, u32[]{:S(2)}, u32[]{:S(2)}) collective-permute-start(f32[8,4096]{1,0:T(8,128)S(1)} %convert_add_fusion), channel_id=1, source_target_pairs={{0,1},{1,0},{2,3},{3,2},{4,5},{5,4},{6,7},{7,6},{8,9},{9,8},{10,11... | collective-permute-start | bytes 393224 | tf_op jit(solution)/shard_map/ppermute | solution.py:338

commit v5 on v4

--- a/solution.py
+++ b/solution.py
@@ -307,7 +307,7 @@
     first, near = place_ref[0] == 0, place_ref[1] == 0
     rows = []
     for mine, across in ((mine_ref, across_ref), (mine1_ref, across1_ref)):
-        mine, across = mine[...], across[...]
+        mine, across = mine[...], across[...].astype(F32)
         rows.append((jnp.where(near, mine, across), jnp.where(near, across, mine)))
     (a0, b0), (a1, b1) = rows
     a_up = jnp.concatenate([jnp.where(first, a0, a1), jnp.where(first, a1, a0)], axis=0)
@@ -427,14 +427,14 @@
         theirs_of = [swap(array, 1, devices) for array in came]
         units += [(array, place + 2 * i) for i, array in enumerate(came)]
         units += [(array, place + 2 * i + 1) for i, array in enumerate(theirs_of)]
-        if step == far - 3:
+        if step == far - 2:
             q_turned = turned(queries, kos)
-            src, q_turned = pin((src, q_turned))
-        if step == far - 2:
             columns = columns_of(src, down_weight, depth, (devices - 2, devices - 1))
-            src, columns = pin((src, columns))
+            src, columns, q_turned = pin((src, columns, q_turned))
         if step == far - 1:
-            quarters = [part] + [swap(part, bit, devices) for bit in (2, 1, 3)]
+            near = [part, swap(part, 1, devices)]
+            beyond = [swap(part.astype(BF16), bit, devices) for bit in (2, 3)]
+            quarters = [near[0], beyond[0], near[1], beyond[1]]
             known = add_step(src, units, down_weight, known)
             known, quarters = pin((known, quarters))
             high, low, down = pair_parts(

time: 136 us -> 134 us (0.985)
  other arithmetic: 5.3 us -> 2.65 us
  waiting for transfers between devices: 30 us -> 31.9 us
    ppermute x21, waiting for transfers between devices: 29.8 us -> 31.8 us  [swap(): return lax.ppermute(value, 'tensor', [(i, i ^ bit) for i in range(devices)])]
    unnamed x20 -> x24, local copies, waits for them, and re-layouts: 7.17 us -> 7.18 us
  transfers between devices with their start and end apart: 29 -> 29, of which waited for: 13 -> 12; matrix products, arithmetic and copies ran while one was open for 5% -> 3% of each run, Pallas kernels for 44% -> 45%
where the time goes in v5:
time: 134 us; the launch traced here: 133 us
  Pallas kernels  67.7 us (51%)
  waiting for transfers between devices  31.9 us (24%)
  starting transfers between devices  22.2 us (17%)
  local copies, waits for them, and re-layouts  8.14 us (6%)
  other arithmetic  2.65 us (2%)
    pallas_call x3, Pallas kernels, add_step(): pl.pallas_call(functools.partial(step_kernel, len(units)), grid_spec=pltp...  42.3 us
    ppermute x21, waiting for transfers between devices, swap(): return lax.ppermute(value, 'tensor', [(i, i ^ bit) for i in range(devices)])  31.8 us
    ppermute x21, starting transfers between devices, swap(): return lax.ppermute(value, 'tensor', [(i, i ^ bit) for i in range(devices)])  13.1 us
    pallas_call x1, Pallas kernels, own_parts(): pl.pallas_call(own_kernel, grid=(units // tile,), in_specs=[tiles, tiles,...  7.61 us
    pallas_call x1, Pallas kernels, last_step(): pl.pallas_call(last_kernel, in_specs=[ANYWHERE] * 4 + [WHOLE] * len(ins),...  7.21 us
    unnamed x24, local copies, waits for them, and re-layouts  7.18 us
    ppermute x4, starting transfers between devices, send(): lax.ppermute(forward, 'tensor', ahead)  5.16 us
    ppermute x4, starting transfers between devices, send(): lax.ppermute(backward, 'tensor', back)  4 us
  transfers between devices with their start and end apart: 29, of which 12 were waited for; matrix products, arithmetic and copies ran while one was open for 3% of the time, Pallas kernels for 45%

profile of v5, /device:TPU:0, one launch (start us, length us, event | category | flops | bytes accessed | tf_op | source)
XLA Modules:
  0.0 133.0 jit_solution(2643858190108439868)
XLA Ops:
  0.0 3.0 %collective-permute-start = (bf16[1024,512]{1,0:T(8,128)(2,1)}, bf16[1024,512]{1,0:T(8,128)(2,1)S(1)}, u32[]{:S(2)}, u32[]{:S(2)}) collective-permute-start(bf16[1024,512]{1,0:T(8,128)(2,1)} %refs_0_.1), channel_id=1, source_target_pairs={{0,4},{1,5},{4,8},{5,9},{8,12},{9,13},{12,14},{13,15},{14,10},{15,... | collective-permute-start | bytes 3145736 | tf_op jit(solution)/shard_map/ppermute | solution.py:386
  3.0 0.0 collective-permute-start.1
  3.0 0.0 collective-permute-start.7
  3.1 0.0 copy-start.3
  3.1 1.3 copy-done.3
  4.3 1.2 copy-done.4
  5.5 0.8 copy-done.7
  6.4 0.7 shard_map.127
  7.1 0.5 collective-permute-start.2
  7.7 0.7 add_convert_fusion
  8.3 0.1 broadcast_in_dim.39
  8.4 0.1 copy.16
  8.5 0.3 collective-permute-done.2
  8.9 2.0 %collective-permute-start.3 = (bf16[32,1024]{1,0:T(8,128)(2,1)S(1)}, bf16[32,1024]{1,0:T(8,128)(2,1)S(1)}, u32[]{:S(2)}, u32[]{:S(2)}) collective-permute-start(bf16[32,1024]{1,0:T(8,128)(2,1)S(1)} %dynamic-slice_convert_fusion), channel_id=1, source_target_pairs={{0,2},{1,3},{2,0},{3,1},{4,6},{5,7},{6,4},{7,5},{8,10},{9,11},{10,... | collective-permute-start | bytes 196616 | tf_op jit(solution)/shard_map/ppermute | solution.py:338
  10.9 0.8 select_reduce_fusion.weight_ref
  11.7 0.9 copy-done.6
  12.6 7.6 %shard_map.128 = (f32[7,1024,256]{2,1,0:T(8,128)S(1)}, f32[64,1024]{1,0:T(8,128)S(1)}) custom-call(bf16[1024,1792]{1,0:T(8,128)(2,1)} %gate_ref, bf16[1024,1792]{1,0:T(8,128)(2,1)} %up_ref, bf16[64,1792]{1,0:T(8,128)(2,1)S(1)} %copy-done.6), custom_call_target="tpu_custom_call" | custom-call | flops 1000 | bytes 1000 | tf_op jit(solution)/shard_map/pallas_call | solution.py:216
  20.3 2.9 %copy-done.2 = f32[7,1024,256]{2,1,0:T(8,128)} copy-done((f32[7,1024,256]{2,1,0:T(8,128)}, f32[7,1024,256]{2,1,0:T(8,128)S(1)}, u32[]{:S(2)}) %copy-start.2) | copy-done | bytes 7340056
  23.2 4.6 %collective-permute-done.3 = bf16[32,1024]{1,0:T(8,128)(2,1)S(1)} collective-permute-done((bf16[32,1024]{1,0:T(8,128)(2,1)S(1)}, bf16[32,1024]{1,0:T(8,128)(2,1)S(1)}, u32[]{:S(2)}, u32[]{:S(2)}) %collective-permute-start.3) | collective-permute-done | bytes 65568 | tf_op jit(solution)/shard_map/ppermute | solution.py:338
  27.7 0.1 collective-permute-done.1.refs_3_
  27.9 0.0 collective-permute-start.8
  27.9 0.5 collective-permute-start.9
  28.4 1.6 %collective-permute-start.4 = (bf16[1024,512]{1,0:T(8,128)(2,1)S(1)}, bf16[1024,512]{1,0:T(8,128)(2,1)S(1)}, u32[]{:S(2)}, u32[]{:S(2)}) collective-permute-start(bf16[1024,512]{1,0:T(8,128)(2,1)S(1)} %collective-permute-done.refs_2_), channel_id=1, source_target_pairs={{0,4},{1,5},{4,8},{5,9},{8,12},{9,13},{12,14},{13,15},{14,10},{15,... | collective-permute-start | bytes 3145736 | tf_op jit(solution)/shard_map/ppermute | solution.py:386
  29.9 0.4 collective-permute-start.5
  30.4 0.9 fusion.3
  31.3 3.6 %collective-permute-start.6 = (bf16[32,1024]{1,0:T(8,128)(2,1)S(1)}, bf16[32,1024]{1,0:T(8,128)(2,1)S(1)}, u32[]{:S(2)}, u32[]{:S(2)}) collective-permute-start(bf16[32,1024]{1,0:T(8,128)(2,1)S(1)} %fusion.3), channel_id=1, source_target_pairs={{0,8},{1,9},{2,10},{3,11},{4,12},{5,13},{6,14},{7,15},{8,0},{9,1},... | collective-permute-start | bytes 196616 | tf_op jit(solution)/shard_map/ppermute | solution.py:338
  34.9 0.7 fusion.4.src_ref
  35.6 17.5 %shard_map.131.refs_8_ = f32[7,1024,256]{2,1,0:T(8,128)S(1)} custom-call(s32[16]{0:T(128)S(1)} %fusion.4.src_ref, bf16[1024,512]{1,0:T(8,128)(2,1)} %refs_0_.1, bf16[1024,512]{1,0:T(8,128)(2,1)} %collective-permute-done.7.refs_1_, bf16[1024,512]{1,0:T(8,128)(2,1)S(1)} %collective-permute-done.refs_2_, bf16[1024,512]{1,0:T(8,128)(2,1)S(1)} %collective-permute-done.1.refs_3_, ...), custom_call_target="tpu_custom_call" | custom-call | flops 1000 | bytes 1000 | tf_op jit(solution)/shard_map/pallas_call | solution.py:109
  53.2 6.7 %collective-permute-done.6 = bf16[32,1024]{1,0:T(8,128)(2,1)S(1)} collective-permute-done((bf16[32,1024]{1,0:T(8,128)(2,1)S(1)}, bf16[32,1024]{1,0:T(8,128)(2,1)S(1)}, u32[]{:S(2)}, u32[]{:S(2)}) %collective-permute-start.6) | collective-permute-done | bytes 65568 | tf_op jit(solution)/shard_map/ppermute | solution.py:338
  59.8 0.5 collective-permute-start.14
  60.3 0.4 collective-permute-start.10
  60.8 1.6 %collective-permute-start.11 = (bf16[1024,512]{1,0:T(8,128)(2,1)}, bf16[1024,512]{1,0:T(8,128)(2,1)S(1)}, u32[]{:S(2)}, u32[]{:S(2)}) collective-permute-start(bf16[1024,512]{1,0:T(8,128)(2,1)} %collective-permute-done.5.refs_1_), channel_id=1, source_target_pairs={{4,0},{5,1},{8,4},{9,5},{12,8},{13,9},{14,12},{15,13},{10,14},{11,... | collective-permute-start | bytes 3145736 | tf_op jit(solution)/shard_map/ppermute | solution.py:386
  62.4 0.5 collective-permute-start.12
  62.9 2.6 %shard_map.129.refs_4_ = bf16[2,1792,512]{2,1,0:T(8,128)(2,1)S(1)} custom-call(s32[16]{0:T(128)S(1)} %fusion.4.src_ref, bf16[1792,8192]{1,0:T(8,128)(2,1)} %refs_7_.5), custom_call_target="tpu_custom_call" | custom-call | flops 1000 | bytes 1000 | tf_op jit(solution)/shard_map/pallas_call | solution.py:140
  65.5 3.9 %shard_map.130.q_ref = bf16[8192,64]{1,0:T(8,128)(2,1)S(1)} custom-call(bf16[64,8192]{1,0:T(8,128)(2,1)} %q_ref.1), custom_call_target="tpu_custom_call" | custom-call | flops 1000 | bytes 1000 | tf_op jit(solution)/shard_map/pallas_call | solution.py:240
  69.4 12.9 %shard_map.132.refs_8_ = f32[7,1024,256]{2,1,0:T(8,128)S(1)} custom-call(s32[16]{0:T(128)S(1)} %fusion.4.src_ref, bf16[1024,512]{1,0:T(8,128)(2,1)S(1)} %collective-permute-done.4.refs_0_, bf16[1024,512]{1,0:T(8,128)(2,1)} %collective-permute-done.5.refs_1_, bf16[1024,512]{1,0:T(8,128)(2,1)S(1)} %collective-permute-done.13.refs_2_, ...), custom_call_target="tpu_custom_call", output_to_operand_aliasing={{}: (9, {})} | custom-call | flops 1000 | bytes 1000 | tf_op jit(solution)/shard_map/pallas_call | solution.py:109
  82.4 4.9 %collective-permute-done.12 = bf16[32,1024]{1,0:T(8,128)(2,1)S(1)} collective-permute-done((bf16[32,1024]{1,0:T(8,128)(2,1)S(1)}, bf16[32,1024]{1,0:T(8,128)(2,1)S(1)}, u32[]{:S(2)}, u32[]{:S(2)}) %collective-permute-start.12) | collective-permute-done | bytes 65568 | tf_op jit(solution)/shard_map/ppermute | solution.py:338
  87.3 0.5 collective-permute-start.16
  87.9 0.1 collective-permute-start.20
  88.0 2.0 %collective-permute-start.21 = (bf16[512,512]{1,0:T(8,128)(2,1)S(1)}, bf16[512,512]{1,0:T(8,128)(2,1)S(1)}, u32[]{:S(2)}, u32[]{:S(2)}) collective-permute-start(bf16[512,512]{1,0:T(8,128)(2,1)S(1)} %slice.7), channel_id=1, source_target_pairs={{4,0},{5,1},{8,4},{9,5},{12,8},{13,9},{14,12},{15,13},{10,14},{11,... | collective-permute-start | bytes 1572872 | tf_op jit(solution)/shard_map/ppermute | solution.py:386
  90.0 0.1 collective-permute-start.18
  90.1 0.0 copy-start.5
  90.1 0.2 collective-permute-start.17
  90.3 1.1 collective-permute-done.16.refs_3_
  91.4 0.6 collective-permute-start.19
  92.0 11.9 %shard_map.133.refs_7_ = f32[7,1024,256]{2,1,0:T(8,128)S(1)} custom-call(s32[16]{0:T(128)S(1)} %fusion.4.src_ref, bf16[1024,512]{1,0:T(8,128)(2,1)S(1)} %collective-permute-done.10.refs_0_, bf16[1024,512]{1,0:T(8,128)(2,1)S(1)} %collective-permute-done.11.refs_1_, ...), custom_call_target="tpu_custom_call", output_to_operand_aliasing={{}: (9, {})} | custom-call | flops 1000 | bytes 1000 | tf_op jit(solution)/shard_map/pallas_call | solution.py:109
  103.9 0.1 collective-permute-done.17.across_ref
  103.9 0.6 collective-permute-start.22
  104.5 0.1 collective-permute-start.23
  104.6 0.1 pad_add_fusion.place_ref
  104.7 2.3 %shard_map.134 = (bf16[512,1024]{1,0:T(8,128)(2,1)S(1)}, bf16[512,1024]{1,0:T(8,128)(2,1)S(1)}, f32[8,4096]{1,0:T(8,128)S(1)}) custom-call(s32[2]{0:T(128)S(1)} %pad_add_fusion.place_ref, f32[8,1024]{1,0:T(8,128)S(1)} %select_reduce_fusion.weight_ref, f32[32,1024]{1,0:T(8,128)S(1)} %get-tuple-element.58.mine_ref, ...), custom_call_target="tpu_custom_call" | custom-call | flops 1000 | bytes 1000 | tf_op jit(solution)/shard_map/pallas_call | solution.py:327
  107.0 0.0 copy-start.1
  107.0 7.2 %shard_map.135 = f32[8,4096]{1,0:T(8,128)S(1)} custom-call(bf16[512,512]{1,0:T(8,128)(2,1)S(1)} %collective-permute-done.20.refs_0_, bf16[512,512]{1,0:T(8,128)(2,1)S(1)} %collective-permute-done.22.refs_1_, bf16[512,512]{1,0:T(8,128)(2,1)S(1)} %collective-permute-done.21.refs_2_, bf16[512,512]{1,0:T(8,128)(2,1)S(1)} %collective-permute-done.23.refs_3_, ...), custom_call_target="tpu_custom_call" | custom-call | flops 1000 | bytes 1000 | tf_op jit(solution)/shard_map/pallas_call | solution.py:181
  114.3 0.5 collective-permute-start.24
  114.8 1.0 collective-permute-done.24
  115.8 1.8 %collective-permute-start.25 = (bf16[8,4096]{1,0:T(8,128)(2,1)S(1)}, bf16[8,4096]{1,0:T(8,128)(2,1)S(1)}, u32[]{:S(2)}, u32[]{:S(2)}) collective-permute-start(bf16[8,4096]{1,0:T(8,128)(2,1)S(1)} %get-tuple-element.73), channel_id=1, source_target_pairs={{0,2},{1,3},{2,0},{3,1},{4,6},{5,7},{6,4},{7,5},{8,10},{9,11},{10,... | collective-permute-start | bytes 196616 | tf_op jit(solution)/shard_map/ppermute | solution.py:338
  117.6 2.6 %collective-permute-done.25 = bf16[8,4096]{1,0:T(8,128)(2,1)S(1)} collective-permute-done((bf16[8,4096]{1,0:T(8,128)(2,1)S(1)}, bf16[8,4096]{1,0:T(8,128)(2,1)S(1)}, u32[]{:S(2)}, u32[]{:S(2)}) %collective-permute-start.25) | collective-permute-done | bytes 65568 | tf_op jit(solution)/shard_map/ppermute | solution.py:338
  120.2 0.9 collective-permute-start.26
  121.1 3.4 %collective-permute-done.26 = bf16[8,4096]{1,0:T(8,128)(2,1)S(1)} collective-permute-done((bf16[8,4096]{1,0:T(8,128)(2,1)S(1)}, bf16[8,4096]{1,0:T(8,128)(2,1)S(1)}, u32[]{:S(2)}, u32[]{:S(2)}) %collective-permute-start.26) | collective-permute-done | bytes 65568 | tf_op jit(solution)/shard_map/ppermute | solution.py:338
  124.6 0.1 collective-permute-start.27
  124.7 5.9 %collective-permute-done.27 = bf16[8,4096]{1,0:T(8,128)(2,1)S(1)} collective-permute-done((bf16[8,4096]{1,0:T(8,128)(2,1)S(1)}, bf16[8,4096]{1,0:T(8,128)(2,1)S(1)}, u32[]{:S(2)}, u32[]{:S(2)}) %collective-permute-start.27) | collective-permute-done | bytes 65568 | tf_op jit(solution)/shard_map/ppermute | solution.py:338
  130.5 0.1 collective-permute-start.28
  130.6 1.3 %collective-permute-done.28 = f32[8,4096]{1,0:T(8,128)S(1)} collective-permute-done((f32[8,4096]{1,0:T(8,128)S(1)}, f32[8,4096]{1,0:T(8,128)S(1)}, u32[]{:S(2)}, u32[]{:S(2)}) %collective-permute-start.28) | collective-permute-done | bytes 131104 | tf_op jit(solution)/shard_map/ppermute | solution.py:338
  132.0 1.0 shard_map.136
  (50 shorter events, 0.4 us)
Async XLA Ops:
  0.0 3.0 %copy-start = (bf16[64,8192]{1,0:T(8,128)(2,1)S(1)}, bf16[64,8192]{1,0:T(8,128)(2,1)}, u32[]{:S(2)}) copy-start(bf16[64,8192]{1,0:T(8,128)(2,1)} %param.19) | copy-start | bytes 3145732
  0.0 27.7 %collective-permute-start = (bf16[1024,512]{1,0:T(8,128)(2,1)}, bf16[1024,512]{1,0:T(8,128)(2,1)S(1)}, u32[]{:S(2)}, u32[]{:S(2)}) collective-permute-start(bf16[1024,512]{1,0:T(8,128)(2,1)} %refs_0_.1), channel_id=1, source_target_pairs={{0,4},{1,5},{4,8},{5,9},{8,12},{9,13},{12,14},{13,15},{14,10},{15,... | collective-permute-start | bytes 3145736 | tf_op jit(solution)/shard_map/ppermute | solution.py:386
  3.0 24.8 %collective-permute-start.1 = (bf16[1024,512]{1,0:T(8,128)(2,1)}, bf16[1024,512]{1,0:T(8,128)(2,1)S(1)}, u32[]{:S(2)}, u32[]{:S(2)}) collective-permute-start(bf16[1024,512]{1,0:T(8,128)(2,1)} %refs_0_.1), channel_id=1, source_target_pairs={{4,0},{5,1},{8,4},{9,5},{12,8},{13,9},{14,12},{15,13},{10,14},{11,... | collective-permute-start | bytes 3145736 | tf_op jit(solution)/shard_map/ppermute | solution.py:386
  3.0 28.3 %collective-permute-start.7 = (bf16[1024,512]{1,0:T(8,128)(2,1)}, bf16[1024,512]{1,0:T(8,128)(2,1)}, u32[]{:S(2)}, u32[]{:S(2)}) collective-permute-start(bf16[1024,512]{1,0:T(8,128)(2,1)} %refs_0_.1), channel_id=1, source_target_pairs={{0,1},{1,0},{2,3},{3,2},{4,5},{5,4},{6,7},{7,6},{8,9},{9,8},{10,11... | collective-permute-start | bytes 3145736 | tf_op jit(solution)/shard_map/ppermute | solution.py:338
  3.1 1.3 copy-start.3
  4.3 1.2 copy-start.4
  5.5 0.8 copy-start.7
  7.1 1.7 %collective-permute-start.2 = (f32[64,1024]{1,0:T(8,128)S(1)}, f32[64,1024]{1,0:T(8,128)S(1)}, u32[]{:S(2)}, u32[]{:S(2)}) collective-permute-start(f32[64,1024]{1,0:T(8,128)S(1)} %get-tuple-element.40), channel_id=1, source_target_pairs={{0,1},{1,0},{2,3},{3,2},{4,5},{5,4},{6,7},{7,6},{8,9},{9,8},{10,11... | collective-permute-start | bytes 786440 | tf_op jit(solution)/shard_map/ppermute | solution.py:338
  8.9 19.0 %copy-start.8 = (f32[64,1024]{1,0:T(8,128)}, f32[64,1024]{1,0:T(8,128)S(1)}, u32[]{:S(2)}) copy-start(f32[64,1024]{1,0:T(8,128)S(1)} %add.54) | copy-start | bytes 786436
  8.9 18.8 %collective-permute-start.3 = (bf16[32,1024]{1,0:T(8,128)(2,1)S(1)}, bf16[32,1024]{1,0:T(8,128)(2,1)S(1)}, u32[]{:S(2)}, u32[]{:S(2)}) collective-permute-start(bf16[32,1024]{1,0:T(8,128)(2,1)S(1)} %dynamic-slice_convert_fusion), channel_id=1, source_target_pairs={{0,2},{1,3},{2,0},{3,1},{4,6},{5,7},{6,4},{7,5},{8,10},{9,11},{10,... | collective-permute-start | bytes 196616 | tf_op jit(solution)/shard_map/ppermute | solution.py:338
  11.7 0.9 copy-start.6
  20.3 2.9 %copy-start.2 = (f32[7,1024,256]{2,1,0:T(8,128)}, f32[7,1024,256]{2,1,0:T(8,128)S(1)}, u32[]{:S(2)}) copy-start(f32[7,1024,256]{2,1,0:T(8,128)S(1)} %get-tuple-element.68.refs_5_) | copy-start | bytes 22020100
  27.9 7.7 %collective-permute-start.8 = (bf16[1024,512]{1,0:T(8,128)(2,1)S(1)}, bf16[1024,512]{1,0:T(8,128)(2,1)}, u32[]{:S(2)}, u32[]{:S(2)}) collective-permute-start(bf16[1024,512]{1,0:T(8,128)(2,1)S(1)} %collective-permute-done.refs_2_), channel_id=1, source_target_pairs={{0,1},{1,0},{2,3},{3,2},{4,5},{5,4},{6,7},{7,6},{8,9},{9,8},{10,11... | collective-permute-start | bytes 3145736 | tf_op jit(solution)/shard_map/ppermute | solution.py:338
  27.9 7.7 %collective-permute-start.9 = (bf16[1024,512]{1,0:T(8,128)(2,1)S(1)}, bf16[1024,512]{1,0:T(8,128)(2,1)}, u32[]{:S(2)}, u32[]{:S(2)}) collective-permute-start(bf16[1024,512]{1,0:T(8,128)(2,1)S(1)} %collective-permute-done.1.refs_3_), channel_id=1, source_target_pairs={{0,1},{1,0},{2,3},{3,2},{4,5},{5,4},{6,7},{7,6},{8,9},{9,8},{10,11... | collective-permute-start | bytes 3145736 | tf_op jit(solution)/shard_map/ppermute | solution.py:338
  28.4 31.5 %collective-permute-start.4 = (bf16[1024,512]{1,0:T(8,128)(2,1)S(1)}, bf16[1024,512]{1,0:T(8,128)(2,1)S(1)}, u32[]{:S(2)}, u32[]{:S(2)}) collective-permute-start(bf16[1024,512]{1,0:T(8,128)(2,1)S(1)} %collective-permute-done.refs_2_), channel_id=1, source_target_pairs={{0,4},{1,5},{4,8},{5,9},{8,12},{9,13},{12,14},{13,15},{14,10},{15,... | collective-permute-start | bytes 3145736 | tf_op jit(solution)/shard_map/ppermute | solution.py:386
  29.9 29.9 %collective-permute-start.5 = (bf16[1024,512]{1,0:T(8,128)(2,1)S(1)}, bf16[1024,512]{1,0:T(8,128)(2,1)}, u32[]{:S(2)}, u32[]{:S(2)}) collective-permute-start(bf16[1024,512]{1,0:T(8,128)(2,1)S(1)} %collective-permute-done.1.refs_3_), channel_id=1, source_target_pairs={{4,0},{5,1},{8,4},{9,5},{12,8},{13,9},{14,12},{15,13},{10,14},{11,... | collective-permute-start | bytes 3145736 | tf_op jit(solution)/shard_map/ppermute | solution.py:386
  31.3 28.5 %collective-permute-start.6 = (bf16[32,1024]{1,0:T(8,128)(2,1)S(1)}, bf16[32,1024]{1,0:T(8,128)(2,1)S(1)}, u32[]{:S(2)}, u32[]{:S(2)}) collective-permute-start(bf16[32,1024]{1,0:T(8,128)(2,1)S(1)} %fusion.3), channel_id=1, source_target_pairs={{0,8},{1,9},{2,10},{3,11},{4,12},{5,13},{6,14},{7,15},{8,0},{9,1},... | collective-permute-start | bytes 196616 | tf_op jit(solution)/shard_map/ppermute | solution.py:338
  35.6 26.8 %copy-start.9 = (f32[64,1024]{1,0:T(8,128)S(1)}, f32[64,1024]{1,0:T(8,128)}, u32[]{:S(2)}) copy-start(f32[64,1024]{1,0:T(8,128)} %copy-done.8) | copy-start | bytes 786436
  59.8 9.6 %collective-permute-start.13 = (bf16[1024,512]{1,0:T(8,128)(2,1)S(1)}, bf16[1024,512]{1,0:T(8,128)(2,1)S(1)}, u32[]{:S(2)}, u32[]{:S(2)}) collective-permute-start(bf16[1024,512]{1,0:T(8,128)(2,1)S(1)} %collective-permute-done.4.refs_0_), channel_id=1, source_target_pairs={{0,1},{1,0},{2,3},{3,2},{4,5},{5,4},{6,7},{7,6},{8,9},{9,8},{10,11... | collective-permute-start | bytes 3145736 | tf_op jit(solution)/shard_map/ppermute | solution.py:338
  59.8 9.6 %collective-permute-start.14 = (bf16[1024,512]{1,0:T(8,128)(2,1)}, bf16[1024,512]{1,0:T(8,128)(2,1)S(1)}, u32[]{:S(2)}, u32[]{:S(2)}) collective-permute-start(bf16[1024,512]{1,0:T(8,128)(2,1)} %collective-permute-done.5.refs_1_), channel_id=1, source_target_pairs={{0,1},{1,0},{2,3},{3,2},{4,5},{5,4},{6,7},{7,6},{8,9},{9,8},{10,11... | collective-permute-start | bytes 3145736 | tf_op jit(solution)/shard_map/ppermute | solution.py:338
  60.3 26.9 %collective-permute-start.10 = (bf16[1024,512]{1,0:T(8,128)(2,1)S(1)}, bf16[1024,512]{1,0:T(8,128)(2,1)S(1)}, u32[]{:S(2)}, u32[]{:S(2)}) collective-permute-start(bf16[1024,512]{1,0:T(8,128)(2,1)S(1)} %collective-permute-done.4.refs_0_), channel_id=1, source_target_pairs={{0,4},{1,5},{4,8},{5,9},{8,12},{9,13},{12,14},{13,15},{14,10},{15,... | collective-permute-start | bytes 3145736 | tf_op jit(solution)/shard_map/ppermute | solution.py:386
  60.8 26.5 %collective-permute-start.11 = (bf16[1024,512]{1,0:T(8,128)(2,1)}, bf16[1024,512]{1,0:T(8,128)(2,1)S(1)}, u32[]{:S(2)}, u32[]{:S(2)}) collective-permute-start(bf16[1024,512]{1,0:T(8,128)(2,1)} %collective-permute-done.5.refs_1_), channel_id=1, source_target_pairs={{4,0},{5,1},{8,4},{9,5},{12,8},{13,9},{14,12},{15,13},{10,14},{11,... | collective-permute-start | bytes 3145736 | tf_op jit(solution)/shard_map/ppermute | solution.py:386
  62.4 24.9 %collective-permute-start.12 = (bf16[32,1024]{1,0:T(8,128)(2,1)S(1)}, bf16[32,1024]{1,0:T(8,128)(2,1)S(1)}, u32[]{:S(2)}, u32[]{:S(2)}) collective-permute-start(bf16[32,1024]{1,0:T(8,128)(2,1)S(1)} %fusion), channel_id=1, source_target_pairs={{0,4},{1,5},{2,6},{3,7},{4,0},{5,1},{6,2},{7,3},{8,12},{9,13},{10,... | collective-permute-start | bytes 196616 | tf_op jit(solution)/shard_map/ppermute | solution.py:338
  87.3 2.8 %collective-permute-start.15 = (bf16[1024,512]{1,0:T(8,128)(2,1)S(1)}, bf16[1024,512]{1,0:T(8,128)(2,1)S(1)}, u32[]{:S(2)}, u32[]{:S(2)}) collective-permute-start(bf16[1024,512]{1,0:T(8,128)(2,1)S(1)} %collective-permute-done.10.refs_0_), channel_id=1, source_target_pairs={{0,1},{1,0},{2,3},{3,2},{4,5},{5,4},{6,7},{7,6},{8,9},{9,8},{10,11... | collective-permute-start | bytes 3145736 | tf_op jit(solution)/shard_map/ppermute | solution.py:338
  87.3 4.2 %collective-permute-start.16 = (bf16[1024,512]{1,0:T(8,128)(2,1)S(1)}, bf16[1024,512]{1,0:T(8,128)(2,1)S(1)}, u32[]{:S(2)}, u32[]{:S(2)}) collective-permute-start(bf16[1024,512]{1,0:T(8,128)(2,1)S(1)} %collective-permute-done.11.refs_1_), channel_id=1, source_target_pairs={{0,1},{1,0},{2,3},{3,2},{4,5},{5,4},{6,7},{7,6},{8,9},{9,8},{10,11... | collective-permute-start | bytes 3145736 | tf_op jit(solution)/shard_map/ppermute | solution.py:338
  87.9 16.1 %collective-permute-start.20 = (bf16[512,512]{1,0:T(8,128)(2,1)S(1)}, bf16[512,512]{1,0:T(8,128)(2,1)S(1)}, u32[]{:S(2)}, u32[]{:S(2)}) collective-permute-start(bf16[512,512]{1,0:T(8,128)(2,1)S(1)} %slice.6), channel_id=1, source_target_pairs={{0,4},{1,5},{4,8},{5,9},{8,12},{9,13},{12,14},{13,15},{14,10},{15,... | collective-permute-start | bytes 1572872 | tf_op jit(solution)/shard_map/ppermute | solution.py:386
  88.0 16.0 %collective-permute-start.21 = (bf16[512,512]{1,0:T(8,128)(2,1)S(1)}, bf16[512,512]{1,0:T(8,128)(2,1)S(1)}, u32[]{:S(2)}, u32[]{:S(2)}) collective-permute-start(bf16[512,512]{1,0:T(8,128)(2,1)S(1)} %slice.7), channel_id=1, source_target_pairs={{4,0},{5,1},{8,4},{9,5},{12,8},{13,9},{14,12},{15,13},{10,14},{11,... | collective-permute-start | bytes 1572872 | tf_op jit(solution)/shard_map/ppermute | solution.py:386
  90.0 13.9 %collective-permute-start.18 = (f32[32,1024]{1,0:T(8,128)S(1)}, f32[32,1024]{1,0:T(8,128)S(1)}, u32[]{:S(2)}, u32[]{:S(2)}) collective-permute-start(f32[32,1024]{1,0:T(8,128)S(1)} %get-tuple-element.58.mine_ref), channel_id=1, source_target_pairs={{0,1},{1,0},{2,3},{3,2},{4,5},{5,4},{6,7},{7,6},{8,9},{9,8},{10,11... | collective-permute-start | bytes 393224 | tf_op jit(solution)/shard_map/ppermute | solution.py:338
  90.1 16.9 %slice-start = ((s8[7340032]{0:T(1024)(128)(4,1)}), s8[4194304]{0:T(1024)(128)(4,1)S(1)}, s32[]{:S(2)}) async-start(s8[7340032]{0:T(1024)(128)(4,1)} %bitcast.5), calls=%async_computation | async-start | bytes 8388608
  90.1 16.9 %slice-start.1 = ((s8[7340032]{0:T(1024)(128)(4,1)}), s8[3145728]{0:T(1024)(128)(4,1)S(1)}, s32[]{:S(2)}) async-start(s8[7340032]{0:T(1024)(128)(4,1)} %bitcast.5), calls=%async_computation.1 | async-start | bytes 6291456
  90.1 16.9 %copy-start.5 = (bf16[64,1792]{1,0:T(8,128)(2,1)S(1)}, bf16[64,1792]{1,0:T(8,128)(2,1)}, u32[]{:S(2)}) copy-start(bf16[64,1792]{1,0:T(8,128)(2,1)} %refs_6_.7) | copy-start | bytes 688132
  90.1 13.8 %collective-permute-start.17 = (bf16[32,1024]{1,0:T(8,128)(2,1)S(1)}, bf16[32,1024]{1,0:T(8,128)(2,1)S(1)}, u32[]{:S(2)}, u32[]{:S(2)}) collective-permute-start(bf16[32,1024]{1,0:T(8,128)(2,1)S(1)} %get-tuple-element.75), channel_id=1, source_target_pairs={{0,2},{1,3},{2,0},{3,1},{4,6},{5,7},{6,4},{7,5},{8,10},{9,11},{10,... | collective-permute-start | bytes 196616 | tf_op jit(solution)/shard_map/ppermute | solution.py:338
  91.4 12.5 %collective-permute-start.19 = (bf16[32,1024]{1,0:T(8,128)(2,1)S(1)}, bf16[32,1024]{1,0:T(8,128)(2,1)S(1)}, u32[]{:S(2)}, u32[]{:S(2)}) collective-permute-start(bf16[32,1024]{1,0:T(8,128)(2,1)S(1)} %get-tuple-element.75), channel_id=1, source_target_pairs={{0,3},{1,2},{2,1},{3,0},{4,7},{5,6},{6,5},{7,4},{8,11},{9,10},{10,... | collective-permute-start | bytes 196616 | tf_op jit(solution)/shard_map/ppermute | solution.py:338
  103.9 3.0 %collective-permute-start.22 = (bf16[512,512]{1,0:T(8,128)(2,1)S(1)}, bf16[512,512]{1,0:T(8,128)(2,1)S(1)}, u32[]{:S(2)}, u32[]{:S(2)}) collective-permute-start(bf16[512,512]{1,0:T(8,128)(2,1)S(1)} %collective-permute-done.20.refs_0_), channel_id=1, source_target_pairs={{0,1},{1,0},{2,3},{3,2},{4,5},{5,4},{6,7},{7,6},{8,9},{9,8},{10,11... | collective-permute-start | bytes 1572872 | tf_op jit(solution)/shard_map/ppermute | solution.py:338
  104.5 2.5 %collective-permute-start.23 = (bf16[512,512]{1,0:T(8,128)(2,1)S(1)}, bf16[512,512]{1,0:T(8,128)(2,1)S(1)}, u32[]{:S(2)}, u32[]{:S(2)}) collective-permute-start(bf16[512,512]{1,0:T(8,128)(2,1)S(1)} %collective-permute-done.21.refs_2_), channel_id=1, source_target_pairs={{0,1},{1,0},{2,3},{3,2},{4,5},{5,4},{6,7},{7,6},{8,9},{9,8},{10,11... | collective-permute-start | bytes 1572872 | tf_op jit(solution)/shard_map/ppermute | solution.py:338
  107.0 26.0 %copy-start.1 = (bf16[64,8192]{1,0:T(8,128)(2,1)S(1)}, bf16[64,8192]{1,0:T(8,128)(2,1)}, u32[]{:S(2)}) copy-start(bf16[64,8192]{1,0:T(8,128)(2,1)} %param.19) | copy-start | bytes 3145732
  114.3 1.5 %collective-permute-start.24 = (f32[8,4096]{1,0:T(8,128)S(1)}, f32[8,4096]{1,0:T(8,128)S(1)}, u32[]{:S(2)}, u32[]{:S(2)}) collective-permute-start(f32[8,4096]{1,0:T(8,128)S(1)} %broadcast_select_fusion.2), channel_id=1, source_target_pairs={{0,1},{1,0},{2,3},{3,2},{4,5},{5,4},{6,7},{7,6},{8,9},{9,8},{10,11... | collective-permute-start | bytes 393224 | tf_op jit(solution)/shard_map/ppermute | solution.py:338
  115.8 4.4 %collective-permute-start.25 = (bf16[8,4096]{1,0:T(8,128)(2,1)S(1)}, bf16[8,4096]{1,0:T(8,128)(2,1)S(1)}, u32[]{:S(2)}, u32[]{:S(2)}) collective-permute-start(bf16[8,4096]{1,0:T(8,128)(2,1)S(1)} %get-tuple-element.73), channel_id=1, source_target_pairs={{0,2},{1,3},{2,0},{3,1},{4,6},{5,7},{6,4},{7,5},{8,10},{9,11},{10,... | collective-permute-start | bytes 196616 | tf_op jit(solution)/shard_map/ppermute | solution.py:338
  120.2 4.3 %collective-permute-start.26 = (bf16[8,4096]{1,0:T(8,128)(2,1)S(1)}, bf16[8,4096]{1,0:T(8,128)(2,1)S(1)}, u32[]{:S(2)}, u32[]{:S(2)}) collective-permute-start(bf16[8,4096]{1,0:T(8,128)(2,1)S(1)} %fusion.1), channel_id=1, source_target_pairs={{0,4},{1,5},{2,6},{3,7},{4,0},{5,1},{6,2},{7,3},{8,12},{9,13},{10,... | collective-permute-start | bytes 196616 | tf_op jit(solution)/shard_map/ppermute | solution.py:338
  124.6 5.9 %collective-permute-start.27 = (bf16[8,4096]{1,0:T(8,128)(2,1)S(1)}, bf16[8,4096]{1,0:T(8,128)(2,1)S(1)}, u32[]{:S(2)}, u32[]{:S(2)}) collective-permute-start(bf16[8,4096]{1,0:T(8,128)(2,1)S(1)} %fusion.2), channel_id=1, source_target_pairs={{0,8},{1,9},{2,10},{3,11},{4,12},{5,13},{6,14},{7,15},{8,0},{9,1},... | collective-permute-start | bytes 196616 | tf_op jit(solution)/shard_map/ppermute | solution.py:338
  130.5 1.4 %collective-permute-start.28 = (f32[8,4096]{1,0:T(8,128)S(1)}, f32[8,4096]{1,0:T(8,128)S(1)}, u32[]{:S(2)}, u32[]{:S(2)}) collective-permute-start(f32[8,4096]{1,0:T(8,128)S(1)} %convert_add_fusion), channel_id=1, source_target_pairs={{0,1},{1,0},{2,3},{3,2},{4,5},{5,4},{6,7},{7,6},{8,9},{9,8},{10,11... | collective-permute-start | bytes 393224 | tf_op jit(solution)/shard_map/ppermute | solution.py:338

commit v6 on v5

--- a/solution.py
+++ b/solution.py
@@ -9,7 +9,7 @@
 from jax.sharding import PartitionSpec as P
 
 F32, BF16 = jnp.float32, jnp.bfloat16
-VMEM_LIMIT = 24 * 1024 * 1024
+VMEM_LIMIT = 14 * 1024 * 1024
 SMALL = pl.CostEstimate(flops=1000, bytes_accessed=1000, transcendentals=0)
 
 
@@ -32,7 +32,7 @@
 def products(lefts, weights):
     total = None
     for i, weight in enumerate(weights):
-        part = dot_t(lefts[i], weight[...])
+        part = dot_t(lefts[i][...], weight[...])
         total = part if total is None else total + part
     return total
 
@@ -62,6 +62,30 @@
 
     total = products(lefts, weights)
     out_ref[step] = total if before_ref is None else total + before_ref[step]
+
+
+def near_kernel(*refs):
+    blocks, weight_ref, before_ref, out_ref = refs[:4], refs[4], refs[5], refs[6]
+    tiles, _, tile = out_ref.shape
+    for i in range(tiles):
+        cols = slice(i * tile, (i + 1) * tile)
+        total = before_ref[i]
+        for m, block in enumerate(blocks):
+            total = total + dot_t(block[...], weight_ref[m, cols, :])
+        out_ref[i] = total
+
+
+def near_step(blocks, columns, before):
+    ins = [in_vmem(x) for x in (*blocks, columns, before)]
+    return pl.pallas_call(
+        near_kernel,
+        in_specs=[WHOLE] * len(ins),
+        out_specs=WHOLE,
+        out_shape=pltpu.VMEM(before.shape, F32),
+        input_output_aliases={len(ins) - 1: 0},
+        cost_estimate=SMALL,
+        compiler_params=pltpu.CompilerParams(vmem_limit_bytes=VMEM_LIMIT),
+    )(*ins)
 
 
 def projected(ups, proj_ref):
@@ -154,16 +178,15 @@
 
 def last_kernel(*refs):
     halves = refs[:4]
-    weight_ref, silu_ref, proj_ref, before_ref, high_ref, low_ref, out_ref, lefts, ups, sems = refs[4:]
-    half, tile = lefts.shape[1] // 2, ups.shape[2]
-    load([(halves[i], 0) for i in (0, 2, 1, 3)], lefts, sems)
+    weight_ref, silu_ref, proj_ref, before_ref, high_ref, low_ref, out_ref, ups = refs[4:]
+    half, tile = halves[0].shape[0], ups.shape[2]
     for i in range(ups.shape[0]):
         cols = slice(i * tile, (i + 1) * tile)
         for h in range(2):
             rows = slice(h * half, (h + 1) * half)
             grad = before_ref[i, rows, :]
-            for m in range(lefts.shape[0]):
-                grad = grad + dot_t(lefts[m, rows, :], weight_ref[m, cols, :])
+            for m in range(2):
+                grad = grad + dot_t(halves[2 * h + m][...], weight_ref[m, cols, :])
             ups[i, rows, :] = (grad * silu_ref[i, rows, :]).astype(BF16)
     b_high, b_low = parts_of(projected(ups, proj_ref))
     kos = b_high.shape[1]
@@ -176,21 +199,17 @@
 
 def last_step(halves, columns, silu, proj_up, before, up, pairs):
     tiles, tokens, tile = silu.shape
-    depth, kos = halves[0].shape[1], proj_up.shape[0]
-    ins = [in_vmem(x) for x in (columns, silu, proj_up, before, *up)]
+    kos = proj_up.shape[0]
+    ins = [in_vmem(x) for x in (*halves, columns, silu, proj_up, before, *up)]
     return pl.pallas_call(
         last_kernel,
-        in_specs=[ANYWHERE] * 4 + [WHOLE] * len(ins),
+        in_specs=[WHOLE] * len(ins),
         out_specs=WHOLE,
         out_shape=jax.ShapeDtypeStruct((pairs, up[0].shape[0] // pairs * kos), F32),
-        scratch_shapes=[
-            pltpu.VMEM((2, tokens, depth), BF16),
-            pltpu.VMEM((tiles, tokens, tile), BF16),
-            pltpu.SemaphoreType.DMA((4,)),
-        ],
-        cost_estimate=SMALL,
-        compiler_params=pltpu.CompilerParams(vmem_limit_bytes=VMEM_LIMIT),
-    )(*halves, *ins)
+        scratch_shapes=[pltpu.VMEM((tiles, tokens, tile), BF16)],
+        cost_estimate=SMALL,
+        compiler_params=pltpu.CompilerParams(vmem_limit_bytes=VMEM_LIMIT),
+    )(*ins)
 
 
 def own_kernel(gate_ref, up_ref, down_ref, silu_ref, out_ref, hidden):
@@ -429,13 +448,16 @@
         units += [(array, place + 2 * i + 1) for i, array in enumerate(theirs_of)]
         if step == far - 2:
             q_turned = turned(queries, kos)
-            columns = columns_of(src, down_weight, depth, (devices - 2, devices - 1))
+            columns = [
+                columns_of(src, down_weight, depth, places)
+                for places in ([place + i for i in (4, 6, 5, 7)], [devices - 2, devices - 1])
+            ]
             src, columns, q_turned = pin((src, columns, q_turned))
         if step == far - 1:
             near = [part, swap(part, 1, devices)]
             beyond = [swap(part.astype(BF16), bit, devices) for bit in (2, 3)]
             quarters = [near[0], beyond[0], near[1], beyond[1]]
-            known = add_step(src, units, down_weight, known)
+            known = near_step([array for array, _ in units], columns[0], known)
             known, quarters = pin((known, quarters))
             high, low, down = pair_parts(
                 jnp.stack([me % 2, side]), pair_weight, quarters, a_down
@@ -448,7 +470,7 @@
             came = (f, b)
     f, b, known = pin((f, b, known))
     halves = [x for block in (f, b) for x in (block, swap(block, 1, devices))]
-    up = last_step(halves, columns, silu_gate, out_proj_up, known, (high, low), pairs)
+    up = last_step(halves, columns[1], silu_gate, out_proj_up, known, (high, low), pairs)
 
     first = core == 0
     total = jnp.where(first, down, up) + swap(jnp.where(first, up, down), 1, devices)

time: 134 us -> 133 us (level)
    pallas_call x3 -> x2, Pallas kernels: 42.3 us -> 30.4 us  [add_step(): pl.pallas_call(functools.partial(step_kernel, len(units)), grid_spec=pltp...]
    pallas_call x1 -> x2, Pallas kernels: 7.21 us -> 14.8 us  [the longest x1 8.02 us: near_step(): pl.pallas_call(near_kernel, in_specs=[WHOLE] * len(ins), out_specs=WHOLE,...]
    pallas_call x1 -> x2, Pallas kernels: 2.63 us -> 6.4 us  [columns_of(): pl.pallas_call(functools.partial(columns_kernel, places), grid_spec=pltpu...]
where the time goes in v6:
time: 133 us; the launch traced here: 132 us
  Pallas kernels  67.1 us (50%)
  waiting for transfers between devices  32.3 us (24%)
  starting transfers between devices  21.4 us (16%)
  local copies, waits for them, and re-layouts  8.14 us (6%)
  other arithmetic  2.65 us (2%)
    ppermute x21, waiting for transfers between devices, swap(): return lax.ppermute(value, 'tensor', [(i, i ^ bit) for i in range(devices)])  32.2 us
    pallas_call x2, Pallas kernels, add_step(): pl.pallas_call(functools.partial(step_kernel, len(units)), grid_spec=pltp...  30.4 us
    ppermute x21, starting transfers between devices, swap(): return lax.ppermute(value, 'tensor', [(i, i ^ bit) for i in range(devices)])  12.2 us
    pallas_call x1, Pallas kernels, near_step(): pl.pallas_call(near_kernel, in_specs=[WHOLE] * len(ins), out_specs=WHOLE,...  8.02 us
    pallas_call x1, Pallas kernels, own_parts(): pl.pallas_call(own_kernel, grid=(units // tile,), in_specs=[tiles, tiles,...  7.61 us
    unnamed x24, local copies, waits for them, and re-layouts  7.18 us
    pallas_call x1, Pallas kernels, last_step(): pl.pallas_call(last_kernel, in_specs=[WHOLE] * len(ins), out_specs=WHOLE,...  6.77 us
    pallas_call x2, Pallas kernels, columns_of(): pl.pallas_call(functools.partial(columns_kernel, places), grid_spec=pltpu...  6.4 us
  transfers between devices with their start and end apart: 29, of which 12 were waited for; matrix products, arithmetic and copies ran while one was open for 3% of the time, Pallas kernels for 45%

profile of v6, /device:TPU:0, one launch (start us, length us, event | category | flops | bytes accessed | tf_op | source)
XLA Modules:
  0.0 132.0 jit_solution(815200648198812628)
XLA Ops:
  0.0 3.0 %collective-permute-start = (bf16[1024,512]{1,0:T(8,128)(2,1)}, bf16[1024,512]{1,0:T(8,128)(2,1)S(1)}, u32[]{:S(2)}, u32[]{:S(2)}) collective-permute-start(bf16[1024,512]{1,0:T(8,128)(2,1)} %refs_0_.1), channel_id=1, source_target_pairs={{0,4},{1,5},{4,8},{5,9},{8,12},{9,13},{12,14},{13,15},{14,10},{15,... | collective-permute-start | bytes 3145736 | tf_op jit(solution)/shard_map/ppermute | solution.py:405
  3.0 0.0 collective-permute-start.1
  3.0 0.0 collective-permute-start.7
  3.1 0.0 copy-start.3
  3.1 1.3 copy-done.3
  4.3 1.2 copy-done.4
  5.5 0.8 copy-done.7
  6.4 0.7 shard_map.127
  7.1 0.5 collective-permute-start.2
  7.7 0.7 add_convert_fusion
  8.3 0.1 broadcast_in_dim.39
  8.4 0.1 copy.16
  8.5 0.3 collective-permute-done.2
  8.9 2.0 %collective-permute-start.3 = (bf16[32,1024]{1,0:T(8,128)(2,1)S(1)}, bf16[32,1024]{1,0:T(8,128)(2,1)S(1)}, u32[]{:S(2)}, u32[]{:S(2)}) collective-permute-start(bf16[32,1024]{1,0:T(8,128)(2,1)S(1)} %dynamic-slice_convert_fusion), channel_id=1, source_target_pairs={{0,2},{1,3},{2,0},{3,1},{4,6},{5,7},{6,4},{7,5},{8,10},{9,11},{10,... | collective-permute-start | bytes 196616 | tf_op jit(solution)/shard_map/ppermute | solution.py:357
  10.9 0.8 select_reduce_fusion.weight_ref
  11.7 0.9 copy-done.6
  12.6 7.6 %shard_map.128 = (f32[7,1024,256]{2,1,0:T(8,128)S(1)}, f32[64,1024]{1,0:T(8,128)S(1)}) custom-call(bf16[1024,1792]{1,0:T(8,128)(2,1)} %gate_ref, bf16[1024,1792]{1,0:T(8,128)(2,1)} %up_ref, bf16[64,1792]{1,0:T(8,128)(2,1)S(1)} %copy-done.6), custom_call_target="tpu_custom_call" | custom-call | flops 1000 | bytes 1000 | tf_op jit(solution)/shard_map/pallas_call | solution.py:235
  20.3 2.9 %copy-done.2 = f32[7,1024,256]{2,1,0:T(8,128)} copy-done((f32[7,1024,256]{2,1,0:T(8,128)}, f32[7,1024,256]{2,1,0:T(8,128)S(1)}, u32[]{:S(2)}) %copy-start.2) | copy-done | bytes 7340056
  23.2 4.6 %collective-permute-done.3 = bf16[32,1024]{1,0:T(8,128)(2,1)S(1)} collective-permute-done((bf16[32,1024]{1,0:T(8,128)(2,1)S(1)}, bf16[32,1024]{1,0:T(8,128)(2,1)S(1)}, u32[]{:S(2)}, u32[]{:S(2)}) %collective-permute-start.3) | collective-permute-done | bytes 65568 | tf_op jit(solution)/shard_map/ppermute | solution.py:357
  27.7 0.1 collective-permute-done.1.refs_3_
  27.9 0.5 collective-permute-start.9
  28.4 1.6 %collective-permute-start.4 = (bf16[1024,512]{1,0:T(8,128)(2,1)S(1)}, bf16[1024,512]{1,0:T(8,128)(2,1)S(1)}, u32[]{:S(2)}, u32[]{:S(2)}) collective-permute-start(bf16[1024,512]{1,0:T(8,128)(2,1)S(1)} %collective-permute-done.refs_2_), channel_id=1, source_target_pairs={{0,4},{1,5},{4,8},{5,9},{8,12},{9,13},{12,14},{13,15},{14,10},{15,... | collective-permute-start | bytes 3145736 | tf_op jit(solution)/shard_map/ppermute | solution.py:405
  29.9 0.4 collective-permute-start.5
  30.4 0.9 fusion.3
  31.3 3.6 %collective-permute-start.6 = (bf16[32,1024]{1,0:T(8,128)(2,1)S(1)}, bf16[32,1024]{1,0:T(8,128)(2,1)S(1)}, u32[]{:S(2)}, u32[]{:S(2)}) collective-permute-start(bf16[32,1024]{1,0:T(8,128)(2,1)S(1)} %fusion.3), channel_id=1, source_target_pairs={{0,8},{1,9},{2,10},{3,11},{4,12},{5,13},{6,14},{7,15},{8,0},{9,1},... | collective-permute-start | bytes 196616 | tf_op jit(solution)/shard_map/ppermute | solution.py:357
  34.9 0.7 fusion.4.src_ref
  35.6 17.5 %shard_map.129.refs_8_ = f32[7,1024,256]{2,1,0:T(8,128)S(1)} custom-call(s32[16]{0:T(128)S(1)} %fusion.4.src_ref, bf16[1024,512]{1,0:T(8,128)(2,1)} %refs_0_.1, bf16[1024,512]{1,0:T(8,128)(2,1)} %collective-permute-done.7.refs_1_, bf16[1024,512]{1,0:T(8,128)(2,1)S(1)} %collective-permute-done.refs_2_, bf16[1024,512]{1,0:T(8,128)(2,1)S(1)} %collective-permute-done.1.refs_3_, ...), custom_call_target="tpu_custom_call" | custom-call | flops 1000 | bytes 1000 | tf_op jit(solution)/shard_map/pallas_call | solution.py:133
  53.2 6.7 %collective-permute-done.6 = bf16[32,1024]{1,0:T(8,128)(2,1)S(1)} collective-permute-done((bf16[32,1024]{1,0:T(8,128)(2,1)S(1)}, bf16[32,1024]{1,0:T(8,128)(2,1)S(1)}, u32[]{:S(2)}, u32[]{:S(2)}) %collective-permute-start.6) | collective-permute-done | bytes 65568 | tf_op jit(solution)/shard_map/ppermute | solution.py:357
  59.8 0.5 collective-permute-start.14
  60.3 0.4 collective-permute-start.10
  60.8 1.6 %collective-permute-start.11 = (bf16[1024,512]{1,0:T(8,128)(2,1)}, bf16[1024,512]{1,0:T(8,128)(2,1)S(1)}, u32[]{:S(2)}, u32[]{:S(2)}) collective-permute-start(bf16[1024,512]{1,0:T(8,128)(2,1)} %collective-permute-done.5.refs_1_), channel_id=1, source_target_pairs={{4,0},{5,1},{8,4},{9,5},{12,8},{13,9},{14,12},{15,13},{10,14},{11,... | collective-permute-start | bytes 3145736 | tf_op jit(solution)/shard_map/ppermute | solution.py:405
  62.4 0.5 collective-permute-start.12
  62.9 3.8 %shard_map.130.refs_4_ = bf16[4,1792,512]{2,1,0:T(8,128)(2,1)S(1)} custom-call(s32[16]{0:T(128)S(1)} %fusion.4.src_ref, bf16[1792,8192]{1,0:T(8,128)(2,1)} %refs_7_.3), custom_call_target="tpu_custom_call" | custom-call | flops 1000 | bytes 1000 | tf_op jit(solution)/shard_map/pallas_call | solution.py:164
  66.7 2.6 %shard_map.131.refs_4_ = bf16[2,1792,512]{2,1,0:T(8,128)(2,1)S(1)} custom-call(s32[16]{0:T(128)S(1)} %fusion.4.src_ref, bf16[1792,8192]{1,0:T(8,128)(2,1)} %refs_7_.3), custom_call_target="tpu_custom_call" | custom-call | flops 1000 | bytes 1000 | tf_op jit(solution)/shard_map/pallas_call | solution.py:164
  69.3 3.9 %shard_map.132.q_ref = bf16[8192,64]{1,0:T(8,128)(2,1)S(1)} custom-call(bf16[64,8192]{1,0:T(8,128)(2,1)} %q_ref.1), custom_call_target="tpu_custom_call" | custom-call | flops 1000 | bytes 1000 | tf_op jit(solution)/shard_map/pallas_call | solution.py:259
  73.2 12.9 %shard_map.133.refs_5_ = f32[7,1024,256]{2,1,0:T(8,128)S(1)} custom-call(s32[16]{0:T(128)S(1)} %fusion.4.src_ref, bf16[1024,512]{1,0:T(8,128)(2,1)S(1)} %collective-permute-done.4.refs_0_, bf16[1024,512]{1,0:T(8,128)(2,1)} %collective-permute-done.5.refs_1_, bf16[1024,512]{1,0:T(8,128)(2,1)S(1)} %collective-permute-done.13.refs_2_, ...), custom_call_target="tpu_custom_call", output_to_operand_aliasing={{}: (9, {})} | custom-call | flops 1000 | bytes 1000 | tf_op jit(solution)/shard_map/pallas_call | solution.py:133
  86.1 1.1 collective-permute-done.12
  87.3 0.5 collective-permute-start.16
  87.9 0.6 collective-permute-start.20
  88.5 1.5 %collective-permute-start.21 = (bf16[512,512]{1,0:T(8,128)(2,1)S(1)}, bf16[512,512]{1,0:T(8,128)(2,1)S(1)}, u32[]{:S(2)}, u32[]{:S(2)}) collective-permute-start(bf16[512,512]{1,0:T(8,128)(2,1)S(1)} %slice.7), channel_id=1, source_target_pairs={{4,0},{5,1},{8,4},{9,5},{12,8},{13,9},{14,12},{15,13},{10,14},{11,... | collective-permute-start | bytes 1572872 | tf_op jit(solution)/shard_map/ppermute | solution.py:405
  90.0 0.1 collective-permute-start.18
  90.1 0.0 copy-start.5
  90.1 0.2 collective-permute-start.17
  90.3 1.1 collective-permute-done.16.refs_3_
  91.4 0.6 collective-permute-start.19
  92.0 8.0 %shard_map.134.refs_7_ = f32[7,1024,256]{2,1,0:T(8,128)S(1)} custom-call(bf16[1024,512]{1,0:T(8,128)(2,1)S(1)} %collective-permute-done.10.refs_0_, bf16[1024,512]{1,0:T(8,128)(2,1)S(1)} %collective-permute-done.11.refs_1_, bf16[1024,512]{1,0:T(8,128)(2,1)S(1)} %collective-permute-done.15.refs_2_, ...), custom_call_target="tpu_custom_call", output_to_operand_aliasing={{}: (5, {})} | custom-call | flops 1000 | bytes 1000 | tf_op jit(solution)/shard_map/pallas_call | solution.py:80
  100.0 3.9 %collective-permute-done.17.across_ref = bf16[32,1024]{1,0:T(8,128)(2,1)S(1)} collective-permute-done((bf16[32,1024]{1,0:T(8,128)(2,1)S(1)}, bf16[32,1024]{1,0:T(8,128)(2,1)S(1)}, u32[]{:S(2)}, u32[]{:S(2)}) %collective-permute-start.17) | collective-permute-done | bytes 65568 | tf_op jit(solution)/shard_map/ppermute | solution.py:357
  103.9 0.6 collective-permute-start.22
  104.5 0.1 collective-permute-start.23
  104.6 0.1 pad_add_fusion.place_ref
  104.7 2.3 %shard_map.135 = (bf16[512,1024]{1,0:T(8,128)(2,1)S(1)}, bf16[512,1024]{1,0:T(8,128)(2,1)S(1)}, f32[8,4096]{1,0:T(8,128)S(1)}) custom-call(s32[2]{0:T(128)S(1)} %pad_add_fusion.place_ref, f32[8,1024]{1,0:T(8,128)S(1)} %select_reduce_fusion.weight_ref, f32[32,1024]{1,0:T(8,128)S(1)} %get-tuple-element.60.mine_ref, ...), custom_call_target="tpu_custom_call" | custom-call | flops 1000 | bytes 1000 | tf_op jit(solution)/shard_map/pallas_call | solution.py:346
  107.0 0.0 copy-start.1
  107.0 6.8 %shard_map.136 = f32[8,4096]{1,0:T(8,128)S(1)} custom-call(bf16[512,512]{1,0:T(8,128)(2,1)S(1)} %collective-permute-done.20.refs_0_, bf16[512,512]{1,0:T(8,128)(2,1)S(1)} %collective-permute-done.22.refs_1_, bf16[512,512]{1,0:T(8,128)(2,1)S(1)} %collective-permute-done.21.refs_2_, bf16[512,512]{1,0:T(8,128)(2,1)S(1)} %collective-permute-done.23.refs_3_, ...), custom_call_target="tpu_custom_call" | custom-call | flops 1000 | bytes 1000 | tf_op jit(solution)/shard_map/pallas_call | solution.py:204
  113.8 0.5 collective-permute-start.24
  114.3 1.0 collective-permute-done.24
  115.3 1.8 %collective-permute-start.25 = (bf16[8,4096]{1,0:T(8,128)(2,1)S(1)}, bf16[8,4096]{1,0:T(8,128)(2,1)S(1)}, u32[]{:S(2)}, u32[]{:S(2)}) collective-permute-start(bf16[8,4096]{1,0:T(8,128)(2,1)S(1)} %get-tuple-element.75), channel_id=1, source_target_pairs={{0,2},{1,3},{2,0},{3,1},{4,6},{5,7},{6,4},{7,5},{8,10},{9,11},{10,... | collective-permute-start | bytes 196616 | tf_op jit(solution)/shard_map/ppermute | solution.py:357
  117.2 2.6 %collective-permute-done.25 = bf16[8,4096]{1,0:T(8,128)(2,1)S(1)} collective-permute-done((bf16[8,4096]{1,0:T(8,128)(2,1)S(1)}, bf16[8,4096]{1,0:T(8,128)(2,1)S(1)}, u32[]{:S(2)}, u32[]{:S(2)}) %collective-permute-start.25) | collective-permute-done | bytes 65568 | tf_op jit(solution)/shard_map/ppermute | solution.py:357
  119.8 0.1 collective-permute-start.26
  119.9 4.3 %collective-permute-done.26 = bf16[8,4096]{1,0:T(8,128)(2,1)S(1)} collective-permute-done((bf16[8,4096]{1,0:T(8,128)(2,1)S(1)}, bf16[8,4096]{1,0:T(8,128)(2,1)S(1)}, u32[]{:S(2)}, u32[]{:S(2)}) %collective-permute-start.26) | collective-permute-done | bytes 65568 | tf_op jit(solution)/shard_map/ppermute | solution.py:357
  124.1 0.1 collective-permute-start.27
  124.2 5.3 %collective-permute-done.27 = bf16[8,4096]{1,0:T(8,128)(2,1)S(1)} collective-permute-done((bf16[8,4096]{1,0:T(8,128)(2,1)S(1)}, bf16[8,4096]{1,0:T(8,128)(2,1)S(1)}, u32[]{:S(2)}, u32[]{:S(2)}) %collective-permute-start.27) | collective-permute-done | bytes 65568 | tf_op jit(solution)/shard_map/ppermute | solution.py:357
  129.5 0.1 collective-permute-start.28
  129.6 1.3 %collective-permute-done.28 = f32[8,4096]{1,0:T(8,128)S(1)} collective-permute-done((f32[8,4096]{1,0:T(8,128)S(1)}, f32[8,4096]{1,0:T(8,128)S(1)}, u32[]{:S(2)}, u32[]{:S(2)}) %collective-permute-start.28) | collective-permute-done | bytes 131104 | tf_op jit(solution)/shard_map/ppermute | solution.py:357
  131.0 1.0 shard_map.137
  (51 shorter events, 0.4 us)
Async XLA Ops:
  0.0 3.0 %copy-start = (bf16[64,8192]{1,0:T(8,128)(2,1)S(1)}, bf16[64,8192]{1,0:T(8,128)(2,1)}, u32[]{:S(2)}) copy-start(bf16[64,8192]{1,0:T(8,128)(2,1)} %param.19) | copy-start | bytes 3145732
  0.0 27.7 %collective-permute-start = (bf16[1024,512]{1,0:T(8,128)(2,1)}, bf16[1024,512]{1,0:T(8,128)(2,1)S(1)}, u32[]{:S(2)}, u32[]{:S(2)}) collective-permute-start(bf16[1024,512]{1,0:T(8,128)(2,1)} %refs_0_.1), channel_id=1, source_target_pairs={{0,4},{1,5},{4,8},{5,9},{8,12},{9,13},{12,14},{13,15},{14,10},{15,... | collective-permute-start | bytes 3145736 | tf_op jit(solution)/shard_map/ppermute | solution.py:405
  3.0 24.8 %collective-permute-start.1 = (bf16[1024,512]{1,0:T(8,128)(2,1)}, bf16[1024,512]{1,0:T(8,128)(2,1)S(1)}, u32[]{:S(2)}, u32[]{:S(2)}) collective-permute-start(bf16[1024,512]{1,0:T(8,128)(2,1)} %refs_0_.1), channel_id=1, source_target_pairs={{4,0},{5,1},{8,4},{9,5},{12,8},{13,9},{14,12},{15,13},{10,14},{11,... | collective-permute-start | bytes 3145736 | tf_op jit(solution)/shard_map/ppermute | solution.py:405
  3.0 28.3 %collective-permute-start.7 = (bf16[1024,512]{1,0:T(8,128)(2,1)}, bf16[1024,512]{1,0:T(8,128)(2,1)}, u32[]{:S(2)}, u32[]{:S(2)}) collective-permute-start(bf16[1024,512]{1,0:T(8,128)(2,1)} %refs_0_.1), channel_id=1, source_target_pairs={{0,1},{1,0},{2,3},{3,2},{4,5},{5,4},{6,7},{7,6},{8,9},{9,8},{10,11... | collective-permute-start | bytes 3145736 | tf_op jit(solution)/shard_map/ppermute | solution.py:357
  3.1 1.3 copy-start.3
  4.3 1.2 copy-start.4
  5.5 0.8 copy-start.7
  7.1 1.7 %collective-permute-start.2 = (f32[64,1024]{1,0:T(8,128)S(1)}, f32[64,1024]{1,0:T(8,128)S(1)}, u32[]{:S(2)}, u32[]{:S(2)}) collective-permute-start(f32[64,1024]{1,0:T(8,128)S(1)} %get-tuple-element.41), channel_id=1, source_target_pairs={{0,1},{1,0},{2,3},{3,2},{4,5},{5,4},{6,7},{7,6},{8,9},{9,8},{10,11... | collective-permute-start | bytes 786440 | tf_op jit(solution)/shard_map/ppermute | solution.py:357
  8.9 19.0 %copy-start.8 = (f32[64,1024]{1,0:T(8,128)}, f32[64,1024]{1,0:T(8,128)S(1)}, u32[]{:S(2)}) copy-start(f32[64,1024]{1,0:T(8,128)S(1)} %add.54) | copy-start | bytes 786436
  8.9 18.8 %collective-permute-start.3 = (bf16[32,1024]{1,0:T(8,128)(2,1)S(1)}, bf16[32,1024]{1,0:T(8,128)(2,1)S(1)}, u32[]{:S(2)}, u32[]{:S(2)}) collective-permute-start(bf16[32,1024]{1,0:T(8,128)(2,1)S(1)} %dynamic-slice_convert_fusion), channel_id=1, source_target_pairs={{0,2},{1,3},{2,0},{3,1},{4,6},{5,7},{6,4},{7,5},{8,10},{9,11},{10,... | collective-permute-start | bytes 196616 | tf_op jit(solution)/shard_map/ppermute | solution.py:357
  11.7 0.9 copy-start.6
  20.3 2.9 %copy-start.2 = (f32[7,1024,256]{2,1,0:T(8,128)}, f32[7,1024,256]{2,1,0:T(8,128)S(1)}, u32[]{:S(2)}) copy-start(f32[7,1024,256]{2,1,0:T(8,128)S(1)} %get-tuple-element.70.refs_5_) | copy-start | bytes 22020100
  27.9 7.7 %collective-permute-start.8 = (bf16[1024,512]{1,0:T(8,128)(2,1)S(1)}, bf16[1024,512]{1,0:T(8,128)(2,1)}, u32[]{:S(2)}, u32[]{:S(2)}) collective-permute-start(bf16[1024,512]{1,0:T(8,128)(2,1)S(1)} %collective-permute-done.refs_2_), channel_id=1, source_target_pairs={{0,1},{1,0},{2,3},{3,2},{4,5},{5,4},{6,7},{7,6},{8,9},{9,8},{10,11... | collective-permute-start | bytes 3145736 | tf_op jit(solution)/shard_map/ppermute | solution.py:357
  27.9 7.7 %collective-permute-start.9 = (bf16[1024,512]{1,0:T(8,128)(2,1)S(1)}, bf16[1024,512]{1,0:T(8,128)(2,1)}, u32[]{:S(2)}, u32[]{:S(2)}) collective-permute-start(bf16[1024,512]{1,0:T(8,128)(2,1)S(1)} %collective-permute-done.1.refs_3_), channel_id=1, source_target_pairs={{0,1},{1,0},{2,3},{3,2},{4,5},{5,4},{6,7},{7,6},{8,9},{9,8},{10,11... | collective-permute-start | bytes 3145736 | tf_op jit(solution)/shard_map/ppermute | solution.py:357
  28.4 31.5 %collective-permute-start.4 = (bf16[1024,512]{1,0:T(8,128)(2,1)S(1)}, bf16[1024,512]{1,0:T(8,128)(2,1)S(1)}, u32[]{:S(2)}, u32[]{:S(2)}) collective-permute-start(bf16[1024,512]{1,0:T(8,128)(2,1)S(1)} %collective-permute-done.refs_2_), channel_id=1, source_target_pairs={{0,4},{1,5},{4,8},{5,9},{8,12},{9,13},{12,14},{13,15},{14,10},{15,... | collective-permute-start | bytes 3145736 | tf_op jit(solution)/shard_map/ppermute | solution.py:405
  29.9 29.9 %collective-permute-start.5 = (bf16[1024,512]{1,0:T(8,128)(2,1)S(1)}, bf16[1024,512]{1,0:T(8,128)(2,1)}, u32[]{:S(2)}, u32[]{:S(2)}) collective-permute-start(bf16[1024,512]{1,0:T(8,128)(2,1)S(1)} %collective-permute-done.1.refs_3_), channel_id=1, source_target_pairs={{4,0},{5,1},{8,4},{9,5},{12,8},{13,9},{14,12},{15,13},{10,14},{11,... | collective-permute-start | bytes 3145736 | tf_op jit(solution)/shard_map/ppermute | solution.py:405
  31.3 28.5 %collective-permute-start.6 = (bf16[32,1024]{1,0:T(8,128)(2,1)S(1)}, bf16[32,1024]{1,0:T(8,128)(2,1)S(1)}, u32[]{:S(2)}, u32[]{:S(2)}) collective-permute-start(bf16[32,1024]{1,0:T(8,128)(2,1)S(1)} %fusion.3), channel_id=1, source_target_pairs={{0,8},{1,9},{2,10},{3,11},{4,12},{5,13},{6,14},{7,15},{8,0},{9,1},... | collective-permute-start | bytes 196616 | tf_op jit(solution)/shard_map/ppermute | solution.py:357
  35.6 26.8 %copy-start.9 = (f32[64,1024]{1,0:T(8,128)S(1)}, f32[64,1024]{1,0:T(8,128)}, u32[]{:S(2)}) copy-start(f32[64,1024]{1,0:T(8,128)} %copy-done.8) | copy-start | bytes 786436
  59.8 13.4 %collective-permute-start.13 = (bf16[1024,512]{1,0:T(8,128)(2,1)S(1)}, bf16[1024,512]{1,0:T(8,128)(2,1)S(1)}, u32[]{:S(2)}, u32[]{:S(2)}) collective-permute-start(bf16[1024,512]{1,0:T(8,128)(2,1)S(1)} %collective-permute-done.4.refs_0_), channel_id=1, source_target_pairs={{0,1},{1,0},{2,3},{3,2},{4,5},{5,4},{6,7},{7,6},{8,9},{9,8},{10,11... | collective-permute-start | bytes 3145736 | tf_op jit(solution)/shard_map/ppermute | solution.py:357
  59.8 13.4 %collective-permute-start.14 = (bf16[1024,512]{1,0:T(8,128)(2,1)}, bf16[1024,512]{1,0:T(8,128)(2,1)S(1)}, u32[]{:S(2)}, u32[]{:S(2)}) collective-permute-start(bf16[1024,512]{1,0:T(8,128)(2,1)} %collective-permute-done.5.refs_1_), channel_id=1, source_target_pairs={{0,1},{1,0},{2,3},{3,2},{4,5},{5,4},{6,7},{7,6},{8,9},{9,8},{10,11... | collective-permute-start | bytes 3145736 | tf_op jit(solution)/shard_map/ppermute | solution.py:357
  60.3 26.9 %collective-permute-start.10 = (bf16[1024,512]{1,0:T(8,128)(2,1)S(1)}, bf16[1024,512]{1,0:T(8,128)(2,1)S(1)}, u32[]{:S(2)}, u32[]{:S(2)}) collective-permute-start(bf16[1024,512]{1,0:T(8,128)(2,1)S(1)} %collective-permute-done.4.refs_0_), channel_id=1, source_target_pairs={{0,4},{1,5},{4,8},{5,9},{8,12},{9,13},{12,14},{13,15},{14,10},{15,... | collective-permute-start | bytes 3145736 | tf_op jit(solution)/shard_map/ppermute | solution.py:405
  60.8 26.5 %collective-permute-start.11 = (bf16[1024,512]{1,0:T(8,128)(2,1)}, bf16[1024,512]{1,0:T(8,128)(2,1)S(1)}, u32[]{:S(2)}, u32[]{:S(2)}) collective-permute-start(bf16[1024,512]{1,0:T(8,128)(2,1)} %collective-permute-done.5.refs_1_), channel_id=1, source_target_pairs={{4,0},{5,1},{8,4},{9,5},{12,8},{13,9},{14,12},{15,13},{10,14},{11,... | collective-permute-start | bytes 3145736 | tf_op jit(solution)/shard_map/ppermute | solution.py:405
  62.4 24.9 %collective-permute-start.12 = (bf16[32,1024]{1,0:T(8,128)(2,1)S(1)}, bf16[32,1024]{1,0:T(8,128)(2,1)S(1)}, u32[]{:S(2)}, u32[]{:S(2)}) collective-permute-start(bf16[32,1024]{1,0:T(8,128)(2,1)S(1)} %fusion), channel_id=1, source_target_pairs={{0,4},{1,5},{2,6},{3,7},{4,0},{5,1},{6,2},{7,3},{8,12},{9,13},{10,... | collective-permute-start | bytes 196616 | tf_op jit(solution)/shard_map/ppermute | solution.py:357
  87.3 2.8 %collective-permute-start.15 = (bf16[1024,512]{1,0:T(8,128)(2,1)S(1)}, bf16[1024,512]{1,0:T(8,128)(2,1)S(1)}, u32[]{:S(2)}, u32[]{:S(2)}) collective-permute-start(bf16[1024,512]{1,0:T(8,128)(2,1)S(1)} %collective-permute-done.10.refs_0_), channel_id=1, source_target_pairs={{0,1},{1,0},{2,3},{3,2},{4,5},{5,4},{6,7},{7,6},{8,9},{9,8},{10,11... | collective-permute-start | bytes 3145736 | tf_op jit(solution)/shard_map/ppermute | solution.py:357
  87.3 4.2 %collective-permute-start.16 = (bf16[1024,512]{1,0:T(8,128)(2,1)S(1)}, bf16[1024,512]{1,0:T(8,128)(2,1)S(1)}, u32[]{:S(2)}, u32[]{:S(2)}) collective-permute-start(bf16[1024,512]{1,0:T(8,128)(2,1)S(1)} %collective-permute-done.11.refs_1_), channel_id=1, source_target_pairs={{0,1},{1,0},{2,3},{3,2},{4,5},{5,4},{6,7},{7,6},{8,9},{9,8},{10,11... | collective-permute-start | bytes 3145736 | tf_op jit(solution)/shard_map/ppermute | solution.py:357
  87.9 16.1 %collective-permute-start.20 = (bf16[512,512]{1,0:T(8,128)(2,1)S(1)}, bf16[512,512]{1,0:T(8,128)(2,1)S(1)}, u32[]{:S(2)}, u32[]{:S(2)}) collective-permute-start(bf16[512,512]{1,0:T(8,128)(2,1)S(1)} %slice.6), channel_id=1, source_target_pairs={{0,4},{1,5},{4,8},{5,9},{8,12},{9,13},{12,14},{13,15},{14,10},{15,... | collective-permute-start | bytes 1572872 | tf_op jit(solution)/shard_map/ppermute | solution.py:405
  88.5 15.5 %collective-permute-start.21 = (bf16[512,512]{1,0:T(8,128)(2,1)S(1)}, bf16[512,512]{1,0:T(8,128)(2,1)S(1)}, u32[]{:S(2)}, u32[]{:S(2)}) collective-permute-start(bf16[512,512]{1,0:T(8,128)(2,1)S(1)} %slice.7), channel_id=1, source_target_pairs={{4,0},{5,1},{8,4},{9,5},{12,8},{13,9},{14,12},{15,13},{10,14},{11,... | collective-permute-start | bytes 1572872 | tf_op jit(solution)/shard_map/ppermute | solution.py:405
  90.0 13.9 %collective-permute-start.18 = (f32[32,1024]{1,0:T(8,128)S(1)}, f32[32,1024]{1,0:T(8,128)S(1)}, u32[]{:S(2)}, u32[]{:S(2)}) collective-permute-start(f32[32,1024]{1,0:T(8,128)S(1)} %get-tuple-element.60.mine_ref), channel_id=1, source_target_pairs={{0,1},{1,0},{2,3},{3,2},{4,5},{5,4},{6,7},{7,6},{8,9},{9,8},{10,11... | collective-permute-start | bytes 393224 | tf_op jit(solution)/shard_map/ppermute | solution.py:357
  90.1 16.9 %slice-start = ((s8[7340032]{0:T(1024)(128)(4,1)}), s8[4194304]{0:T(1024)(128)(4,1)S(1)}, s32[]{:S(2)}) async-start(s8[7340032]{0:T(1024)(128)(4,1)} %bitcast.5), calls=%async_computation | async-start | bytes 8388608
  90.1 16.9 %slice-start.1 = ((s8[7340032]{0:T(1024)(128)(4,1)}), s8[3145728]{0:T(1024)(128)(4,1)S(1)}, s32[]{:S(2)}) async-start(s8[7340032]{0:T(1024)(128)(4,1)} %bitcast.5), calls=%async_computation.1 | async-start | bytes 6291456
  90.1 16.9 %copy-start.5 = (bf16[64,1792]{1,0:T(8,128)(2,1)S(1)}, bf16[64,1792]{1,0:T(8,128)(2,1)}, u32[]{:S(2)}) copy-start(bf16[64,1792]{1,0:T(8,128)(2,1)} %refs_6_.5) | copy-start | bytes 688132
  90.1 13.8 %collective-permute-start.17 = (bf16[32,1024]{1,0:T(8,128)(2,1)S(1)}, bf16[32,1024]{1,0:T(8,128)(2,1)S(1)}, u32[]{:S(2)}, u32[]{:S(2)}) collective-permute-start(bf16[32,1024]{1,0:T(8,128)(2,1)S(1)} %get-tuple-element.77), channel_id=1, source_target_pairs={{0,2},{1,3},{2,0},{3,1},{4,6},{5,7},{6,4},{7,5},{8,10},{9,11},{10,... | collective-permute-start | bytes 196616 | tf_op jit(solution)/shard_map/ppermute | solution.py:357
  91.4 12.5 %collective-permute-start.19 = (bf16[32,1024]{1,0:T(8,128)(2,1)S(1)}, bf16[32,1024]{1,0:T(8,128)(2,1)S(1)}, u32[]{:S(2)}, u32[]{:S(2)}) collective-permute-start(bf16[32,1024]{1,0:T(8,128)(2,1)S(1)} %get-tuple-element.77), channel_id=1, source_target_pairs={{0,3},{1,2},{2,1},{3,0},{4,7},{5,6},{6,5},{7,4},{8,11},{9,10},{10,... | collective-permute-start | bytes 196616 | tf_op jit(solution)/shard_map/ppermute | solution.py:357
  103.9 3.0 %collective-permute-start.22 = (bf16[512,512]{1,0:T(8,128)(2,1)S(1)}, bf16[512,512]{1,0:T(8,128)(2,1)S(1)}, u32[]{:S(2)}, u32[]{:S(2)}) collective-permute-start(bf16[512,512]{1,0:T(8,128)(2,1)S(1)} %collective-permute-done.20.refs_0_), channel_id=1, source_target_pairs={{0,1},{1,0},{2,3},{3,2},{4,5},{5,4},{6,7},{7,6},{8,9},{9,8},{10,11... | collective-permute-start | bytes 1572872 | tf_op jit(solution)/shard_map/ppermute | solution.py:357
  104.5 2.4 %collective-permute-start.23 = (bf16[512,512]{1,0:T(8,128)(2,1)S(1)}, bf16[512,512]{1,0:T(8,128)(2,1)S(1)}, u32[]{:S(2)}, u32[]{:S(2)}) collective-permute-start(bf16[512,512]{1,0:T(8,128)(2,1)S(1)} %collective-permute-done.21.refs_2_), channel_id=1, source_target_pairs={{0,1},{1,0},{2,3},{3,2},{4,5},{5,4},{6,7},{7,6},{8,9},{9,8},{10,11... | collective-permute-start | bytes 1572872 | tf_op jit(solution)/shard_map/ppermute | solution.py:357
  107.0 25.0 %copy-start.1 = (bf16[64,8192]{1,0:T(8,128)(2,1)S(1)}, bf16[64,8192]{1,0:T(8,128)(2,1)}, u32[]{:S(2)}) copy-start(bf16[64,8192]{1,0:T(8,128)(2,1)} %param.19) | copy-start | bytes 3145732
  113.8 1.5 %collective-permute-start.24 = (f32[8,4096]{1,0:T(8,128)S(1)}, f32[8,4096]{1,0:T(8,128)S(1)}, u32[]{:S(2)}, u32[]{:S(2)}) collective-permute-start(f32[8,4096]{1,0:T(8,128)S(1)} %broadcast_select_fusion.2), channel_id=1, source_target_pairs={{0,1},{1,0},{2,3},{3,2},{4,5},{5,4},{6,7},{7,6},{8,9},{9,8},{10,11... | collective-permute-start | bytes 393224 | tf_op jit(solution)/shard_map/ppermute | solution.py:357
  115.3 4.4 %collective-permute-start.25 = (bf16[8,4096]{1,0:T(8,128)(2,1)S(1)}, bf16[8,4096]{1,0:T(8,128)(2,1)S(1)}, u32[]{:S(2)}, u32[]{:S(2)}) collective-permute-start(bf16[8,4096]{1,0:T(8,128)(2,1)S(1)} %get-tuple-element.75), channel_id=1, source_target_pairs={{0,2},{1,3},{2,0},{3,1},{4,6},{5,7},{6,4},{7,5},{8,10},{9,11},{10,... | collective-permute-start | bytes 196616 | tf_op jit(solution)/shard_map/ppermute | solution.py:357
  119.8 4.3 %collective-permute-start.26 = (bf16[8,4096]{1,0:T(8,128)(2,1)S(1)}, bf16[8,4096]{1,0:T(8,128)(2,1)S(1)}, u32[]{:S(2)}, u32[]{:S(2)}) collective-permute-start(bf16[8,4096]{1,0:T(8,128)(2,1)S(1)} %fusion.1), channel_id=1, source_target_pairs={{0,4},{1,5},{2,6},{3,7},{4,0},{5,1},{6,2},{7,3},{8,12},{9,13},{10,... | collective-permute-start | bytes 196616 | tf_op jit(solution)/shard_map/ppermute | solution.py:357
  124.1 5.4 %collective-permute-start.27 = (bf16[8,4096]{1,0:T(8,128)(2,1)S(1)}, bf16[8,4096]{1,0:T(8,128)(2,1)S(1)}, u32[]{:S(2)}, u32[]{:S(2)}) collective-permute-start(bf16[8,4096]{1,0:T(8,128)(2,1)S(1)} %fusion.2), channel_id=1, source_target_pairs={{0,8},{1,9},{2,10},{3,11},{4,12},{5,13},{6,14},{7,15},{8,0},{9,1},... | collective-permute-start | bytes 196616 | tf_op jit(solution)/shard_map/ppermute | solution.py:357
  129.5 1.4 %collective-permute-start.28 = (f32[8,4096]{1,0:T(8,128)S(1)}, f32[8,4096]{1,0:T(8,128)S(1)}, u32[]{:S(2)}, u32[]{:S(2)}) collective-permute-start(f32[8,4096]{1,0:T(8,128)S(1)} %convert_add_fusion), channel_id=1, source_target_pairs={{0,1},{1,0},{2,3},{3,2},{4,5},{5,4},{6,7},{7,6},{8,9},{9,8},{10,11... | collective-permute-start | bytes 393224 | tf_op jit(solution)/shard_map/ppermute | solution.py:357

commit v7 on v6

--- a/solution.py
+++ b/solution.py
@@ -458,10 +458,6 @@
             beyond = [swap(part.astype(BF16), bit, devices) for bit in (2, 3)]
             quarters = [near[0], beyond[0], near[1], beyond[1]]
             known = near_step([array for array, _ in units], columns[0], known)
-            known, quarters = pin((known, quarters))
-            high, low, down = pair_parts(
-                jnp.stack([me % 2, side]), pair_weight, quarters, a_down
-            )
         else:
             known = add_step(src, units, down_weight, known)
             units = []
@@ -470,6 +466,8 @@
             came = (f, b)
     f, b, known = pin((f, b, known))
     halves = [x for block in (f, b) for x in (block, swap(block, 1, devices))]
+    known, quarters = pin((known, quarters))
+    high, low, down = pair_parts(jnp.stack([me % 2, side]), pair_weight, quarters, a_down)
     up = last_step(halves, columns[1], silu_gate, out_proj_up, known, (high, low), pairs)
 
     first = core == 0

time: 133 us -> 137 us (1.030)
  starting transfers between devices: 21.4 us -> 23.6 us
  waiting for transfers between devices: 32.3 us -> 34.2 us
    ppermute x4, waiting for transfers between devices: 0.01 us -> 2.4 us  [send(): lax.ppermute(forward, 'tensor', ahead)]
    ppermute x21, starting transfers between devices: 12.2 us -> 14.4 us  [swap(): return lax.ppermute(value, 'tensor', [(i, i ^ bit) for i in range(devices)])]
  transfers between devices with their start and end apart: 29 -> 29, of which waited for: 12 -> 15; matrix products, arithmetic and copies ran while one was open for 3% -> 3% of each run, Pallas kernels for 45% -> 44%
where the time goes in v7:
time: 137 us; the launch traced here: 136 us
  Pallas kernels  67.1 us (49%)
  waiting for transfers between devices  34.2 us (25%)
  starting transfers between devices  23.6 us (17%)
  local copies, waits for them, and re-layouts  8.14 us (6%)
  other arithmetic  2.65 us (2%)
    ppermute x21, waiting for transfers between devices, swap(): return lax.ppermute(value, 'tensor', [(i, i ^ bit) for i in range(devices)])  31.4 us
    pallas_call x2, Pallas kernels, add_step(): pl.pallas_call(functools.partial(step_kernel, len(units)), grid_spec=pltp...  30.4 us
    ppermute x21, starting transfers between devices, swap(): return lax.ppermute(value, 'tensor', [(i, i ^ bit) for i in range(devices)])  14.4 us
    pallas_call x1, Pallas kernels, near_step(): pl.pallas_call(near_kernel, in_specs=[WHOLE] * len(ins), out_specs=WHOLE,...  8.02 us
    pallas_call x1, Pallas kernels, own_parts(): pl.pallas_call(own_kernel, grid=(units // tile,), in_specs=[tiles, tiles,...  7.61 us
    unnamed x24, local copies, waits for them, and re-layouts  7.18 us
    pallas_call x1, Pallas kernels, last_step(): pl.pallas_call(last_kernel, in_specs=[WHOLE] * len(ins), out_specs=WHOLE,...  6.76 us
    pallas_call x2, Pallas kernels, columns_of(): pl.pallas_call(functools.partial(columns_kernel, places), grid_spec=pltpu...  6.4 us
  transfers between devices with their start and end apart: 29, of which 15 were waited for; matrix products, arithmetic and copies ran while one was open for 3% of the time, Pallas kernels for 44%

profile of v7, /device:TPU:0, one launch (start us, length us, event | category | flops | bytes accessed | tf_op | source)
XLA Modules:
  0.0 136.0 jit_solution(10841160007018043994)
XLA Ops:
  0.0 3.0 %collective-permute-start = (bf16[1024,512]{1,0:T(8,128)(2,1)}, bf16[1024,512]{1,0:T(8,128)(2,1)S(1)}, u32[]{:S(2)}, u32[]{:S(2)}) collective-permute-start(bf16[1024,512]{1,0:T(8,128)(2,1)} %refs_0_.1), channel_id=1, source_target_pairs={{0,4},{1,5},{4,8},{5,9},{8,12},{9,13},{12,14},{13,15},{14,10},{15,... | collective-permute-start | bytes 3145736 | tf_op jit(solution)/shard_map/ppermute | solution.py:405
  3.1 0.0 copy-start.3
  3.1 1.3 copy-done.3
  4.3 1.2 copy-done.4
  5.5 0.8 copy-done.7
  6.4 0.7 shard_map.127
  7.1 0.5 collective-permute-start.2
  7.7 0.7 add_convert_fusion
  8.3 0.1 broadcast_in_dim.39
  8.4 0.1 copy.16
  8.5 0.3 collective-permute-done.2
  8.9 2.0 %collective-permute-start.3 = (bf16[32,1024]{1,0:T(8,128)(2,1)S(1)}, bf16[32,1024]{1,0:T(8,128)(2,1)S(1)}, u32[]{:S(2)}, u32[]{:S(2)}) collective-permute-start(bf16[32,1024]{1,0:T(8,128)(2,1)S(1)} %dynamic-slice_convert_fusion), channel_id=1, source_target_pairs={{0,2},{1,3},{2,0},{3,1},{4,6},{5,7},{6,4},{7,5},{8,10},{9,11},{10,... | collective-permute-start | bytes 196616 | tf_op jit(solution)/shard_map/ppermute | solution.py:357
  10.9 0.8 select_reduce_fusion.weight_ref
  11.7 0.9 copy-done.6
  12.6 7.6 %shard_map.128 = (f32[7,1024,256]{2,1,0:T(8,128)S(1)}, f32[64,1024]{1,0:T(8,128)S(1)}) custom-call(bf16[1024,1792]{1,0:T(8,128)(2,1)} %gate_ref, bf16[1024,1792]{1,0:T(8,128)(2,1)} %up_ref, bf16[64,1792]{1,0:T(8,128)(2,1)S(1)} %copy-done.6), custom_call_target="tpu_custom_call" | custom-call | flops 1000 | bytes 1000 | tf_op jit(solution)/shard_map/pallas_call | solution.py:235
  20.3 2.9 %copy-done.2 = f32[7,1024,256]{2,1,0:T(8,128)} copy-done((f32[7,1024,256]{2,1,0:T(8,128)}, f32[7,1024,256]{2,1,0:T(8,128)S(1)}, u32[]{:S(2)}) %copy-start.2) | copy-done | bytes 7340056
  23.2 4.6 %collective-permute-done.3 = bf16[32,1024]{1,0:T(8,128)(2,1)S(1)} collective-permute-done((bf16[32,1024]{1,0:T(8,128)(2,1)S(1)}, bf16[32,1024]{1,0:T(8,128)(2,1)S(1)}, u32[]{:S(2)}, u32[]{:S(2)}) %collective-permute-start.3) | collective-permute-done | bytes 65568 | tf_op jit(solution)/shard_map/ppermute | solution.py:357
  27.7 0.1 collective-permute-done.1.refs_3_
  27.9 0.5 collective-permute-start.9
  28.4 1.6 %collective-permute-start.4 = (bf16[1024,512]{1,0:T(8,128)(2,1)S(1)}, bf16[1024,512]{1,0:T(8,128)(2,1)S(1)}, u32[]{:S(2)}, u32[]{:S(2)}) collective-permute-start(bf16[1024,512]{1,0:T(8,128)(2,1)S(1)} %collective-permute-done.refs_2_), channel_id=1, source_target_pairs={{0,4},{1,5},{4,8},{5,9},{8,12},{9,13},{12,14},{13,15},{14,10},{15,... | collective-permute-start | bytes 3145736 | tf_op jit(solution)/shard_map/ppermute | solution.py:405
  29.9 0.4 collective-permute-start.5
  30.4 0.9 fusion.3
  31.3 3.6 %collective-permute-start.6 = (bf16[32,1024]{1,0:T(8,128)(2,1)S(1)}, bf16[32,1024]{1,0:T(8,128)(2,1)S(1)}, u32[]{:S(2)}, u32[]{:S(2)}) collective-permute-start(bf16[32,1024]{1,0:T(8,128)(2,1)S(1)} %fusion.3), channel_id=1, source_target_pairs={{0,8},{1,9},{2,10},{3,11},{4,12},{5,13},{6,14},{7,15},{8,0},{9,1},... | collective-permute-start | bytes 196616 | tf_op jit(solution)/shard_map/ppermute | solution.py:357
  34.9 0.7 fusion.4.src_ref
  35.6 17.5 %shard_map.129.refs_8_ = f32[7,1024,256]{2,1,0:T(8,128)S(1)} custom-call(s32[16]{0:T(128)S(1)} %fusion.4.src_ref, bf16[1024,512]{1,0:T(8,128)(2,1)} %refs_0_.1, bf16[1024,512]{1,0:T(8,128)(2,1)} %collective-permute-done.7.refs_1_, bf16[1024,512]{1,0:T(8,128)(2,1)S(1)} %collective-permute-done.refs_2_, bf16[1024,512]{1,0:T(8,128)(2,1)S(1)} %collective-permute-done.1.refs_3_, ...), custom_call_target="tpu_custom_call" | custom-call | flops 1000 | bytes 1000 | tf_op jit(solution)/shard_map/pallas_call | solution.py:133
  53.2 6.7 %collective-permute-done.6 = bf16[32,1024]{1,0:T(8,128)(2,1)S(1)} collective-permute-done((bf16[32,1024]{1,0:T(8,128)(2,1)S(1)}, bf16[32,1024]{1,0:T(8,128)(2,1)S(1)}, u32[]{:S(2)}, u32[]{:S(2)}) %collective-permute-start.6) | collective-permute-done | bytes 65568 | tf_op jit(solution)/shard_map/ppermute | solution.py:357
  59.8 0.5 collective-permute-start.14
  60.3 0.4 collective-permute-start.10
  60.8 1.6 %collective-permute-start.11 = (bf16[1024,512]{1,0:T(8,128)(2,1)}, bf16[1024,512]{1,0:T(8,128)(2,1)S(1)}, u32[]{:S(2)}, u32[]{:S(2)}) collective-permute-start(bf16[1024,512]{1,0:T(8,128)(2,1)} %collective-permute-done.5.refs_1_), channel_id=1, source_target_pairs={{4,0},{5,1},{8,4},{9,5},{12,8},{13,9},{14,12},{15,13},{10,14},{11,... | collective-permute-start | bytes 3145736 | tf_op jit(solution)/shard_map/ppermute | solution.py:405
  62.4 0.5 collective-permute-start.12
  62.9 3.8 %shard_map.130.refs_4_ = bf16[4,1792,512]{2,1,0:T(8,128)(2,1)S(1)} custom-call(s32[16]{0:T(128)S(1)} %fusion.4.src_ref, bf16[1792,8192]{1,0:T(8,128)(2,1)} %refs_7_.3), custom_call_target="tpu_custom_call" | custom-call | flops 1000 | bytes 1000 | tf_op jit(solution)/shard_map/pallas_call | solution.py:164
  66.7 2.6 %shard_map.131.refs_4_ = bf16[2,1792,512]{2,1,0:T(8,128)(2,1)S(1)} custom-call(s32[16]{0:T(128)S(1)} %fusion.4.src_ref, bf16[1792,8192]{1,0:T(8,128)(2,1)} %refs_7_.3), custom_call_target="tpu_custom_call" | custom-call | flops 1000 | bytes 1000 | tf_op jit(solution)/shard_map/pallas_call | solution.py:164
  69.3 3.9 %shard_map.132.q_ref = bf16[8192,64]{1,0:T(8,128)(2,1)S(1)} custom-call(bf16[64,8192]{1,0:T(8,128)(2,1)} %q_ref.1), custom_call_target="tpu_custom_call" | custom-call | flops 1000 | bytes 1000 | tf_op jit(solution)/shard_map/pallas_call | solution.py:259
  73.2 12.9 %shard_map.133.refs_5_ = f32[7,1024,256]{2,1,0:T(8,128)S(1)} custom-call(s32[16]{0:T(128)S(1)} %fusion.4.src_ref, bf16[1024,512]{1,0:T(8,128)(2,1)S(1)} %collective-permute-done.4.refs_0_, bf16[1024,512]{1,0:T(8,128)(2,1)} %collective-permute-done.5.refs_1_, bf16[1024,512]{1,0:T(8,128)(2,1)S(1)} %collective-permute-done.13.refs_2_, ...), custom_call_target="tpu_custom_call", output_to_operand_aliasing={{}: (9, {})} | custom-call | flops 1000 | bytes 1000 | tf_op jit(solution)/shard_map/pallas_call | solution.py:133
  86.1 1.1 collective-permute-done.12
  87.3 0.5 collective-permute-start.18
  87.9 0.0 copy-start.5
  87.9 0.6 collective-permute-start.15
  88.5 1.5 %collective-permute-start.16 = (bf16[512,512]{1,0:T(8,128)(2,1)S(1)}, bf16[512,512]{1,0:T(8,128)(2,1)S(1)}, u32[]{:S(2)}, u32[]{:S(2)}) collective-permute-start(bf16[512,512]{1,0:T(8,128)(2,1)S(1)} %slice.7), channel_id=1, source_target_pairs={{4,0},{5,1},{8,4},{9,5},{12,8},{13,9},{14,12},{15,13},{10,14},{11,... | collective-permute-start | bytes 1572872 | tf_op jit(solution)/shard_map/ppermute | solution.py:405
  90.0 1.5 %collective-permute-done.18.refs_3_ = bf16[1024,512]{1,0:T(8,128)(2,1)S(1)} collective-permute-done((bf16[1024,512]{1,0:T(8,128)(2,1)S(1)}, bf16[1024,512]{1,0:T(8,128)(2,1)S(1)}, u32[]{:S(2)}, u32[]{:S(2)}) %collective-permute-start.18) | collective-permute-done | bytes 1048608 | tf_op jit(solution)/shard_map/ppermute | solution.py:357
  91.4 8.0 %shard_map.134.refs_7_ = f32[7,1024,256]{2,1,0:T(8,128)S(1)} custom-call(bf16[1024,512]{1,0:T(8,128)(2,1)S(1)} %collective-permute-done.10.refs_0_, bf16[1024,512]{1,0:T(8,128)(2,1)S(1)} %collective-permute-done.11.refs_1_, bf16[1024,512]{1,0:T(8,128)(2,1)S(1)} %collective-permute-done.17.refs_2_, ...), custom_call_target="tpu_custom_call", output_to_operand_aliasing={{}: (5, {})} | custom-call | flops 1000 | bytes 1000 | tf_op jit(solution)/shard_map/pallas_call | solution.py:80
  99.4 2.4 %collective-permute-done.15.refs_0_ = bf16[512,512]{1,0:T(8,128)(2,1)S(1)} collective-permute-done((bf16[512,512]{1,0:T(8,128)(2,1)S(1)}, bf16[512,512]{1,0:T(8,128)(2,1)S(1)}, u32[]{:S(2)}, u32[]{:S(2)}) %collective-permute-start.15) | collective-permute-done | bytes 524320 | tf_op jit(solution)/shard_map/ppermute | solution.py:405
  101.8 0.3 collective-permute-done.16.refs_2_
  102.1 0.5 collective-permute-start.23
  102.7 0.1 collective-permute-start.20
  102.8 1.5 %collective-permute-start.19 = (bf16[32,1024]{1,0:T(8,128)(2,1)S(1)}, bf16[32,1024]{1,0:T(8,128)(2,1)S(1)}, u32[]{:S(2)}, u32[]{:S(2)}) collective-permute-start(bf16[32,1024]{1,0:T(8,128)(2,1)S(1)} %get-tuple-element.77), channel_id=1, source_target_pairs={{0,2},{1,3},{2,0},{3,1},{4,6},{5,7},{6,4},{7,5},{8,10},{9,11},{10,... | collective-permute-start | bytes 196616 | tf_op jit(solution)/shard_map/ppermute | solution.py:357
  104.3 0.3 collective-permute-start.21
  104.6 0.1 pad_add_fusion.place_ref
  104.7 2.6 %collective-permute-done.19.across_ref = bf16[32,1024]{1,0:T(8,128)(2,1)S(1)} collective-permute-done((bf16[32,1024]{1,0:T(8,128)(2,1)S(1)}, bf16[32,1024]{1,0:T(8,128)(2,1)S(1)}, u32[]{:S(2)}, u32[]{:S(2)}) %collective-permute-start.19) | collective-permute-done | bytes 65568 | tf_op jit(solution)/shard_map/ppermute | solution.py:357
  107.3 1.1 collective-permute-done.21.across1_ref
  108.3 2.3 %shard_map.135 = (bf16[512,1024]{1,0:T(8,128)(2,1)S(1)}, bf16[512,1024]{1,0:T(8,128)(2,1)S(1)}, f32[8,4096]{1,0:T(8,128)S(1)}) custom-call(s32[2]{0:T(128)S(1)} %pad_add_fusion.place_ref, f32[8,1024]{1,0:T(8,128)S(1)} %select_reduce_fusion.weight_ref, f32[32,1024]{1,0:T(8,128)S(1)} %get-tuple-element.61.mine_ref, ...), custom_call_target="tpu_custom_call" | custom-call | flops 1000 | bytes 1000 | tf_op jit(solution)/shard_map/pallas_call | solution.py:346
  110.7 0.0 copy-start.1
  110.7 6.8 %shard_map.136 = f32[8,4096]{1,0:T(8,128)S(1)} custom-call(bf16[512,512]{1,0:T(8,128)(2,1)S(1)} %collective-permute-done.15.refs_0_, bf16[512,512]{1,0:T(8,128)(2,1)S(1)} %collective-permute-done.22.refs_1_, bf16[512,512]{1,0:T(8,128)(2,1)S(1)} %collective-permute-done.16.refs_2_, bf16[512,512]{1,0:T(8,128)(2,1)S(1)} %collective-permute-done.23.refs_3_, ...), custom_call_target="tpu_custom_call" | custom-call | flops 1000 | bytes 1000 | tf_op jit(solution)/shard_map/pallas_call | solution.py:204
  117.5 0.2 collective-permute-start.24
  117.7 1.2 collective-permute-done.24
  118.9 1.4 %collective-permute-start.25 = (bf16[8,4096]{1,0:T(8,128)(2,1)S(1)}, bf16[8,4096]{1,0:T(8,128)(2,1)S(1)}, u32[]{:S(2)}, u32[]{:S(2)}) collective-permute-start(bf16[8,4096]{1,0:T(8,128)(2,1)S(1)} %get-tuple-element.75), channel_id=1, source_target_pairs={{0,2},{1,3},{2,0},{3,1},{4,6},{5,7},{6,4},{7,5},{8,10},{9,11},{10,... | collective-permute-start | bytes 196616 | tf_op jit(solution)/shard_map/ppermute | solution.py:357
  120.3 2.9 %collective-permute-done.25 = bf16[8,4096]{1,0:T(8,128)(2,1)S(1)} collective-permute-done((bf16[8,4096]{1,0:T(8,128)(2,1)S(1)}, bf16[8,4096]{1,0:T(8,128)(2,1)S(1)}, u32[]{:S(2)}, u32[]{:S(2)}) %collective-permute-start.25) | collective-permute-done | bytes 65568 | tf_op jit(solution)/shard_map/ppermute | solution.py:357
  123.3 0.7 collective-permute-start.26
  124.0 3.6 %collective-permute-done.26 = bf16[8,4096]{1,0:T(8,128)(2,1)S(1)} collective-permute-done((bf16[8,4096]{1,0:T(8,128)(2,1)S(1)}, bf16[8,4096]{1,0:T(8,128)(2,1)S(1)}, u32[]{:S(2)}, u32[]{:S(2)}) %collective-permute-start.26) | collective-permute-done | bytes 65568 | tf_op jit(solution)/shard_map/ppermute | solution.py:357
  127.6 1.4 %collective-permute-start.27 = (bf16[8,4096]{1,0:T(8,128)(2,1)S(1)}, bf16[8,4096]{1,0:T(8,128)(2,1)S(1)}, u32[]{:S(2)}, u32[]{:S(2)}) collective-permute-start(bf16[8,4096]{1,0:T(8,128)(2,1)S(1)} %fusion.2), channel_id=1, source_target_pairs={{0,8},{1,9},{2,10},{3,11},{4,12},{5,13},{6,14},{7,15},{8,0},{9,1},... | collective-permute-start | bytes 196616 | tf_op jit(solution)/shard_map/ppermute | solution.py:357
  129.0 4.5 %collective-permute-done.27 = bf16[8,4096]{1,0:T(8,128)(2,1)S(1)} collective-permute-done((bf16[8,4096]{1,0:T(8,128)(2,1)S(1)}, bf16[8,4096]{1,0:T(8,128)(2,1)S(1)}, u32[]{:S(2)}, u32[]{:S(2)}) %collective-permute-start.27) | collective-permute-done | bytes 65568 | tf_op jit(solution)/shard_map/ppermute | solution.py:357
  133.6 0.1 collective-permute-start.28
  133.7 1.3 collective-permute-done.28
  135.0 1.0 shard_map.137
  (51 shorter events, 0.4 us)
Async XLA Ops:
  0.0 3.0 %copy-start = (bf16[64,8192]{1,0:T(8,128)(2,1)S(1)}, bf16[64,8192]{1,0:T(8,128)(2,1)}, u32[]{:S(2)}) copy-start(bf16[64,8192]{1,0:T(8,128)(2,1)} %param.19) | copy-start | bytes 3145732
  0.0 27.7 %collective-permute-start = (bf16[1024,512]{1,0:T(8,128)(2,1)}, bf16[1024,512]{1,0:T(8,128)(2,1)S(1)}, u32[]{:S(2)}, u32[]{:S(2)}) collective-permute-start(bf16[1024,512]{1,0:T(8,128)(2,1)} %refs_0_.1), channel_id=1, source_target_pairs={{0,4},{1,5},{4,8},{5,9},{8,12},{9,13},{12,14},{13,15},{14,10},{15,... | collective-permute-start | bytes 3145736 | tf_op jit(solution)/shard_map/ppermute | solution.py:405
  3.0 24.8 %collective-permute-start.1 = (bf16[1024,512]{1,0:T(8,128)(2,1)}, bf16[1024,512]{1,0:T(8,128)(2,1)S(1)}, u32[]{:S(2)}, u32[]{:S(2)}) collective-permute-start(bf16[1024,512]{1,0:T(8,128)(2,1)} %refs_0_.1), channel_id=1, source_target_pairs={{4,0},{5,1},{8,4},{9,5},{12,8},{13,9},{14,12},{15,13},{10,14},{11,... | collective-permute-start | bytes 3145736 | tf_op jit(solution)/shard_map/ppermute | solution.py:405
  3.0 28.3 %collective-permute-start.7 = (bf16[1024,512]{1,0:T(8,128)(2,1)}, bf16[1024,512]{1,0:T(8,128)(2,1)}, u32[]{:S(2)}, u32[]{:S(2)}) collective-permute-start(bf16[1024,512]{1,0:T(8,128)(2,1)} %refs_0_.1), channel_id=1, source_target_pairs={{0,1},{1,0},{2,3},{3,2},{4,5},{5,4},{6,7},{7,6},{8,9},{9,8},{10,11... | collective-permute-start | bytes 3145736 | tf_op jit(solution)/shard_map/ppermute | solution.py:357
  3.1 1.3 copy-start.3
  4.3 1.2 copy-start.4
  5.5 0.8 copy-start.7
  7.1 1.7 %collective-permute-start.2 = (f32[64,1024]{1,0:T(8,128)S(1)}, f32[64,1024]{1,0:T(8,128)S(1)}, u32[]{:S(2)}, u32[]{:S(2)}) collective-permute-start(f32[64,1024]{1,0:T(8,128)S(1)} %get-tuple-element.41), channel_id=1, source_target_pairs={{0,1},{1,0},{2,3},{3,2},{4,5},{5,4},{6,7},{7,6},{8,9},{9,8},{10,11... | collective-permute-start | bytes 786440 | tf_op jit(solution)/shard_map/ppermute | solution.py:357
  8.9 19.0 %copy-start.8 = (f32[64,1024]{1,0:T(8,128)}, f32[64,1024]{1,0:T(8,128)S(1)}, u32[]{:S(2)}) copy-start(f32[64,1024]{1,0:T(8,128)S(1)} %add.54) | copy-start | bytes 786436
  8.9 18.8 %collective-permute-start.3 = (bf16[32,1024]{1,0:T(8,128)(2,1)S(1)}, bf16[32,1024]{1,0:T(8,128)(2,1)S(1)}, u32[]{:S(2)}, u32[]{:S(2)}) collective-permute-start(bf16[32,1024]{1,0:T(8,128)(2,1)S(1)} %dynamic-slice_convert_fusion), channel_id=1, source_target_pairs={{0,2},{1,3},{2,0},{3,1},{4,6},{5,7},{6,4},{7,5},{8,10},{9,11},{10,... | collective-permute-start | bytes 196616 | tf_op jit(solution)/shard_map/ppermute | solution.py:357
  11.7 0.9 copy-start.6
  20.3 2.9 %copy-start.2 = (f32[7,1024,256]{2,1,0:T(8,128)}, f32[7,1024,256]{2,1,0:T(8,128)S(1)}, u32[]{:S(2)}) copy-start(f32[7,1024,256]{2,1,0:T(8,128)S(1)} %get-tuple-element.70.refs_5_) | copy-start | bytes 22020100
  27.9 7.7 %collective-permute-start.8 = (bf16[1024,512]{1,0:T(8,128)(2,1)S(1)}, bf16[1024,512]{1,0:T(8,128)(2,1)}, u32[]{:S(2)}, u32[]{:S(2)}) collective-permute-start(bf16[1024,512]{1,0:T(8,128)(2,1)S(1)} %collective-permute-done.refs_2_), channel_id=1, source_target_pairs={{0,1},{1,0},{2,3},{3,2},{4,5},{5,4},{6,7},{7,6},{8,9},{9,8},{10,11... | collective-permute-start | bytes 3145736 | tf_op jit(solution)/shard_map/ppermute | solution.py:357
  27.9 7.7 %collective-permute-start.9 = (bf16[1024,512]{1,0:T(8,128)(2,1)S(1)}, bf16[1024,512]{1,0:T(8,128)(2,1)}, u32[]{:S(2)}, u32[]{:S(2)}) collective-permute-start(bf16[1024,512]{1,0:T(8,128)(2,1)S(1)} %collective-permute-done.1.refs_3_), channel_id=1, source_target_pairs={{0,1},{1,0},{2,3},{3,2},{4,5},{5,4},{6,7},{7,6},{8,9},{9,8},{10,11... | collective-permute-start | bytes 3145736 | tf_op jit(solution)/shard_map/ppermute | solution.py:357
  28.4 31.5 %collective-permute-start.4 = (bf16[1024,512]{1,0:T(8,128)(2,1)S(1)}, bf16[1024,512]{1,0:T(8,128)(2,1)S(1)}, u32[]{:S(2)}, u32[]{:S(2)}) collective-permute-start(bf16[1024,512]{1,0:T(8,128)(2,1)S(1)} %collective-permute-done.refs_2_), channel_id=1, source_target_pairs={{0,4},{1,5},{4,8},{5,9},{8,12},{9,13},{12,14},{13,15},{14,10},{15,... | collective-permute-start | bytes 3145736 | tf_op jit(solution)/shard_map/ppermute | solution.py:405
  29.9 29.9 %collective-permute-start.5 = (bf16[1024,512]{1,0:T(8,128)(2,1)S(1)}, bf16[1024,512]{1,0:T(8,128)(2,1)}, u32[]{:S(2)}, u32[]{:S(2)}) collective-permute-start(bf16[1024,512]{1,0:T(8,128)(2,1)S(1)} %collective-permute-done.1.refs_3_), channel_id=1, source_target_pairs={{4,0},{5,1},{8,4},{9,5},{12,8},{13,9},{14,12},{15,13},{10,14},{11,... | collective-permute-start | bytes 3145736 | tf_op jit(solution)/shard_map/ppermute | solution.py:405
  31.3 28.5 %collective-permute-start.6 = (bf16[32,1024]{1,0:T(8,128)(2,1)S(1)}, bf16[32,1024]{1,0:T(8,128)(2,1)S(1)}, u32[]{:S(2)}, u32[]{:S(2)}) collective-permute-start(bf16[32,1024]{1,0:T(8,128)(2,1)S(1)} %fusion.3), channel_id=1, source_target_pairs={{0,8},{1,9},{2,10},{3,11},{4,12},{5,13},{6,14},{7,15},{8,0},{9,1},... | collective-permute-start | bytes 196616 | tf_op jit(solution)/shard_map/ppermute | solution.py:357
  35.6 26.8 %copy-start.9 = (f32[64,1024]{1,0:T(8,128)S(1)}, f32[64,1024]{1,0:T(8,128)}, u32[]{:S(2)}) copy-start(f32[64,1024]{1,0:T(8,128)} %copy-done.8) | copy-start | bytes 786436
  59.8 13.4 %collective-permute-start.13 = (bf16[1024,512]{1,0:T(8,128)(2,1)S(1)}, bf16[1024,512]{1,0:T(8,128)(2,1)S(1)}, u32[]{:S(2)}, u32[]{:S(2)}) collective-permute-start(bf16[1024,512]{1,0:T(8,128)(2,1)S(1)} %collective-permute-done.4.refs_0_), channel_id=1, source_target_pairs={{0,1},{1,0},{2,3},{3,2},{4,5},{5,4},{6,7},{7,6},{8,9},{9,8},{10,11... | collective-permute-start | bytes 3145736 | tf_op jit(solution)/shard_map/ppermute | solution.py:357
  59.8 13.4 %collective-permute-start.14 = (bf16[1024,512]{1,0:T(8,128)(2,1)}, bf16[1024,512]{1,0:T(8,128)(2,1)S(1)}, u32[]{:S(2)}, u32[]{:S(2)}) collective-permute-start(bf16[1024,512]{1,0:T(8,128)(2,1)} %collective-permute-done.5.refs_1_), channel_id=1, source_target_pairs={{0,1},{1,0},{2,3},{3,2},{4,5},{5,4},{6,7},{7,6},{8,9},{9,8},{10,11... | collective-permute-start | bytes 3145736 | tf_op jit(solution)/shard_map/ppermute | solution.py:357
  60.3 26.9 %collective-permute-start.10 = (bf16[1024,512]{1,0:T(8,128)(2,1)S(1)}, bf16[1024,512]{1,0:T(8,128)(2,1)S(1)}, u32[]{:S(2)}, u32[]{:S(2)}) collective-permute-start(bf16[1024,512]{1,0:T(8,128)(2,1)S(1)} %collective-permute-done.4.refs_0_), channel_id=1, source_target_pairs={{0,4},{1,5},{4,8},{5,9},{8,12},{9,13},{12,14},{13,15},{14,10},{15,... | collective-permute-start | bytes 3145736 | tf_op jit(solution)/shard_map/ppermute | solution.py:405
  60.8 26.5 %collective-permute-start.11 = (bf16[1024,512]{1,0:T(8,128)(2,1)}, bf16[1024,512]{1,0:T(8,128)(2,1)S(1)}, u32[]{:S(2)}, u32[]{:S(2)}) collective-permute-start(bf16[1024,512]{1,0:T(8,128)(2,1)} %collective-permute-done.5.refs_1_), channel_id=1, source_target_pairs={{4,0},{5,1},{8,4},{9,5},{12,8},{13,9},{14,12},{15,13},{10,14},{11,... | collective-permute-start | bytes 3145736 | tf_op jit(solution)/shard_map/ppermute | solution.py:405
  62.4 24.9 %collective-permute-start.12 = (bf16[32,1024]{1,0:T(8,128)(2,1)S(1)}, bf16[32,1024]{1,0:T(8,128)(2,1)S(1)}, u32[]{:S(2)}, u32[]{:S(2)}) collective-permute-start(bf16[32,1024]{1,0:T(8,128)(2,1)S(1)} %fusion), channel_id=1, source_target_pairs={{0,4},{1,5},{2,6},{3,7},{4,0},{5,1},{6,2},{7,3},{8,12},{9,13},{10,... | collective-permute-start | bytes 196616 | tf_op jit(solution)/shard_map/ppermute | solution.py:357
  87.3 2.7 %collective-permute-start.17 = (bf16[1024,512]{1,0:T(8,128)(2,1)S(1)}, bf16[1024,512]{1,0:T(8,128)(2,1)S(1)}, u32[]{:S(2)}, u32[]{:S(2)}) collective-permute-start(bf16[1024,512]{1,0:T(8,128)(2,1)S(1)} %collective-permute-done.10.refs_0_), channel_id=1, source_target_pairs={{0,1},{1,0},{2,3},{3,2},{4,5},{5,4},{6,7},{7,6},{8,9},{9,8},{10,11... | collective-permute-start | bytes 3145736 | tf_op jit(solution)/shard_map/ppermute | solution.py:357
  87.3 4.2 %collective-permute-start.18 = (bf16[1024,512]{1,0:T(8,128)(2,1)S(1)}, bf16[1024,512]{1,0:T(8,128)(2,1)S(1)}, u32[]{:S(2)}, u32[]{:S(2)}) collective-permute-start(bf16[1024,512]{1,0:T(8,128)(2,1)S(1)} %collective-permute-done.11.refs_1_), channel_id=1, source_target_pairs={{0,1},{1,0},{2,3},{3,2},{4,5},{5,4},{6,7},{7,6},{8,9},{9,8},{10,11... | collective-permute-start | bytes 3145736 | tf_op jit(solution)/shard_map/ppermute | solution.py:357
  87.8 22.8 %slice-start = ((s8[7340032]{0:T(1024)(128)(4,1)}), s8[4194304]{0:T(1024)(128)(4,1)S(1)}, s32[]{:S(2)}) async-start(s8[7340032]{0:T(1024)(128)(4,1)} %bitcast.5), calls=%async_computation | async-start | bytes 8388608
  87.9 22.8 %slice-start.1 = ((s8[7340032]{0:T(1024)(128)(4,1)}), s8[3145728]{0:T(1024)(128)(4,1)S(1)}, s32[]{:S(2)}) async-start(s8[7340032]{0:T(1024)(128)(4,1)} %bitcast.5), calls=%async_computation.1 | async-start | bytes 6291456
  87.9 22.8 %copy-start.5 = (bf16[64,1792]{1,0:T(8,128)(2,1)S(1)}, bf16[64,1792]{1,0:T(8,128)(2,1)}, u32[]{:S(2)}) copy-start(bf16[64,1792]{1,0:T(8,128)(2,1)} %refs_6_.5) | copy-start | bytes 688132
  87.9 14.0 %collective-permute-start.15 = (bf16[512,512]{1,0:T(8,128)(2,1)S(1)}, bf16[512,512]{1,0:T(8,128)(2,1)S(1)}, u32[]{:S(2)}, u32[]{:S(2)}) collective-permute-start(bf16[512,512]{1,0:T(8,128)(2,1)S(1)} %slice.6), channel_id=1, source_target_pairs={{0,4},{1,5},{4,8},{5,9},{8,12},{9,13},{12,14},{13,15},{14,10},{15,... | collective-permute-start | bytes 1572872 | tf_op jit(solution)/shard_map/ppermute | solution.py:405
  88.5 13.6 %collective-permute-start.16 = (bf16[512,512]{1,0:T(8,128)(2,1)S(1)}, bf16[512,512]{1,0:T(8,128)(2,1)S(1)}, u32[]{:S(2)}, u32[]{:S(2)}) collective-permute-start(bf16[512,512]{1,0:T(8,128)(2,1)S(1)} %slice.7), channel_id=1, source_target_pairs={{4,0},{5,1},{8,4},{9,5},{12,8},{13,9},{14,12},{15,13},{10,14},{11,... | collective-permute-start | bytes 1572872 | tf_op jit(solution)/shard_map/ppermute | solution.py:405
  102.1 8.5 %collective-permute-start.22 = (bf16[512,512]{1,0:T(8,128)(2,1)S(1)}, bf16[512,512]{1,0:T(8,128)(2,1)S(1)}, u32[]{:S(2)}, u32[]{:S(2)}) collective-permute-start(bf16[512,512]{1,0:T(8,128)(2,1)S(1)} %collective-permute-done.15.refs_0_), channel_id=1, source_target_pairs={{0,1},{1,0},{2,3},{3,2},{4,5},{5,4},{6,7},{7,6},{8,9},{9,8},{10,11... | collective-permute-start | bytes 1572872 | tf_op jit(solution)/shard_map/ppermute | solution.py:357
  102.1 8.5 %collective-permute-start.23 = (bf16[512,512]{1,0:T(8,128)(2,1)S(1)}, bf16[512,512]{1,0:T(8,128)(2,1)S(1)}, u32[]{:S(2)}, u32[]{:S(2)}) collective-permute-start(bf16[512,512]{1,0:T(8,128)(2,1)S(1)} %collective-permute-done.16.refs_2_), channel_id=1, source_target_pairs={{0,1},{1,0},{2,3},{3,2},{4,5},{5,4},{6,7},{7,6},{8,9},{9,8},{10,11... | collective-permute-start | bytes 1572872 | tf_op jit(solution)/shard_map/ppermute | solution.py:357
  102.7 5.7 %collective-permute-start.20 = (f32[32,1024]{1,0:T(8,128)S(1)}, f32[32,1024]{1,0:T(8,128)S(1)}, u32[]{:S(2)}, u32[]{:S(2)}) collective-permute-start(f32[32,1024]{1,0:T(8,128)S(1)} %get-tuple-element.61.mine_ref), channel_id=1, source_target_pairs={{0,1},{1,0},{2,3},{3,2},{4,5},{5,4},{6,7},{7,6},{8,9},{9,8},{10,11... | collective-permute-start | bytes 393224 | tf_op jit(solution)/shard_map/ppermute | solution.py:357
  102.8 4.5 %collective-permute-start.19 = (bf16[32,1024]{1,0:T(8,128)(2,1)S(1)}, bf16[32,1024]{1,0:T(8,128)(2,1)S(1)}, u32[]{:S(2)}, u32[]{:S(2)}) collective-permute-start(bf16[32,1024]{1,0:T(8,128)(2,1)S(1)} %get-tuple-element.77), channel_id=1, source_target_pairs={{0,2},{1,3},{2,0},{3,1},{4,6},{5,7},{6,4},{7,5},{8,10},{9,11},{10,... | collective-permute-start | bytes 196616 | tf_op jit(solution)/shard_map/ppermute | solution.py:357
  104.3 4.1 %collective-permute-start.21 = (bf16[32,1024]{1,0:T(8,128)(2,1)S(1)}, bf16[32,1024]{1,0:T(8,128)(2,1)S(1)}, u32[]{:S(2)}, u32[]{:S(2)}) collective-permute-start(bf16[32,1024]{1,0:T(8,128)(2,1)S(1)} %get-tuple-element.77), channel_id=1, source_target_pairs={{0,3},{1,2},{2,1},{3,0},{4,7},{5,6},{6,5},{7,4},{8,11},{9,10},{10,... | collective-permute-start | bytes 196616 | tf_op jit(solution)/shard_map/ppermute | solution.py:357
  110.7 25.3 %copy-start.1 = (bf16[64,8192]{1,0:T(8,128)(2,1)S(1)}, bf16[64,8192]{1,0:T(8,128)(2,1)}, u32[]{:S(2)}) copy-start(bf16[64,8192]{1,0:T(8,128)(2,1)} %param.19) | copy-start | bytes 3145732
  117.5 1.4 %collective-permute-start.24 = (f32[8,4096]{1,0:T(8,128)S(1)}, f32[8,4096]{1,0:T(8,128)S(1)}, u32[]{:S(2)}, u32[]{:S(2)}) collective-permute-start(f32[8,4096]{1,0:T(8,128)S(1)} %broadcast_select_fusion.2), channel_id=1, source_target_pairs={{0,1},{1,0},{2,3},{3,2},{4,5},{5,4},{6,7},{7,6},{8,9},{9,8},{10,11... | collective-permute-start | bytes 393224 | tf_op jit(solution)/shard_map/ppermute | solution.py:357
  118.9 4.3 %collective-permute-start.25 = (bf16[8,4096]{1,0:T(8,128)(2,1)S(1)}, bf16[8,4096]{1,0:T(8,128)(2,1)S(1)}, u32[]{:S(2)}, u32[]{:S(2)}) collective-permute-start(bf16[8,4096]{1,0:T(8,128)(2,1)S(1)} %get-tuple-element.75), channel_id=1, source_target_pairs={{0,2},{1,3},{2,0},{3,1},{4,6},{5,7},{6,4},{7,5},{8,10},{9,11},{10,... | collective-permute-start | bytes 196616 | tf_op jit(solution)/shard_map/ppermute | solution.py:357
  123.3 4.3 %collective-permute-start.26 = (bf16[8,4096]{1,0:T(8,128)(2,1)S(1)}, bf16[8,4096]{1,0:T(8,128)(2,1)S(1)}, u32[]{:S(2)}, u32[]{:S(2)}) collective-permute-start(bf16[8,4096]{1,0:T(8,128)(2,1)S(1)} %fusion.1), channel_id=1, source_target_pairs={{0,4},{1,5},{2,6},{3,7},{4,0},{5,1},{6,2},{7,3},{8,12},{9,13},{10,... | collective-permute-start | bytes 196616 | tf_op jit(solution)/shard_map/ppermute | solution.py:357
  127.6 5.9 %collective-permute-start.27 = (bf16[8,4096]{1,0:T(8,128)(2,1)S(1)}, bf16[8,4096]{1,0:T(8,128)(2,1)S(1)}, u32[]{:S(2)}, u32[]{:S(2)}) collective-permute-start(bf16[8,4096]{1,0:T(8,128)(2,1)S(1)} %fusion.2), channel_id=1, source_target_pairs={{0,8},{1,9},{2,10},{3,11},{4,12},{5,13},{6,14},{7,15},{8,0},{9,1},... | collective-permute-start | bytes 196616 | tf_op jit(solution)/shard_map/ppermute | solution.py:357
  133.6 1.4 %collective-permute-start.28 = (f32[8,4096]{1,0:T(8,128)S(1)}, f32[8,4096]{1,0:T(8,128)S(1)}, u32[]{:S(2)}, u32[]{:S(2)}) collective-permute-start(f32[8,4096]{1,0:T(8,128)S(1)} %convert_add_fusion), channel_id=1, source_target_pairs={{0,1},{1,0},{2,3},{3,2},{4,5},{5,4},{6,7},{7,6},{8,9},{9,8},{10,11... | collective-permute-start | bytes 393224 | tf_op jit(solution)/shard_map/ppermute | solution.py:357
